TPU v7x, 32 devices: a whole 2x2x4 slice. The times are simulated.
32 devices in a mesh: row: 8 (over z, core), col: 4 (over y, x).
Axes of the slice: x: 2, y: 2, z: 4, core: 2. Of those that a mesh axis runs over, the one named last changes fastest.
Arguments:
- curve_embed: bfloat16 [2048, 128], P(('row', 'col')), may hold values from -6 to 6
- solution: float32 [2048, 256], P(('row', 'col')), may hold values from -0.5 to 0.5
- targets: bfloat16 [2048, 256], P(('row', 'col')), may hold values from -6 to 6
- lengths: int32 [2048], P(('row', 'col')), may hold values from 1 to 256
- slot_curve: int32 [2048], P(('row', 'col')), may hold values from 0 to 2047, as said below
- epoch_kernel: float32 [256, 256], replicated, as said below
Outputs:
- row_grad: float32 [2048, 128], P(('row', 'col'))
- col_grad: float32 [2048, 128], P(('row', 'col'))
Inputs may be any that keep to these rules, and one draw needn't show every extreme that they name: Within each aligned group of 256 slots, slot_curve is a permutation of that group's own slot numbers. `epoch_kernel`: symmetric positive definite.
All inputs are finite; a program needn't handle non-finite values.
Results may differ from a plain program's by a relative error of at most 0.0036.
Values may be sent and summed in bfloat16 or wider, within the bound.
No kernel may reach another device: no remote copies, remote signals or barrier semaphores. Data moves between devices by JAX's collectives and lax.ppermute only.
A program may use at most 64 MiB of HBM per device.

v0:
```python
import jax
import jax.numpy as jnp
from jax import lax
from jax.sharding import PartitionSpec as P


def kernel_block(row_embed, row_square, piece_embed):
    piece_wide = piece_embed.astype(jnp.float32)
    products = lax.dot_general(
        row_embed, piece_embed, (((1,), (1,)), ((), ())), preferred_element_type=jnp.float32
    )
    distance = (
        row_square[:, None] + jnp.sum(piece_wide * piece_wide, axis=1)[None, :] - 2.0 * products
    )
    return jnp.exp(-distance / row_embed.shape[1])


def block_width():
    return 256


def make_fit(row_embed, row_square):

    def fit_fold(summed, pieces, offset):
        piece_embed, piece_fitted = pieces
        extent = piece_embed.shape[0]
        width_blk = block_width()

        def fit_advance(position, running):
            embed_part = lax.dynamic_slice_in_dim(piece_embed, position * width_blk, width_blk, 0)
            fitted_part = lax.dynamic_slice_in_dim(piece_fitted, position * width_blk, width_blk, 0)
            kernel = kernel_block(row_embed, row_square, embed_part).astype(jnp.bfloat16)
            return running + jnp.dot(kernel, fitted_part, preferred_element_type=jnp.float32)

        return lax.fori_loop(0, extent // width_blk, fit_advance, summed)

    return fit_fold


def make_grad(row_embed, row_square, row_wide, adjoint):

    def grad_fold(carry, pieces, offset):
        piece_embed, piece_fitted = pieces
        extent = piece_embed.shape[0]
        width_blk = block_width()

        def grad_advance(position, running):
            row_part, col_part = running
            embed_part = lax.dynamic_slice_in_dim(piece_embed, position * width_blk, width_blk, 0)
            fitted_part = lax.dynamic_slice_in_dim(piece_fitted, position * width_blk, width_blk, 0)
            kernel = kernel_block(row_embed, row_square, embed_part)
            link = lax.dot_general(
                adjoint, fitted_part, (((1,), (1,)), ((), ())), preferred_element_type=jnp.float32
            )
            weight = (link * kernel).astype(jnp.bfloat16)
            across = (
                jnp.dot(weight, embed_part, preferred_element_type=jnp.float32)
                - row_wide * jnp.sum(weight, axis=1, dtype=jnp.float32)[:, None]
            )
            down = lax.dot_general(
                weight, row_embed, (((0,), (0,)), ((), ())), preferred_element_type=jnp.float32
            )
            down = (
                down
                - embed_part.astype(jnp.float32)
                * jnp.sum(weight, axis=0, dtype=jnp.float32)[:, None]
            )
            first_row = offset + position * width_blk
            col_part = lax.dynamic_update_slice_in_dim(col_part, down, first_row, 0)
            return (row_part + across, col_part)

        return lax.fori_loop(0, extent // width_blk, grad_advance, carry)

    return grad_fold


def per_device(curve_embed, solution, targets, lengths, slot_curve, epoch_kernel):
    own_rows = curve_embed.shape[0]
    width = curve_embed.shape[1]
    epochs_count = solution.shape[1]
    group_size = own_rows * lax.axis_size("col")
    column_size = own_rows * lax.axis_size("row")
    fitted_own = jnp.dot(
        solution, epoch_kernel, precision=lax.Precision.HIGHEST, preferred_element_type=jnp.float32
    ).astype(jnp.bfloat16)
    row_embed, row_curve = (
        lax.all_gather(curve_embed, "col", axis=0, tiled=True),
        lax.all_gather(slot_curve, "col", axis=0, tiled=True),
    )
    row_wide = row_embed.astype(jnp.float32)
    row_square = jnp.sum(row_wide * row_wide, axis=1)
    fit_fold = make_fit(row_embed, row_square)
    start_fit = jnp.zeros((group_size, epochs_count), jnp.float32)
    col_embed, col_fitted = (
        lax.all_gather(curve_embed, "row", axis=0, tiled=True),
        lax.all_gather(fitted_own, "row", axis=0, tiled=True),
    )
    fitted_sum = fit_fold(start_fit, (col_embed, col_fitted), 0)
    epochs = jnp.arange(epochs_count, dtype=jnp.int32)
    fitted_mine = lax.psum_scatter(fitted_sum, "col", scatter_dimension=0, tiled=True)
    observed = epochs[None, :] < lengths[:, None]
    adjoint_own = jnp.where(observed, targets.astype(jnp.float32) - fitted_mine, 0.0).astype(
        jnp.bfloat16
    )
    adjoint = lax.all_gather(adjoint_own, "col", axis=0, tiled=True)
    grad_fold = make_grad(row_embed, row_square, row_wide, adjoint)
    start_grad = (
        jnp.zeros((group_size, width), jnp.float32),
        jnp.zeros((column_size, width), jnp.float32),
    )
    row_sum, col_sum = grad_fold(start_grad, (col_embed, col_fitted), 0)
    group_base = lax.axis_index("row") * group_size
    local_curve = (row_curve - group_base).astype(jnp.int32)
    inverse = (
        jnp.zeros((group_size,), jnp.int32)
        .at[local_curve]
        .set(jnp.arange(group_size, dtype=jnp.int32))
    )
    reordered = jnp.take(row_sum, inverse, axis=0)
    factor = 2.0 / width
    row_grad = lax.psum_scatter(reordered, "col", scatter_dimension=0, tiled=True) * factor
    col_grad = lax.psum_scatter(col_sum, "row", scatter_dimension=0, tiled=True) * factor
    return (row_grad, col_grad)


def solution(mesh):
    in_specs = (
        P(("row", "col"), None),
        P(("row", "col"), None),
        P(("row", "col"), None),
        P(("row", "col")),
        P(("row", "col")),
        P(),
    )
    out_specs = (P(("row", "col"), None), P(("row", "col"), None))
    return jax.shard_map(
        per_device, mesh=mesh, in_specs=in_specs, out_specs=out_specs, check_vma=False
    )
```

profile of v0, /device:TPU:0, one launch (start us, length us, event | category | flops | bytes accessed | tf_op | source)
XLA Modules:
  0.0 150.7 jit_solution(10122669738126206920)
XLA Ops:
  7.2 0.0 copy-start
  7.2 0.0 reduce-scatter.4.cloned.1.call-start
  7.2 10.0 %all_gather.17 = bf16[256,128]{1,0:T(8,128)(2,1)S(1)} all-gather(bf16[64,128]{1,0:T(8,128)(2,1)} %param.10), channel_id=1, replica_groups=mesh['row'=8,'col'=4] {'col'}, dimensions={0}, use_global_device_ids=true | all-gather | bytes 81920 | tf_op jit(solution)/shard_map/all_gather | solution.py:87
  17.2 14.3 %all_gather.18 = bf16[512,128]{1,0:T(8,128)(2,1)S(1)} all-gather(bf16[64,128]{1,0:T(8,128)(2,1)S(1)} %copy-done.3), channel_id=1, replica_groups=mesh['row'=8,'col'=4] {'row'}, dimensions={0}, use_global_device_ids=true | all-gather | bytes 147456 | tf_op jit(solution)/shard_map/all_gather | solution.py:95
  31.5 0.1 multiply_reduce_fusion.1
  31.6 0.7 copy-done.4
  32.3 0.2 convolution_convert_fusion
  32.6 14.2 %all_gather.16 = bf16[512,256]{1,0:T(8,128)(2,1)S(1)} all-gather(bf16[64,256]{1,0:T(8,128)(2,1)S(1)} %convolution_convert_fusion), channel_id=1, replica_groups=mesh['row'=8,'col'=4] {'row'}, dimensions={0}, use_global_device_ids=true | all-gather | bytes 294912 | tf_op jit(solution)/shard_map/all_gather | solution.py:96
  46.8 1.1 while.30
  46.8 0.1 multiply_reduce_fusion.3
  46.9 0.4 convolution_add_fusion.2
  47.3 0.1 multiply_reduce_fusion.3
  47.4 0.4 convolution_add_fusion.2
  47.9 0.7 copy-done.2
  48.5 0.0 reduce-scatter.4.cloned.1.call-update
  48.6 0.0 reduce-scatter.6.cloned.1.call-start
  48.6 0.0 copy-start.8
  48.6 0.0 copy-start.7
  48.7 0.0 copy-start.5
  48.7 0.6 copy-done.8
  49.3 0.6 dynamic-slice
  50.5 0.2 dynamic-update-slice
  50.8 7.2 %all-reduce = s32[256]{0:T(256)S(1)} all-reduce(s32[256]{0:T(256)S(1)} %dynamic-update-slice), channel_id=1, replica_groups=mesh['row'=8,'col'=4] {'col'}, use_global_device_ids=true, to_apply=%add | all-reduce | flops 256 | bytes 2048
  58.0 1.4 scatter_custom_fusion
  59.4 0.0 copy-start.6
  59.4 13.5 %reduce-scatter.4.cloned.1.call-done = f32[64,256]{1,0:T(8,128)} async-done(((f32[256,256]{1,0:T(8,128)}), f32[64,256]{1,0:T(8,128)}) %reduce-scatter.4.cloned.1.call-update) | async-done | bytes 65552 | tf_op jit(solution)/shard_map/reduce_scatter | solution.py:100
  72.9 0.9 select_convert_fusion
  73.8 8.6 %all_gather.19 = bf16[256,256]{1,0:T(8,128)(2,1)S(1)} all-gather(bf16[64,256]{1,0:T(8,128)(2,1)S(1)} %select_convert_fusion), channel_id=1, replica_groups=mesh['row'=8,'col'=4] {'col'}, dimensions={0}, use_global_device_ids=true | all-gather | bytes 163840 | tf_op jit(solution)/shard_map/all_gather | solution.py:105
  82.4 2.3 %while.31 = (s32[]{:T(128)}, f32[256,128]{1,0:T(8,128)S(1)}, f32[512,128]{1,0:T(8,128)S(1)}, bf16[512,256]{1,0:T(8,128)(2,1)S(1)}, bf16[256,256]{1,0:T(8,128)(2,...) while((s32[]{:T(128)}, f32[256,128]{1,0:T(8,128)S(1)}, ...), condition=%wide.region_10.11_spmd.clone, body=%wide.region_6.10_spmd.clone.sunk | while | flops 84868352 | bytes 2104521 | solution.py:72
  82.4 0.1 fusion.67
  82.6 0.2 convolution_bitcast_fusion.2
  82.8 0.3 convert_reduce_fusion.3
  83.1 0.2 fusion.69
  83.3 0.3 fusion.68
  83.6 0.1 fusion.67
  83.7 0.2 convolution_bitcast_fusion.2
  83.9 0.3 convert_reduce_fusion.3
  84.2 0.2 fusion.69
  84.4 0.3 fusion.68
  84.7 0.7 gather_fusion
  85.5 0.8 broadcast_select_fusion
  86.2 0.0 reduce-scatter.6.cloned.1.call-update
  86.2 0.0 reduce-scatter.8.cloned.1.call-start
  86.3 0.7 reduce-scatter.8.cloned.1.call-update
  87.0 23.3 %reduce-scatter.6.cloned.1.call-done = f32[64,128]{1,0:T(8,128)} async-done(((f32[256,128]{1,0:T(8,128)}), f32[64,128]{1,0:T(8,128)}) %reduce-scatter.6.cloned.1.call-update) | async-done | bytes 32784 | tf_op jit(solution)/shard_map/reduce_scatter | solution.py:121
  110.2 1.4 broadcast_multiply_fusion.1
  111.6 31.2 %reduce-scatter.8.cloned.1.call-done = f32[64,128]{1,0:T(8,128)} async-done(((f32[512,128]{1,0:T(8,128)}), f32[64,128]{1,0:T(8,128)}) %reduce-scatter.8.cloned.1.call-update) | async-done | bytes 32784 | tf_op jit(solution)/shard_map/reduce_scatter | solution.py:122
  142.8 1.4 broadcast_multiply_fusion
  (20 shorter events, 0.1 us)
Async XLA Ops:
  7.2 24.4 %copy-start = (f32[256,256]{1,0:T(8,128)S(1)}, f32[256,256]{1,0:T(8,128)}, u32[]{:S(2)}) copy-start(f32[256,256]{1,0:T(8,128)} %param.15) | copy-start | bytes 786436
  7.2 10.0 %copy-start.3 = (bf16[64,128]{1,0:T(8,128)(2,1)S(1)}, bf16[64,128]{1,0:T(8,128)(2,1)}, u32[]{:S(2)}) copy-start(bf16[64,128]{1,0:T(8,128)(2,1)} %param.10) | copy-start | bytes 49156
  7.2 65.7 %reduce-scatter.4.cloned.1.call-start = ((), (), s32[]{:S(2)}) async-start(), calls=%async_computation.3 | async-start | bytes 327680 | tf_op jit(solution)/shard_map/reduce_scatter | solution.py:100
  31.5 0.8 copy-start.4
  47.8 0.7 copy-start.2
  48.6 61.7 %reduce-scatter.6.cloned.1.call-start = ((), (), s32[]{:S(2)}) async-start(), calls=%async_computation.4 | async-start | bytes 163840 | tf_op jit(solution)/shard_map/reduce_scatter | solution.py:121
  48.6 0.7 copy-start.8
  48.6 1.9 %copy-start.7 = (s32[64]{0:T(128)S(1)}, s32[64]{0:T(128)}, u32[]{:S(2)}) copy-start(s32[64]{0:T(128)} %param.14) | copy-start | bytes 772
  48.7 24.2 %copy-start.5 = (bf16[64,256]{1,0:T(8,128)(2,1)S(1)}, bf16[64,256]{1,0:T(8,128)(2,1)}, u32[]{:S(2)}) copy-start(bf16[64,256]{1,0:T(8,128)(2,1)} %param.12) | copy-start | bytes 98308
  59.4 13.5 %copy-start.6 = (s32[64]{0:T(128)S(1)}, s32[64]{0:T(128)}, u32[]{:S(2)}) copy-start(s32[64]{0:T(128)} %param.13) | copy-start | bytes 772
  84.7 0.7 copy-start.1
  86.2 56.6 %reduce-scatter.8.cloned.1.call-start = ((), (), s32[]{:S(2)}) async-start(), calls=%async_computation.5 | async-start | bytes 294912 | tf_op jit(solution)/shard_map/reduce_scatter | solution.py:122
Sparse Core Ops, SparseCore 0:
  48.7 24.1 reduce-scatter.3
  86.4 23.8 reduce-scatter.5
  112.5 30.3 reduce-scatter.7
where the time goes:
time: 151 us
  waiting for transfers between devices  68.7 us (45%)
  blocking collectives  54.2 us (36%)
  between operations  14.6 us (10%)
  other arithmetic  5.04 us (3%)
  local copies, waits for them, and re-layouts  4.99 us (3%)
  matrix products  2.97 us (2%)
    reduce_scatter x1, waiting for transfers between devices, per_device(): lax.psum_scatter(col_sum, 'row', scatter_dimension=0, tiled=True) * factor  31.2 us
    reduce_scatter x1, waiting for transfers between devices, per_device(): lax.psum_scatter(reordered, 'col', scatter_dimension=0, tiled=True) * factor  23.3 us
    all_gather x1, blocking collectives, per_device(): lax.all_gather(curve_embed, 'row', axis=0, tiled=True)  14.3 us
    all_gather x1, blocking collectives, per_device(): lax.all_gather(fitted_own, 'row', axis=0, tiled=True)  14.2 us
    reduce_scatter x1, waiting for transfers between devices, per_device(): lax.psum_scatter(fitted_sum, 'col', scatter_dimension=0, tiled=True)  13.5 us
    all_gather x1, blocking collectives, per_device(): lax.all_gather(curve_embed, 'col', axis=0, tiled=True)  9.98 us
    all_gather x1, blocking collectives, per_device(): adjoint = lax.all_gather(adjoint_own, 'col', axis=0, tiled=True)  8.57 us
    unnamed x1, blocking collectives  7.19 us
  transfers between devices with their start and end apart: 3, of which 3 were waited for; matrix products, arithmetic and copies ran while one was open for 2% of the time, Pallas kernels for 0%

commit v1 on v0

--- a/solution.py
+++ b/solution.py
@@ -1,7 +1,215 @@
+import functools
+import math
+
 import jax
 import jax.numpy as jnp
 from jax import lax
+from jax.experimental import pallas as pl
+from jax.experimental.pallas import tpu as pltpu
 from jax.sharding import PartitionSpec as P
+
+GATHER_LIMIT = 4 << 20
+BF16, F32 = jnp.bfloat16, jnp.float32
+VMEM = pl.BlockSpec(memory_space=pltpu.VMEM)
+SMEM = pl.BlockSpec(memory_space=pltpu.SMEM)
+PARAMS = pltpu.CompilerParams(vmem_limit_bytes=24 << 20)
+
+
+def nt_dot(left, right):
+    return lax.dot_general(left, right, (((1,), (1,)), ((), ())), preferred_element_type=F32)
+
+
+def nn_dot(left, right):
+    return jnp.dot(left, right, preferred_element_type=F32)
+
+
+def extended(embed):
+    rows, width = embed.shape
+    wide = embed.astype(F32)
+    square = wide * wide
+    high = square.astype(BF16)
+    low = (square - high.astype(F32)).astype(BF16)
+    ones = jnp.ones((2 * width, width), BF16)
+    half = -0.5 * nn_dot(jnp.concatenate([high, low], axis=1), ones)
+    first = half.astype(BF16).astype(F32)
+    second = (half - first).astype(BF16).astype(F32)
+    third = half - first - second
+    lane = lax.broadcasted_iota(jnp.int32, (rows, width), 1)
+
+    def lanes(at, one_at):
+        tail = jnp.where((lane >= one_at) & (lane < one_at + 3), 1.0, 0.0)
+        for offset, term in enumerate((first, second, third)):
+            tail = jnp.where(lane == at + offset, term, tail)
+        return jnp.concatenate([embed, tail.astype(BF16)], axis=1)
+
+    return lanes
+
+
+def head_kernel(width, embed_ref, solution_ref, targets_ref, lengths_ref, epoch_ref, out_ref):
+    rows, epochs = solution_ref.shape
+    fitted = jnp.dot(
+        solution_ref[...], epoch_ref[...], precision=lax.Precision.HIGHEST, preferred_element_type=F32
+    )
+    row = lax.broadcasted_iota(jnp.int32, (rows, rows), 0)
+    column = lax.broadcasted_iota(jnp.int32, (rows, rows), 1)
+    lengths = jnp.sum(
+        jnp.where(row == column, lengths_ref[...], 0).astype(F32), axis=1, keepdims=True
+    )
+    epoch = lax.broadcasted_iota(jnp.int32, (rows, epochs), 1).astype(F32)
+    targets = jnp.where(epoch < lengths, targets_ref[...].astype(F32), jnp.inf)
+    out_ref[:, :width] = embed_ref[...]
+    out_ref[:, width : width + epochs] = fitted.astype(BF16)
+    out_ref[:, width + epochs :] = targets.astype(BF16)
+
+
+def fit_chunks(left, right_ref, fields_ref, scale, width, chunk):
+    total = None
+    for at in range(0, fields_ref.shape[0], chunk):
+        kernel = jnp.exp2(nt_dot(left, right_ref[at : at + chunk, :]) * scale).astype(BF16)
+        part = nn_dot(kernel, fields_ref[at : at + chunk, width:])
+        total = part if total is None else total + part
+    return total
+
+
+def block_of(ref, block, rows, mask):
+    return pl.ds(pl.multiple_of((lax.axis_index("col") ^ mask) * block, block), rows)
+
+
+def near_kernel(scale, chunk, near_ref, left_ref, right_ref, fit_ref):
+    width = left_ref.shape[1] // 2
+    block = near_ref.shape[0] // lax.axis_size("col")
+    for part in range(left_ref.shape[0] // block):
+        embed = near_ref[block_of(near_ref, block, block, 2 * part), :width]
+        left_ref[part * block : (part + 1) * block, :] = extended(embed)(3, 0)
+    for at in range(0, near_ref.shape[0], chunk):
+        right_ref[at : at + chunk, :] = extended(near_ref[at : at + chunk, :width])(0, 3)
+    fit_ref[...] = fit_chunks(left_ref[...], right_ref, near_ref, scale, width, chunk)
+
+
+def far_kernel(scale, factor, chunk, parts, own, *refs):
+    near_ref, far_ref, left_ref, right_near_ref, fit_ref = refs[:5]
+    targets_refs, ids_refs = refs[5 : 5 + parts], refs[5 + parts : 5 + 2 * parts]
+    col_far_ref, col_near_ref, row_ref, right_far_ref, adjoint_ref = refs[5 + 2 * parts :]
+    width = left_ref.shape[1] // 2
+    block = near_ref.shape[0] // lax.axis_size("col")
+    for at in range(0, far_ref.shape[0], chunk):
+        right_far_ref[at : at + chunk, :] = extended(far_ref[at : at + chunk, :width])(0, 3)
+    left = left_ref[...]
+    fit = fit_ref[...] + fit_chunks(left, right_far_ref, far_ref, scale, width, chunk)
+    for part in range(parts):
+        rows = slice(part * block, (part + 1) * block)
+        targets = targets_refs[part][...].astype(F32)
+        adjoint = jnp.where(targets == jnp.inf, 0.0, targets - fit[rows])
+        adjoint_ref[rows, :] = adjoint.astype(BF16)
+    adjoint = adjoint_ref[...]
+
+    def with_ones(embed):
+        return jnp.concatenate([embed, jnp.ones_like(embed)], axis=1)
+
+    def weighted(fields, adjoint, right, left):
+        return (nt_dot(fields, adjoint) * jnp.exp2(nt_dot(right, left) * scale)).astype(BF16)
+
+    def gradient(summed, embed):
+        return factor * (summed[:, :width] - embed.astype(F32) * summed[:, width:])
+
+    row_sources = with_ones(left[:, :width])
+    for fields_ref, right_ref, out_ref in (
+        (far_ref, right_far_ref, col_far_ref),
+        (near_ref, right_near_ref, col_near_ref),
+    ):
+        picks = [block_of(fields_ref, block, own, mask) for mask in (0, 1)]
+        fields = jnp.concatenate([fields_ref[pick, width:] for pick in picks], axis=0)
+        right = jnp.concatenate([right_ref[pick, :] for pick in picks], axis=0)
+        summed = nn_dot(weighted(fields, adjoint, right, left), row_sources)
+        out_ref[...] = gradient(summed, right[:, :width])
+
+    starts = range(0, parts * block, block)
+    slots_left = jnp.concatenate([left_ref[at : at + own, :] for at in starts], axis=0)
+    slots_adjoint = jnp.concatenate([adjoint_ref[at : at + own, :] for at in starts], axis=0)
+    summed = None
+    for fields_ref, right_ref in ((near_ref, right_near_ref), (far_ref, right_far_ref)):
+        for at in range(0, fields_ref.shape[0], chunk):
+            run = slice(at, at + chunk)
+            weight = weighted(slots_adjoint, fields_ref[run, width:], slots_left, right_ref[run, :])
+            part = nn_dot(weight, with_ones(fields_ref[run, :width]))
+            summed = part if summed is None else summed + part
+    slot_rows = gradient(summed, slots_left[:, :width])
+    ids = jnp.concatenate([jnp.broadcast_to(ref[...], (own, own)) for ref in ids_refs], axis=1)
+    wanted = lax.broadcasted_iota(jnp.int32, ids.shape, 0)
+    first = lax.axis_index("row") * lax.axis_size("col")
+    for mask in (0, 1):
+        base = (first + (lax.axis_index("col") ^ mask)) * own
+        chosen = (ids == wanted + base).astype(F32)
+        row_ref[mask * own : (mask + 1) * own, :] = jnp.dot(
+            chosen, slot_rows, precision=lax.Precision.HIGHEST, preferred_element_type=F32
+        )
+
+
+def swap(array, axis, mask):
+    pairs = [(index, index ^ mask) for index in range(lax.axis_size(axis))]
+    return lax.ppermute(array, axis, pairs)
+
+
+def joined(array, axis, mask):
+    return jnp.concatenate([array, swap(array, axis, mask)], axis=0)
+
+
+def gathered_plan(curve_embed, solution, targets, lengths, slot_curve, epoch_kernel):
+    own, width = curve_embed.shape
+    epochs = solution.shape[1]
+    rows_axis, cols_axis = lax.axis_size("row"), lax.axis_size("col")
+    scale = 2.0 * math.log2(math.e) / width
+    factor = 2.0 / width
+    shape = jax.ShapeDtypeStruct
+
+    packed = pl.pallas_call(
+        functools.partial(head_kernel, width),
+        out_shape=shape((own, width + 2 * epochs), BF16),
+        in_specs=[VMEM] * 5,
+        out_specs=VMEM,
+        compiler_params=PARAMS,
+    )(curve_embed, solution, targets, lengths.reshape(1, own), epoch_kernel)
+    columns, observed = packed[:, : width + epochs], packed[:, width + epochs :]
+    step = 2
+    if step < rows_axis:
+        other = swap(packed, "row", step)
+        columns = jnp.concatenate([columns, other[:, : width + epochs]], axis=0)
+        observed = jnp.concatenate([observed, other[:, width + epochs :]], axis=0)
+        step *= 2
+    while step < rows_axis:
+        columns, observed = joined(columns, "row", step), joined(observed, "row", step)
+        step *= 2
+    near = lax.all_gather(columns, "col", axis=0, tiled=True)
+    far = swap(near, "row", 1)
+    observed, ids = [observed], [slot_curve.reshape(1, own)]
+    step = 2
+    while step < cols_axis:
+        observed += [swap(array, "col", step) for array in observed]
+        ids += [swap(array, "col", step) for array in ids]
+        step *= 2
+    parts, block, half = len(observed), observed[0].shape[0], near.shape[0]
+    held, chunk = parts * block, block
+    left, right, fit = pl.pallas_call(
+        functools.partial(near_kernel, scale, chunk),
+        out_shape=(shape((held, 2 * width), BF16), shape((half, 2 * width), BF16), shape((held, epochs), F32)),
+        in_specs=[VMEM],
+        out_specs=[VMEM] * 3,
+        compiler_params=PARAMS,
+        cost_estimate=pl.CostEstimate(
+            flops=2 * held * half * (2 * width + epochs), bytes_accessed=2 << 20, transcendentals=held * half
+        ),
+    )(near)
+    col_far, col_near, row_part = pl.pallas_call(
+        functools.partial(far_kernel, scale, factor, chunk, parts, own),
+        out_shape=(shape((2 * own, width), F32),) * 3,
+        in_specs=[VMEM] * (5 + 2 * parts),
+        out_specs=[VMEM] * 3,
+        scratch_shapes=[pltpu.VMEM((half, 2 * width), BF16), pltpu.VMEM((held, epochs), BF16)],
+        compiler_params=PARAMS,
+    )(near, far, left, right, fit, *observed, *ids)
+    col_part = col_near + swap(col_far, "row", 1)
+    other = swap(jnp.concatenate([col_part[own:], row_part[own:]], axis=0), "col", 1)
+    return row_part[:own] + other[own:], col_part[:own] + other[:own]
 
 
 def kernel_block(row_embed, row_square, piece_embed):
@@ -74,7 +282,7 @@
     return grad_fold
 
 
-def per_device(curve_embed, solution, targets, lengths, slot_curve, epoch_kernel):
+def tiled_plan(curve_embed, solution, targets, lengths, slot_curve, epoch_kernel):
     own_rows = curve_embed.shape[0]
     width = curve_embed.shape[1]
     epochs_count = solution.shape[1]
@@ -123,6 +331,19 @@
     return (row_grad, col_grad)
 
 
+def power_of_two(number):
+    return number >= 2 and number & (number - 1) == 0
+
+
+def per_device(curve_embed, solution, *rest):
+    own, width = curve_embed.shape
+    rows_axis, cols_axis = lax.axis_size("row"), lax.axis_size("col")
+    gathered = own * rows_axis * cols_axis * (width + solution.shape[1]) * 2
+    if gathered <= GATHER_LIMIT and power_of_two(rows_axis) and power_of_two(cols_axis):
+        return gathered_plan(curve_embed, solution, *rest)
+    return tiled_plan(curve_embed, solution, *rest)
+
+
 def solution(mesh):
     in_specs = (
         P(("row", "col"), None),

time: 151 us -> 49.5 us (0.33)
  waiting for transfers between devices: 68.7 us -> 14.4 us
  blocking collectives: 54.2 us -> 11.9 us
  between operations: 14.6 us -> 0.74 us
  starting transfers between devices: 0.12 us -> 12.6 us
  Pallas kernels: 0 us -> 4.78 us
  other arithmetic: 5.04 us -> 0.69 us
  matrix products: 2.97 us -> 0 us
    reduce_scatter x3 -> x0, waiting for transfers between devices: 68 us -> none  [the longest x1 31.2 us: per_device(): lax.psum_scatter(col_sum, 'row', scatter_dimension=0, tiled=True) * factor]
    all_gather x4 -> x1, blocking collectives: 47 us -> 11.9 us  [gathered_plan(): near = lax.all_gather(columns, 'col', axis=0, tiled=True)]
    ppermute x0 -> x8, waiting for transfers between devices: none -> 14.4 us  [swap(): return lax.ppermute(array, axis, pairs)]
    ppermute x0 -> x8, starting transfers between devices: none -> 12.6 us  [swap(): return lax.ppermute(array, axis, pairs)]
    unnamed x1 -> x0, blocking collectives: 7.19 us -> none
    pallas_call x0 -> x3, Pallas kernels: none -> 4.78 us  [the longest x1 3.24 us: gathered_plan(): pl.pallas_call(functools.partial(far_kernel, scale, factor, chunk, parts,...]
    dot_general x11 -> x0, matrix products: 2.97 us -> none  [the longest x2 0.79 us: fit_advance(): jnp.dot(kernel, fitted_part, preferred_element_type=jnp.float32)]
    mul x2 -> x0, other arithmetic: 2.75 us -> none  [the longest x1 1.37 us: per_device(): lax.psum_scatter(reordered, 'col', scatter_dimension=0, tiled=True) * factor]
  transfers between devices with their start and end apart: 3 -> 8, of which waited for: 3 -> 6; matrix products, arithmetic and copies ran while one was open for 2% -> 0% of each run, Pallas kernels for 0% -> 3%
where the time goes in v1:
time: 49.5 us; the launch traced here: 49.1 us
  waiting for transfers between devices  14.4 us (29%)
  starting transfers between devices  12.6 us (25%)
  blocking collectives  11.9 us (24%)
  Pallas kernels  4.78 us (10%)
  local copies, waits for them, and re-layouts  3.95 us (8%)
  between operations  0.74 us (1%)
  other arithmetic  0.69 us (1%)
    ppermute x8, waiting for transfers between devices, swap(): return lax.ppermute(array, axis, pairs)  14.4 us
    ppermute x8, starting transfers between devices, swap(): return lax.ppermute(array, axis, pairs)  12.6 us
    all_gather x1, blocking collectives, gathered_plan(): near = lax.all_gather(columns, 'col', axis=0, tiled=True)  11.9 us
    unnamed x12, local copies, waits for them, and re-layouts  3.92 us
    pallas_call x1, Pallas kernels, gathered_plan(): pl.pallas_call(functools.partial(far_kernel, scale, factor, chunk, parts,...  3.24 us
    pallas_call x1, Pallas kernels, gathered_plan(): pl.pallas_call(functools.partial(near_kernel, scale, chunk), out_shape=(s...  1.3 us
  transfers between devices with their start and end apart: 8, of which 6 were waited for; matrix products, arithmetic and copies ran while one was open for 0% of the time, Pallas kernels for 3%

profile of v1, /device:TPU:0, one launch (start us, length us, event | category | flops | bytes accessed | tf_op | source)
XLA Modules:
  0.0 49.1 jit_solution(7344608018698083309)
XLA Ops:
  0.6 0.0 copy-start.5
  0.6 0.6 %copy-done.5 = s32[64]{0:T(128)S(1)} copy-done((s32[64]{0:T(128)S(1)}, s32[64]{0:T(128)}, u32[]{:S(2)}) %copy-start.5) | copy-done | bytes 280
  1.3 0.0 copy-start
  1.3 0.9 %copy-done = f32[256,256]{1,0:T(8,128)S(1)} copy-done((f32[256,256]{1,0:T(8,128)S(1)}, f32[256,256]{1,0:T(8,128)}, u32[]{:S(2)}) %copy-start) | copy-done | bytes 262168
  2.2 0.0 copy-start.1
  2.2 0.8 %copy-done.1 = f32[64,256]{1,0:T(8,128)S(1)} copy-done((f32[64,256]{1,0:T(8,128)S(1)}, f32[64,256]{1,0:T(8,128)}, u32[]{:S(2)}) %copy-start.1) | copy-done | bytes 65560
  3.1 0.0 copy-start.2
  3.1 0.8 %copy-done.2 = bf16[64,256]{1,0:T(8,128)(2,1)S(1)} copy-done((bf16[64,256]{1,0:T(8,128)(2,1)S(1)}, bf16[64,256]{1,0:T(8,128)(2,1)}, u32[]{:S(2)}) %copy-start.2) | copy-done | bytes 32792
  3.8 0.0 copy-start.3
  3.8 0.7 %copy-done.3 = bf16[64,128]{1,0:T(8,128)(2,1)S(1)} copy-done((bf16[64,128]{1,0:T(8,128)(2,1)S(1)}, bf16[64,128]{1,0:T(8,128)(2,1)}, u32[]{:S(2)}) %copy-start.3) | copy-done | bytes 16408
  4.6 0.2 shard_map.77
  4.8 3.1 %collective-permute-start = (bf16[64,640]{1,0:T(8,128)(2,1)S(1)}, bf16[64,640]{1,0:T(8,128)(2,1)S(1)}, u32[]{:S(2)}, u32[]{:S(2)}) collective-permute-start(bf16[64,640]{1,0:T(8,128)(2,1)S(1)} %shard_map.77), channel_id=1, source_target_pairs={{0,8},{4,12},{8,0},{12,4},{16,24},{20,28},{24,16},{28,20},{1,9},{5... | collective-permute-start | bytes 245768 | tf_op jit(solution)/shard_map/ppermute | solution.py:150
  7.9 2.4 %collective-permute-done = bf16[64,640]{1,0:T(8,128)(2,1)S(1)} collective-permute-done((bf16[64,640]{1,0:T(8,128)(2,1)S(1)}, bf16[64,640]{1,0:T(8,128)(2,1)S(1)}, u32[]{:S(2)}, u32[]{:S(2)}) %collective-permute-start) | collective-permute-done | bytes 81952 | tf_op jit(solution)/shard_map/ppermute | solution.py:150
  10.3 3.1 %collective-permute-start.1 = (bf16[128,384]{1,0:T(8,128)(2,1)S(1)}, bf16[128,384]{1,0:T(8,128)(2,1)S(1)}, u32[]{:S(2)}, u32[]{:S(2)}) collective-permute-start(bf16[128,384]{1,0:T(8,128)(2,1)S(1)} %pad_maximum_fusion.2), channel_id=1, source_target_pairs={{0,16},{4,20},{8,24},{12,28},{16,0},{20,4},{24,8},{28,12},{1,17},{... | collective-permute-start | bytes 294920 | tf_op jit(solution)/shard_map/ppermute | solution.py:150
  13.4 2.9 %collective-permute-done.1 = bf16[128,384]{1,0:T(8,128)(2,1)S(1)} collective-permute-done((bf16[128,384]{1,0:T(8,128)(2,1)S(1)}, bf16[128,384]{1,0:T(8,128)(2,1)S(1)}, u32[]{:S(2)}, u32[]{:S(2)}) %collective-permute-start.1) | collective-permute-done | bytes 98336 | tf_op jit(solution)/shard_map/ppermute | solution.py:150
  16.4 11.9 %all_gather.3.near_ref.refs_0_ = bf16[1024,384]{1,0:T(8,128)(2,1)S(1)} all-gather(bf16[256,384]{1,0:T(8,128)(2,1)S(1)} %pad_maximum_fusion), channel_id=1, replica_groups=mesh['row'=8,'col'=4] {'col'}, dimensions={0}, use_global_device_ids=true | all-gather | bytes 983040 | tf_op jit(solution)/shard_map/all_gather | solution.py:182
  28.3 0.0 collective-permute-start.2
  28.3 3.0 %collective-permute-start.3 = (bf16[128,256]{1,0:T(8,128)(2,1)S(1)}, bf16[128,256]{1,0:T(8,128)(2,1)S(1)}, u32[]{:S(2)}, u32[]{:S(2)}) collective-permute-start(bf16[128,256]{1,0:T(8,128)(2,1)S(1)} %pad_maximum_fusion.3), channel_id=1, source_target_pairs={{0,16},{4,20},{8,24},{12,28},{16,0},{20,4},{24,8},{28,12},{1,17},{... | collective-permute-start | bytes 196616 | tf_op jit(solution)/shard_map/ppermute | solution.py:150
  31.3 2.7 %collective-permute-done.3 = bf16[128,256]{1,0:T(8,128)(2,1)S(1)} collective-permute-done((bf16[128,256]{1,0:T(8,128)(2,1)S(1)}, bf16[128,256]{1,0:T(8,128)(2,1)S(1)}, u32[]{:S(2)}, u32[]{:S(2)}) %collective-permute-start.3) | collective-permute-done | bytes 65568 | tf_op jit(solution)/shard_map/ppermute | solution.py:150
  34.1 0.0 copy-start.4
  34.1 1.5 %collective-permute-start.4 = (bf16[256,256]{1,0:T(8,128)(2,1)S(1)}, bf16[256,256]{1,0:T(8,128)(2,1)S(1)}, u32[]{:S(2)}, u32[]{:S(2)}) collective-permute-start(bf16[256,256]{1,0:T(8,128)(2,1)S(1)} %pad_maximum_fusion.1.refs_5_), channel_id=1, source_target_pairs={{0,2},{1,3},{2,0},{3,1},{4,6},{5,7},{6,4},{7,5},{8,10},{9,11},{10,... | collective-permute-start | bytes 393224 | tf_op jit(solution)/shard_map/ppermute | solution.py:150
  35.6 0.0 copy-done.4
  35.6 0.6 %collective-permute-start.5 = (s32[1,64]{1,0:T(1,128)S(1)}, s32[1,64]{1,0:T(1,128)S(1)}, u32[]{:S(2)}, u32[]{:S(2)}) collective-permute-start(s32[1,64]{1,0:T(1,128)S(1)} %bitcast.2), channel_id=1, source_target_pairs={{0,2},{1,3},{2,0},{3,1},{4,6},{5,7},{6,4},{7,5},{8,10},{9,11},{10,... | collective-permute-start | bytes 776 | tf_op jit(solution)/shard_map/ppermute | solution.py:150
  36.2 1.3 %shard_map.78 = (bf16[512,256]{1,0:T(8,128)(2,1)S(1)}, bf16[1024,256]{1,0:T(8,128)(2,1)S(1)}, f32[512,256]{1,0:T(8,128)S(1)}) custom-call(bf16[1024,384]{1,0:T(8,128)(2,1)S(1)} %all_gather.3.near_ref.refs_0_), custom_call_target="tpu_custom_call" | custom-call | flops 536870912 | bytes 2097152 | tf_op jit(solution)/shard_map/pallas_call | solution.py:192
  37.5 2.0 %collective-permute-done.5.refs_8_ = s32[1,64]{1,0:T(1,128)S(1)} collective-permute-done((s32[1,64]{1,0:T(1,128)S(1)}, s32[1,64]{1,0:T(1,128)S(1)}, u32[]{:S(2)}, u32[]{:S(2)}) %collective-permute-start.5) | collective-permute-done | bytes 288 | tf_op jit(solution)/shard_map/ppermute | solution.py:150
  39.5 0.0 collective-permute-done.4.refs_6_
  39.5 0.0 collective-permute-done.2.refs_1_
  39.5 3.2 %shard_map.79 = (f32[128,128]{1,0:T(8,128)S(1)}, f32[128,128]{1,0:T(8,128)S(1)}, f32[128,128]{1,0:T(8,128)S(1)}) custom-call(bf16[1024,384]{1,0:T(8,128)(2,1)S(1)} %all_gather.3.near_ref.refs_0_, bf16[1024,384]{1,0:T(8,128)(2,1)S(1)} %collective-permute-done.2.refs_1_, bf16[512,256]{1,0:T(8,128)(2,1)S(1)} %get-tuple-element.8.refs_2_, ...), custom_call_target="tpu_custom_call" | custom-call | tf_op jit(solution)/shard_map/pallas_call | solution.py:202
  42.8 0.0 collective-permute-start.6
  42.8 1.2 %collective-permute-done.6 = f32[128,128]{1,0:T(8,128)S(1)} collective-permute-done((f32[128,128]{1,0:T(8,128)S(1)}, f32[128,128]{1,0:T(8,128)S(1)}, u32[]{:S(2)}, u32[]{:S(2)}) %collective-permute-start.6) | collective-permute-done | bytes 65568 | tf_op jit(solution)/shard_map/ppermute | solution.py:150
  44.1 1.3 %collective-permute-start.7 = (f32[128,128]{1,0:T(8,128)S(1)}, f32[128,128]{1,0:T(8,128)S(1)}, u32[]{:S(2)}, u32[]{:S(2)}) collective-permute-start(f32[128,128]{1,0:T(8,128)S(1)} %pad_maximum_fusion.4), channel_id=1, source_target_pairs={{0,1},{1,0},{2,3},{3,2},{4,5},{5,4},{6,7},{7,6},{8,9},{9,8},{10,11... | collective-permute-start | bytes 196616 | tf_op jit(solution)/shard_map/ppermute | solution.py:150
  45.4 3.0 %collective-permute-done.7 = f32[128,128]{1,0:T(8,128)S(1)} collective-permute-done((f32[128,128]{1,0:T(8,128)S(1)}, f32[128,128]{1,0:T(8,128)S(1)}, u32[]{:S(2)}, u32[]{:S(2)}) %collective-permute-start.7) | collective-permute-done | bytes 65568 | tf_op jit(solution)/shard_map/ppermute | solution.py:150
  48.4 0.6 %slice_add_fusion = (f32[64,128]{1,0:T(8,128)}, f32[64,128]{1,0:T(8,128)}) fusion(f32[128,128]{1,0:T(8,128)S(1)} %collective-permute-done.7, f32[128,128]{1,0:T(8,128)S(1)} %add.9, f32[128,128]{1,0:T(8,128)S(1)} %get-tuple-element.11), kind=kLoop, calls=%fused_computation.5 | loop fusion | flops 16384 | bytes 196608 | tf_op jit(solution)/shard_map/add | solution.py:212
  (12 shorter events, 0.1 us)
Async XLA Ops:
  0.6 0.7 %copy-start.5 = (s32[64]{0:T(128)S(1)}, s32[64]{0:T(128)}, u32[]{:S(2)}) copy-start(s32[64]{0:T(128)} %param.9) | copy-start | bytes 772
  1.3 0.9 %copy-start = (f32[256,256]{1,0:T(8,128)S(1)}, f32[256,256]{1,0:T(8,128)}, u32[]{:S(2)}) copy-start(f32[256,256]{1,0:T(8,128)} %epoch_ref.1) | copy-start | bytes 786436
  2.2 0.8 %copy-start.1 = (f32[64,256]{1,0:T(8,128)S(1)}, f32[64,256]{1,0:T(8,128)}, u32[]{:S(2)}) copy-start(f32[64,256]{1,0:T(8,128)} %solution_ref.1) | copy-start | bytes 196612
  3.1 0.8 %copy-start.2 = (bf16[64,256]{1,0:T(8,128)(2,1)S(1)}, bf16[64,256]{1,0:T(8,128)(2,1)}, u32[]{:S(2)}) copy-start(bf16[64,256]{1,0:T(8,128)(2,1)} %targets_ref.1) | copy-start | bytes 98308
  3.8 0.7 %copy-start.3 = (bf16[64,128]{1,0:T(8,128)(2,1)S(1)}, bf16[64,128]{1,0:T(8,128)(2,1)}, u32[]{:S(2)}) copy-start(bf16[64,128]{1,0:T(8,128)(2,1)} %embed_ref.1) | copy-start | bytes 49156
  4.8 5.5 %collective-permute-start = (bf16[64,640]{1,0:T(8,128)(2,1)S(1)}, bf16[64,640]{1,0:T(8,128)(2,1)S(1)}, u32[]{:S(2)}, u32[]{:S(2)}) collective-permute-start(bf16[64,640]{1,0:T(8,128)(2,1)S(1)} %shard_map.77), channel_id=1, source_target_pairs={{0,8},{4,12},{8,0},{12,4},{16,24},{20,28},{24,16},{28,20},{1,9},{5... | collective-permute-start | bytes 245768 | tf_op jit(solution)/shard_map/ppermute | solution.py:150
  10.3 6.0 %collective-permute-start.1 = (bf16[128,384]{1,0:T(8,128)(2,1)S(1)}, bf16[128,384]{1,0:T(8,128)(2,1)S(1)}, u32[]{:S(2)}, u32[]{:S(2)}) collective-permute-start(bf16[128,384]{1,0:T(8,128)(2,1)S(1)} %pad_maximum_fusion.2), channel_id=1, source_target_pairs={{0,16},{4,20},{8,24},{12,28},{16,0},{20,4},{24,8},{28,12},{1,17},{... | collective-permute-start | bytes 294920 | tf_op jit(solution)/shard_map/ppermute | solution.py:150
  28.3 11.3 %collective-permute-start.2 = (bf16[1024,384]{1,0:T(8,128)(2,1)S(1)}, bf16[1024,384]{1,0:T(8,128)(2,1)S(1)}, u32[]{:S(2)}, u32[]{:S(2)}) collective-permute-start(bf16[1024,384]{1,0:T(8,128)(2,1)S(1)} %all_gather.3.near_ref.refs_0_), channel_id=1, source_target_pairs={{0,4},{4,0},{8,12},{12,8},{16,20},{20,16},{24,28},{28,24},{1,5},{5... | collective-permute-start | bytes 2359304 | tf_op jit(solution)/shard_map/ppermute | solution.py:150
  28.3 5.8 %collective-permute-start.3 = (bf16[128,256]{1,0:T(8,128)(2,1)S(1)}, bf16[128,256]{1,0:T(8,128)(2,1)S(1)}, u32[]{:S(2)}, u32[]{:S(2)}) collective-permute-start(bf16[128,256]{1,0:T(8,128)(2,1)S(1)} %pad_maximum_fusion.3), channel_id=1, source_target_pairs={{0,16},{4,20},{8,24},{12,28},{16,0},{20,4},{24,8},{28,12},{1,17},{... | collective-permute-start | bytes 196616 | tf_op jit(solution)/shard_map/ppermute | solution.py:150
  34.1 1.5 %copy-start.4 = (s32[64]{0:T(128)S(1)}, s32[64]{0:T(128)}, u32[]{:S(2)}) copy-start(s32[64]{0:T(128)} %param.10) | copy-start | bytes 772
  34.1 5.4 %collective-permute-start.4 = (bf16[256,256]{1,0:T(8,128)(2,1)S(1)}, bf16[256,256]{1,0:T(8,128)(2,1)S(1)}, u32[]{:S(2)}, u32[]{:S(2)}) collective-permute-start(bf16[256,256]{1,0:T(8,128)(2,1)S(1)} %pad_maximum_fusion.1.refs_5_), channel_id=1, source_target_pairs={{0,2},{1,3},{2,0},{3,1},{4,6},{5,7},{6,4},{7,5},{8,10},{9,11},{10,... | collective-permute-start | bytes 393224 | tf_op jit(solution)/shard_map/ppermute | solution.py:150
  35.6 3.9 %collective-permute-start.5 = (s32[1,64]{1,0:T(1,128)S(1)}, s32[1,64]{1,0:T(1,128)S(1)}, u32[]{:S(2)}, u32[]{:S(2)}) collective-permute-start(s32[1,64]{1,0:T(1,128)S(1)} %bitcast.2), channel_id=1, source_target_pairs={{0,2},{1,3},{2,0},{3,1},{4,6},{5,7},{6,4},{7,5},{8,10},{9,11},{10,... | collective-permute-start | bytes 776 | tf_op jit(solution)/shard_map/ppermute | solution.py:150
  42.8 1.3 %collective-permute-start.6 = (f32[128,128]{1,0:T(8,128)S(1)}, f32[128,128]{1,0:T(8,128)S(1)}, u32[]{:S(2)}, u32[]{:S(2)}) collective-permute-start(f32[128,128]{1,0:T(8,128)S(1)} %get-tuple-element.13), channel_id=1, source_target_pairs={{0,4},{4,0},{8,12},{12,8},{16,20},{20,16},{24,28},{28,24},{1,5},{5... | collective-permute-start | bytes 196616 | tf_op jit(solution)/shard_map/ppermute | solution.py:150
  44.1 4.3 %collective-permute-start.7 = (f32[128,128]{1,0:T(8,128)S(1)}, f32[128,128]{1,0:T(8,128)S(1)}, u32[]{:S(2)}, u32[]{:S(2)}) collective-permute-start(f32[128,128]{1,0:T(8,128)S(1)} %pad_maximum_fusion.4), channel_id=1, source_target_pairs={{0,1},{1,0},{2,3},{3,2},{4,5},{5,4},{6,7},{7,6},{8,9},{9,8},{10,11... | collective-permute-start | bytes 196616 | tf_op jit(solution)/shard_map/ppermute | solution.py:150

commit v2 on v1

--- a/solution.py
+++ b/solution.py
@@ -45,7 +45,17 @@
     return lanes
 
 
-def head_kernel(width, embed_ref, solution_ref, targets_ref, lengths_ref, epoch_ref, out_ref):
+def head_kernel(width, *refs):
+    out_ref, held, semaphores = refs[5], refs[6:11], refs[11]
+    copies = [
+        pltpu.make_async_copy(source, target, semaphores.at[index])
+        for index, (source, target) in enumerate(zip(refs[:5], held))
+    ]
+    for copy in copies:
+        copy.start()
+    for copy in copies:
+        copy.wait()
+    embed_ref, solution_ref, targets_ref, lengths_ref, epoch_ref = held
     rows, epochs = solution_ref.shape
     fitted = jnp.dot(
         solution_ref[...], epoch_ref[...], precision=lax.Precision.HIGHEST, preferred_element_type=F32
@@ -86,54 +96,67 @@
     fit_ref[...] = fit_chunks(left_ref[...], right_ref, near_ref, scale, width, chunk)
 
 
-def far_kernel(scale, factor, chunk, parts, own, *refs):
-    near_ref, far_ref, left_ref, right_near_ref, fit_ref = refs[:5]
-    targets_refs, ids_refs = refs[5 : 5 + parts], refs[5 + parts : 5 + 2 * parts]
-    col_far_ref, col_near_ref, row_ref, right_far_ref, adjoint_ref = refs[5 + 2 * parts :]
+def with_ones(embed):
+    return jnp.concatenate([embed, jnp.ones_like(embed)], axis=1)
+
+
+def weighted(scale, fields, adjoint, right, left):
+    return (nt_dot(fields, adjoint) * jnp.exp2(nt_dot(right, left) * scale)).astype(BF16)
+
+
+def gradient(factor, summed, embed):
+    width = embed.shape[1]
+    return factor * (summed[:, :width] - embed.astype(F32) * summed[:, width:])
+
+
+def column_part(scale, factor, own, adjoint, left, fields_ref, right_ref):
+    width = left.shape[1] // 2
+    block = fields_ref.shape[0] // lax.axis_size("col")
+    picks = [block_of(fields_ref, block, own, mask) for mask in (0, 1)]
+    fields = jnp.concatenate([fields_ref[pick, width:] for pick in picks], axis=0)
+    right = jnp.concatenate([right_ref[pick, :] for pick in picks], axis=0)
+    weight = weighted(scale, fields, adjoint, right, left)
+    return gradient(factor, nn_dot(weight, with_ones(left[:, :width])), right[:, :width])
+
+
+def far_kernel(scale, factor, chunk, parts, own, run, *refs):
+    far_ref, left_ref, fit_ref, targets_ref, right_ref, adjoint_ref, col_ref = refs
     width = left_ref.shape[1] // 2
-    block = near_ref.shape[0] // lax.axis_size("col")
+    held = left_ref.shape[0]
     for at in range(0, far_ref.shape[0], chunk):
-        right_far_ref[at : at + chunk, :] = extended(far_ref[at : at + chunk, :width])(0, 3)
+        right_ref[at : at + chunk, :] = extended(far_ref[at : at + chunk, :width])(0, 3)
     left = left_ref[...]
-    fit = fit_ref[...] + fit_chunks(left, right_far_ref, far_ref, scale, width, chunk)
-    for part in range(parts):
-        rows = slice(part * block, (part + 1) * block)
-        targets = targets_refs[part][...].astype(F32)
-        adjoint = jnp.where(targets == jnp.inf, 0.0, targets - fit[rows])
-        adjoint_ref[rows, :] = adjoint.astype(BF16)
-    adjoint = adjoint_ref[...]
-
-    def with_ones(embed):
-        return jnp.concatenate([embed, jnp.ones_like(embed)], axis=1)
-
-    def weighted(fields, adjoint, right, left):
-        return (nt_dot(fields, adjoint) * jnp.exp2(nt_dot(right, left) * scale)).astype(BF16)
-
-    def gradient(summed, embed):
-        return factor * (summed[:, :width] - embed.astype(F32) * summed[:, width:])
-
-    row_sources = with_ones(left[:, :width])
-    for fields_ref, right_ref, out_ref in (
-        (far_ref, right_far_ref, col_far_ref),
-        (near_ref, right_near_ref, col_near_ref),
-    ):
-        picks = [block_of(fields_ref, block, own, mask) for mask in (0, 1)]
-        fields = jnp.concatenate([fields_ref[pick, width:] for pick in picks], axis=0)
-        right = jnp.concatenate([right_ref[pick, :] for pick in picks], axis=0)
-        summed = nn_dot(weighted(fields, adjoint, right, left), row_sources)
-        out_ref[...] = gradient(summed, right[:, :width])
-
+    fit = fit_ref[...] + fit_chunks(left, right_ref, far_ref, scale, width, chunk)
+    for at in range(0, held, run):
+        part, piece = divmod(at, held // parts)
+        first = piece * parts + part * run
+        targets = targets_ref[first : first + run, :].astype(F32)
+        adjoint = jnp.where(targets == jnp.inf, 0.0, targets - fit[at : at + run])
+        adjoint_ref[at : at + run, :] = adjoint.astype(BF16)
+    col_ref[...] = column_part(scale, factor, own, adjoint_ref[...], left, far_ref, right_ref)
+
+
+def last_kernel(scale, factor, chunk, parts, own, *refs):
+    near_ref, far_ref, left_ref, right_near_ref, right_far_ref, adjoint_ref = refs[:6]
+    ids_refs, (col_ref, row_ref) = refs[6 : 6 + parts], refs[6 + parts :]
+    width = left_ref.shape[1] // 2
+    block = left_ref.shape[0] // parts
+    col_ref[...] = column_part(
+        scale, factor, own, adjoint_ref[...], left_ref[...], near_ref, right_near_ref
+    )
     starts = range(0, parts * block, block)
     slots_left = jnp.concatenate([left_ref[at : at + own, :] for at in starts], axis=0)
     slots_adjoint = jnp.concatenate([adjoint_ref[at : at + own, :] for at in starts], axis=0)
     summed = None
     for fields_ref, right_ref in ((near_ref, right_near_ref), (far_ref, right_far_ref)):
         for at in range(0, fields_ref.shape[0], chunk):
-            run = slice(at, at + chunk)
-            weight = weighted(slots_adjoint, fields_ref[run, width:], slots_left, right_ref[run, :])
-            part = nn_dot(weight, with_ones(fields_ref[run, :width]))
+            span = slice(at, at + chunk)
+            weight = weighted(
+                scale, slots_adjoint, fields_ref[span, width:], slots_left, right_ref[span, :]
+            )
+            part = nn_dot(weight, with_ones(fields_ref[span, :width]))
             summed = part if summed is None else summed + part
-    slot_rows = gradient(summed, slots_left[:, :width])
+    slot_rows = gradient(factor, summed, slots_left[:, :width])
     ids = jnp.concatenate([jnp.broadcast_to(ref[...], (own, own)) for ref in ids_refs], axis=1)
     wanted = lax.broadcasted_iota(jnp.int32, ids.shape, 0)
     first = lax.axis_index("row") * lax.axis_size("col")
@@ -162,52 +185,81 @@
     factor = 2.0 / width
     shape = jax.ShapeDtypeStruct
 
+    arrays = (curve_embed, solution, targets, lengths.reshape(1, own), epoch_kernel)
     packed = pl.pallas_call(
         functools.partial(head_kernel, width),
         out_shape=shape((own, width + 2 * epochs), BF16),
-        in_specs=[VMEM] * 5,
+        in_specs=[pl.BlockSpec(memory_space=pltpu.HBM)] * 5,
         out_specs=VMEM,
-        compiler_params=PARAMS,
-    )(curve_embed, solution, targets, lengths.reshape(1, own), epoch_kernel)
+        scratch_shapes=[
+            *(pltpu.VMEM(array.shape, array.dtype) for array in arrays),
+            pltpu.SemaphoreType.DMA((5,)),
+        ],
+    )(*arrays)
     columns, observed = packed[:, : width + epochs], packed[:, width + epochs :]
+    ids = [slot_curve.reshape(1, own)]
     step = 2
     if step < rows_axis:
         other = swap(packed, "row", step)
         columns = jnp.concatenate([columns, other[:, : width + epochs]], axis=0)
         observed = jnp.concatenate([observed, other[:, width + epochs :]], axis=0)
         step *= 2
+    run = observed.shape[0]
+    turn = 2
+    while turn < cols_axis:
+        observed = joined(observed, "col", turn)
+        ids += [swap(array, "col", turn) for array in ids]
+        turn *= 2
+    observed, ids = lax.optimization_barrier((observed, ids))
     while step < rows_axis:
         columns, observed = joined(columns, "row", step), joined(observed, "row", step)
         step *= 2
     near = lax.all_gather(columns, "col", axis=0, tiled=True)
+    near, observed = lax.optimization_barrier((near, observed))
     far = swap(near, "row", 1)
-    observed, ids = [observed], [slot_curve.reshape(1, own)]
-    step = 2
-    while step < cols_axis:
-        observed += [swap(array, "col", step) for array in observed]
-        ids += [swap(array, "col", step) for array in ids]
-        step *= 2
-    parts, block, half = len(observed), observed[0].shape[0], near.shape[0]
-    held, chunk = parts * block, block
-    left, right, fit = pl.pallas_call(
+    parts, held, half = len(ids), observed.shape[0], near.shape[0]
+    chunk = columns.shape[0]
+    left, right_near, fit = pl.pallas_call(
         functools.partial(near_kernel, scale, chunk),
-        out_shape=(shape((held, 2 * width), BF16), shape((half, 2 * width), BF16), shape((held, epochs), F32)),
+        out_shape=(
+            shape((held, 2 * width), BF16),
+            shape((half, 2 * width), BF16),
+            shape((held, epochs), F32),
+        ),
         in_specs=[VMEM],
         out_specs=[VMEM] * 3,
         compiler_params=PARAMS,
         cost_estimate=pl.CostEstimate(
-            flops=2 * held * half * (2 * width + epochs), bytes_accessed=2 << 20, transcendentals=held * half
+            flops=2 * held * half * (2 * width + epochs),
+            bytes_accessed=2 << 20,
+            transcendentals=held * half,
         ),
     )(near)
-    col_far, col_near, row_part = pl.pallas_call(
-        functools.partial(far_kernel, scale, factor, chunk, parts, own),
-        out_shape=(shape((2 * own, width), F32),) * 3,
-        in_specs=[VMEM] * (5 + 2 * parts),
+    right_far, adjoint, col_far = pl.pallas_call(
+        functools.partial(far_kernel, scale, factor, chunk, parts, own, run),
+        out_shape=(
+            shape((half, 2 * width), BF16),
+            shape((held, epochs), BF16),
+            shape((2 * own, width), F32),
+        ),
+        in_specs=[VMEM] * 4,
         out_specs=[VMEM] * 3,
-        scratch_shapes=[pltpu.VMEM((half, 2 * width), BF16), pltpu.VMEM((held, epochs), BF16)],
         compiler_params=PARAMS,
-    )(near, far, left, right, fit, *observed, *ids)
-    col_part = col_near + swap(col_far, "row", 1)
+    )(far, left, fit, observed)
+    col_other = swap(col_far, "row", 1)
+    col_near, row_part = pl.pallas_call(
+        functools.partial(last_kernel, scale, factor, chunk, parts, own),
+        out_shape=(shape((2 * own, width), F32),) * 2,
+        in_specs=[VMEM] * (6 + parts),
+        out_specs=[VMEM] * 2,
+        compiler_params=PARAMS,
+        cost_estimate=pl.CostEstimate(
+            flops=2 * held * half * (2 * width + epochs),
+            bytes_accessed=2 << 20,
+            transcendentals=held * half,
+        ),
+    )(near, far, left, right_near, right_far, adjoint, *ids)
+    col_part = col_near + col_other
     other = swap(jnp.concatenate([col_part[own:], row_part[own:]], axis=0), "col", 1)
     return row_part[:own] + other[own:], col_part[:own] + other[:own]
 

time: 49.5 us -> 43.6 us (0.88)
  waiting for transfers between devices: 14.4 us -> 9.97 us
  local copies, waits for them, and re-layouts: 3.95 us -> 1.59 us
  Pallas kernels: 4.78 us -> 6.84 us
  blocking collectives: 11.9 us -> 11.1 us
    ppermute x8, waiting for transfers between devices: 14.4 us -> 9.97 us  [swap(): return lax.ppermute(array, axis, pairs)]
    unnamed x12 -> x2, local copies, waits for them, and re-layouts: 3.92 us -> 0.01 us
    pallas_call x0 -> x1, Pallas kernels: none -> 2.03 us  [gathered_plan(): pl.pallas_call(functools.partial(last_kernel, scale, factor, chunk, parts...]
    pallas_call x1, Pallas kernels: 0.23 us -> 1.95 us  [gathered_plan(): pl.pallas_call(functools.partial(head_kernel, width), out_shape=shape((ow...]
    pallas_call x1, Pallas kernels: 3.24 us -> 1.55 us  [gathered_plan(): pl.pallas_call(functools.partial(far_kernel, scale, factor, chunk, parts,...]
    slice x2, local copies, waits for them, and re-layouts: 0.01 us -> 1.56 us  [gathered_plan(): columns, observed = (packed[:, :width + epochs], packed[:, width + epochs:])]
    all_gather x1, blocking collectives: 11.9 us -> 11.1 us  [gathered_plan(): near = lax.all_gather(columns, 'col', axis=0, tiled=True)]
  transfers between devices with their start and end apart: 8 -> 8, of which waited for: 6 -> 4; matrix products, arithmetic and copies ran while one was open for 0% -> 4% of each run, Pallas kernels for 3% -> 8%
where the time goes in v2:
time: 43.6 us; the launch traced here: 43.3 us
  starting transfers between devices  12.4 us (28%)
  blocking collectives  11.1 us (25%)
  waiting for transfers between devices  9.97 us (23%)
  Pallas kernels  6.84 us (16%)
  local copies, waits for them, and re-layouts  1.59 us (4%)
  between operations  0.75 us (2%)
  other arithmetic  0.72 us (2%)
    ppermute x8, starting transfers between devices, swap(): return lax.ppermute(array, axis, pairs)  12.4 us
    all_gather x1, blocking collectives, gathered_plan(): near = lax.all_gather(columns, 'col', axis=0, tiled=True)  11.1 us
    ppermute x8, waiting for transfers between devices, swap(): return lax.ppermute(array, axis, pairs)  9.97 us
    pallas_call x1, Pallas kernels, gathered_plan(): pl.pallas_call(functools.partial(last_kernel, scale, factor, chunk, parts...  2.03 us
    pallas_call x1, Pallas kernels, gathered_plan(): pl.pallas_call(functools.partial(head_kernel, width), out_shape=shape((ow...  1.95 us
    slice x2, local copies, waits for them, and re-layouts, gathered_plan(): columns, observed = (packed[:, :width + epochs], packed[:, width + epochs:])  1.56 us
    pallas_call x1, Pallas kernels, gathered_plan(): pl.pallas_call(functools.partial(far_kernel, scale, factor, chunk, parts,...  1.55 us
    pallas_call x1, Pallas kernels, gathered_plan(): pl.pallas_call(functools.partial(near_kernel, scale, chunk), out_shape=(s...  1.3 us
  transfers between devices with their start and end apart: 8, of which 4 were waited for; matrix products, arithmetic and copies ran while one was open for 4% of the time, Pallas kernels for 8%

profile of v2, /device:TPU:0, one launch (start us, length us, event | category | flops | bytes accessed | tf_op | source)
XLA Modules:
  0.0 43.3 jit_solution(383157837528240714)
XLA Ops:
  0.6 2.0 %shard_map.77 = bf16[64,640]{1,0:T(8,128)(2,1)} custom-call(bf16[64,128]{1,0:T(8,128)(2,1)} %refs_0_.1, f32[64,256]{1,0:T(8,128)} %refs_1_.1, bf16[64,256]{1,0:T(8,128)(2,1)} %refs_2_.1, s32[1,64]{1,0:T(1,128)} %bitcast.4, f32[256,256]{1,0:T(8,128)} %refs_4_.1), custom_call_target="tpu_custom_call" | custom-call | tf_op jit(solution)/shard_map/pallas_call | solution.py:189
  2.6 0.0 copy-start
  2.6 3.1 %collective-permute-start = (bf16[64,640]{1,0:T(8,128)(2,1)}, bf16[64,640]{1,0:T(8,128)(2,1)S(1)}, u32[]{:S(2)}, u32[]{:S(2)}) collective-permute-start(bf16[64,640]{1,0:T(8,128)(2,1)} %shard_map.77), channel_id=1, source_target_pairs={{0,8},{4,12},{8,0},{12,4},{16,24},{20,28},{24,16},{28,20},{1,9},{5... | collective-permute-start | bytes 245768 | tf_op jit(solution)/shard_map/ppermute | solution.py:173
  5.7 0.0 copy-done
  5.7 1.5 %collective-permute-start.3 = (s32[1,64]{1,0:T(1,128)S(1)}, s32[1,64]{1,0:T(1,128)S(1)}, u32[]{:S(2)}, u32[]{:S(2)}) collective-permute-start(s32[1,64]{1,0:T(1,128)S(1)} %bitcast.2), channel_id=1, source_target_pairs={{0,2},{1,3},{2,0},{3,1},{4,6},{5,7},{6,4},{7,5},{8,10},{9,11},{10,... | collective-permute-start | bytes 776 | tf_op jit(solution)/shard_map/ppermute | solution.py:173
  7.2 0.8 %slice.42 = bf16[64,256]{1,0:T(8,128)(2,1)S(1)} slice(bf16[64,640]{1,0:T(8,128)(2,1)} %shard_map.77), slice={[0:64], [384:640]} | slice | bytes 65536 | tf_op jit(solution)/shard_map/slice | solution.py:199
  8.0 0.8 %slice.40 = bf16[64,384]{1,0:T(8,128)(2,1)S(1)} slice(bf16[64,640]{1,0:T(8,128)(2,1)} %shard_map.77), slice={[0:64], [0:384]} | slice | bytes 98304 | tf_op jit(solution)/shard_map/slice | solution.py:199
  8.8 0.0 collective-permute-done
  8.8 1.6 %collective-permute-start.2 = (bf16[128,256]{1,0:T(8,128)(2,1)S(1)}, bf16[128,256]{1,0:T(8,128)(2,1)S(1)}, u32[]{:S(2)}, u32[]{:S(2)}) collective-permute-start(bf16[128,256]{1,0:T(8,128)(2,1)S(1)} %pad_maximum_fusion.4), channel_id=1, source_target_pairs={{0,2},{1,3},{2,0},{3,1},{4,6},{5,7},{6,4},{7,5},{8,10},{9,11},{10,... | collective-permute-start | bytes 196616 | tf_op jit(solution)/shard_map/ppermute | solution.py:173
  10.4 2.7 %collective-permute-start.1 = (bf16[128,384]{1,0:T(8,128)(2,1)S(1)}, bf16[128,384]{1,0:T(8,128)(2,1)S(1)}, u32[]{:S(2)}, u32[]{:S(2)}) collective-permute-start(bf16[128,384]{1,0:T(8,128)(2,1)S(1)} %pad_maximum_fusion.3), channel_id=1, source_target_pairs={{0,16},{4,20},{8,24},{12,28},{16,0},{20,4},{24,8},{28,12},{1,17},{... | collective-permute-start | bytes 294920 | tf_op jit(solution)/shard_map/ppermute | solution.py:173
  13.0 0.1 collective-permute-done.2
  13.1 0.0 collective-permute-done.3.refs_7_
  13.2 2.7 %collective-permute-start.4 = (bf16[256,256]{1,0:T(8,128)(2,1)S(1)}, bf16[256,256]{1,0:T(8,128)(2,1)S(1)}, u32[]{:S(2)}, u32[]{:S(2)}) collective-permute-start(bf16[256,256]{1,0:T(8,128)(2,1)S(1)} %pad_maximum_fusion.2), channel_id=1, source_target_pairs={{0,16},{4,20},{8,24},{12,28},{16,0},{20,4},{24,8},{28,12},{1,17},{... | collective-permute-start | bytes 393224 | tf_op jit(solution)/shard_map/ppermute | solution.py:173
  15.8 5.1 %collective-permute-done.1 = bf16[128,384]{1,0:T(8,128)(2,1)S(1)} collective-permute-done((bf16[128,384]{1,0:T(8,128)(2,1)S(1)}, bf16[128,384]{1,0:T(8,128)(2,1)S(1)}, u32[]{:S(2)}, u32[]{:S(2)}) %collective-permute-start.1) | collective-permute-done | bytes 98336 | tf_op jit(solution)/shard_map/ppermute | solution.py:173
  20.9 11.1 %all_gather.3.near_ref.refs_0_ = bf16[1024,384]{1,0:T(8,128)(2,1)S(1)} all-gather(bf16[256,384]{1,0:T(8,128)(2,1)S(1)} %pad_maximum_fusion.1), channel_id=1, replica_groups=mesh['row'=8,'col'=4] {'col'}, dimensions={0}, use_global_device_ids=true | all-gather | bytes 983040 | tf_op jit(solution)/shard_map/all_gather | solution.py:217
  32.0 0.0 collective-permute-done.4
  32.0 0.1 collective-permute-start.5
  32.1 1.3 %shard_map.78 = (bf16[512,256]{1,0:T(8,128)(2,1)S(1)}, bf16[1024,256]{1,0:T(8,128)(2,1)S(1)}, f32[512,256]{1,0:T(8,128)S(1)}) custom-call(bf16[1024,384]{1,0:T(8,128)(2,1)S(1)} %all_gather.3.near_ref.refs_0_), custom_call_target="tpu_custom_call" | custom-call | flops 536870912 | bytes 2097152 | tf_op jit(solution)/shard_map/pallas_call | solution.py:222
  33.4 1.0 %collective-permute-done.5.refs_0_.refs_1_ = bf16[1024,384]{1,0:T(8,128)(2,1)S(1)} collective-permute-done((bf16[1024,384]{1,0:T(8,128)(2,1)S(1)}, bf16[1024,384]{1,0:T(8,128)(2,1)S(1)}, u32[]{:S(2)}, u32[]{:S(2)}) %collective-permute-start.5) | collective-permute-done | bytes 786464 | tf_op jit(solution)/shard_map/ppermute | solution.py:173
  34.4 1.6 %shard_map.79 = (bf16[1024,256]{1,0:T(8,128)(2,1)S(1)}, bf16[512,256]{1,0:T(8,128)(2,1)S(1)}, f32[128,128]{1,0:T(8,128)S(1)}) custom-call(bf16[1024,384]{1,0:T(8,128)(2,1)S(1)} %collective-permute-done.5.refs_0_.refs_1_, bf16[512,256]{1,0:T(8,128)(2,1)S(1)} %get-tuple-element.17.refs_1_.refs_2_, f32[512,256]{1,0:T(8,128)S(1)} %get-tuple-element.19.refs_2_, ...), custom_call_target="tpu_custom_call" | custom-call | tf_op jit(solution)/shard_map/pallas_call | solution.py:238
  35.9 0.2 collective-permute-start.6
  36.1 2.0 %shard_map.80 = (f32[128,128]{1,0:T(8,128)S(1)}, f32[128,128]{1,0:T(8,128)S(1)}) custom-call(bf16[1024,384]{1,0:T(8,128)(2,1)S(1)} %all_gather.3.near_ref.refs_0_, bf16[1024,384]{1,0:T(8,128)(2,1)S(1)} %collective-permute-done.5.refs_0_.refs_1_, bf16[512,256]{1,0:T(8,128)(2,1)S(1)} %get-tuple-element.17.refs_1_.refs_2_, ...), custom_call_target="tpu_custom_call" | custom-call | flops 536870912 | bytes 2097152 | tf_op jit(solution)/shard_map/pallas_call | solution.py:250
  38.2 0.0 collective-permute-done.6
  38.2 0.6 %collective-permute-start.7 = (f32[128,128]{1,0:T(8,128)S(1)}, f32[128,128]{1,0:T(8,128)S(1)}, u32[]{:S(2)}, u32[]{:S(2)}) collective-permute-start(f32[128,128]{1,0:T(8,128)S(1)} %pad_maximum_fusion.5), channel_id=1, source_target_pairs={{0,1},{1,0},{2,3},{3,2},{4,5},{5,4},{6,7},{7,6},{8,9},{9,8},{10,11... | collective-permute-start | bytes 196616 | tf_op jit(solution)/shard_map/ppermute | solution.py:173
  38.8 3.8 %collective-permute-done.7 = f32[128,128]{1,0:T(8,128)S(1)} collective-permute-done((f32[128,128]{1,0:T(8,128)S(1)}, f32[128,128]{1,0:T(8,128)S(1)}, u32[]{:S(2)}, u32[]{:S(2)}) %collective-permute-start.7) | collective-permute-done | bytes 65568 | tf_op jit(solution)/shard_map/ppermute | solution.py:173
  42.7 0.6 %slice_add_fusion = (f32[64,128]{1,0:T(8,128)}, f32[64,128]{1,0:T(8,128)}) fusion(f32[128,128]{1,0:T(8,128)S(1)} %collective-permute-done.7, f32[128,128]{1,0:T(8,128)S(1)} %add.9, f32[128,128]{1,0:T(8,128)S(1)} %get-tuple-element.25), kind=kLoop, calls=%fused_computation.6 | loop fusion | flops 16384 | bytes 196608 | tf_op jit(solution)/shard_map/add | solution.py:264
  (11 shorter events, 0.1 us)
Async XLA Ops:
  2.6 3.1 %copy-start = (s32[64]{0:T(128)S(1)}, s32[64]{0:T(128)}, u32[]{:S(2)}) copy-start(s32[64]{0:T(128)} %param.10) | copy-start | bytes 772
  2.6 6.2 %collective-permute-start = (bf16[64,640]{1,0:T(8,128)(2,1)}, bf16[64,640]{1,0:T(8,128)(2,1)S(1)}, u32[]{:S(2)}, u32[]{:S(2)}) collective-permute-start(bf16[64,640]{1,0:T(8,128)(2,1)} %shard_map.77), channel_id=1, source_target_pairs={{0,8},{4,12},{8,0},{12,4},{16,24},{20,28},{24,16},{28,20},{1,9},{5... | collective-permute-start | bytes 245768 | tf_op jit(solution)/shard_map/ppermute | solution.py:173
  5.7 7.5 %collective-permute-start.3 = (s32[1,64]{1,0:T(1,128)S(1)}, s32[1,64]{1,0:T(1,128)S(1)}, u32[]{:S(2)}, u32[]{:S(2)}) collective-permute-start(s32[1,64]{1,0:T(1,128)S(1)} %bitcast.2), channel_id=1, source_target_pairs={{0,2},{1,3},{2,0},{3,1},{4,6},{5,7},{6,4},{7,5},{8,10},{9,11},{10,... | collective-permute-start | bytes 776 | tf_op jit(solution)/shard_map/ppermute | solution.py:173
  8.8 4.3 %collective-permute-start.2 = (bf16[128,256]{1,0:T(8,128)(2,1)S(1)}, bf16[128,256]{1,0:T(8,128)(2,1)S(1)}, u32[]{:S(2)}, u32[]{:S(2)}) collective-permute-start(bf16[128,256]{1,0:T(8,128)(2,1)S(1)} %pad_maximum_fusion.4), channel_id=1, source_target_pairs={{0,2},{1,3},{2,0},{3,1},{4,6},{5,7},{6,4},{7,5},{8,10},{9,11},{10,... | collective-permute-start | bytes 196616 | tf_op jit(solution)/shard_map/ppermute | solution.py:173
  10.4 10.5 %collective-permute-start.1 = (bf16[128,384]{1,0:T(8,128)(2,1)S(1)}, bf16[128,384]{1,0:T(8,128)(2,1)S(1)}, u32[]{:S(2)}, u32[]{:S(2)}) collective-permute-start(bf16[128,384]{1,0:T(8,128)(2,1)S(1)} %pad_maximum_fusion.3), channel_id=1, source_target_pairs={{0,16},{4,20},{8,24},{12,28},{16,0},{20,4},{24,8},{28,12},{1,17},{... | collective-permute-start | bytes 294920 | tf_op jit(solution)/shard_map/ppermute | solution.py:173
  13.2 18.8 %collective-permute-start.4 = (bf16[256,256]{1,0:T(8,128)(2,1)S(1)}, bf16[256,256]{1,0:T(8,128)(2,1)S(1)}, u32[]{:S(2)}, u32[]{:S(2)}) collective-permute-start(bf16[256,256]{1,0:T(8,128)(2,1)S(1)} %pad_maximum_fusion.2), channel_id=1, source_target_pairs={{0,16},{4,20},{8,24},{12,28},{16,0},{20,4},{24,8},{28,12},{1,17},{... | collective-permute-start | bytes 393224 | tf_op jit(solution)/shard_map/ppermute | solution.py:173
  32.0 2.4 %collective-permute-start.5 = (bf16[1024,384]{1,0:T(8,128)(2,1)S(1)}, bf16[1024,384]{1,0:T(8,128)(2,1)S(1)}, u32[]{:S(2)}, u32[]{:S(2)}) collective-permute-start(bf16[1024,384]{1,0:T(8,128)(2,1)S(1)} %all_gather.3.near_ref.refs_0_), channel_id=1, source_target_pairs={{0,4},{4,0},{8,12},{12,8},{16,20},{20,16},{24,28},{28,24},{1,5},{5... | collective-permute-start | bytes 2359304 | tf_op jit(solution)/shard_map/ppermute | solution.py:173
  35.9 2.2 %collective-permute-start.6 = (f32[128,128]{1,0:T(8,128)S(1)}, f32[128,128]{1,0:T(8,128)S(1)}, u32[]{:S(2)}, u32[]{:S(2)}) collective-permute-start(f32[128,128]{1,0:T(8,128)S(1)} %get-tuple-element.27), channel_id=1, source_target_pairs={{0,4},{4,0},{8,12},{12,8},{16,20},{20,16},{24,28},{28,24},{1,5},{5... | collective-permute-start | bytes 196616 | tf_op jit(solution)/shard_map/ppermute | solution.py:173
  38.2 4.5 %collective-permute-start.7 = (f32[128,128]{1,0:T(8,128)S(1)}, f32[128,128]{1,0:T(8,128)S(1)}, u32[]{:S(2)}, u32[]{:S(2)}) collective-permute-start(f32[128,128]{1,0:T(8,128)S(1)} %pad_maximum_fusion.5), channel_id=1, source_target_pairs={{0,1},{1,0},{2,3},{3,2},{4,5},{5,4},{6,7},{7,6},{8,9},{9,8},{10,11... | collective-permute-start | bytes 196616 | tf_op jit(solution)/shard_map/ppermute | solution.py:173

commit v3 on v2

--- a/solution.py
+++ b/solution.py
@@ -46,7 +46,8 @@
 
 
 def head_kernel(width, *refs):
-    out_ref, held, semaphores = refs[5], refs[6:11], refs[11]
+    out_ref, columns_ref, observed_ref = refs[5:8]
+    held, semaphores = refs[8:13], refs[13]
     copies = [
         pltpu.make_async_copy(source, target, semaphores.at[index])
         for index, (source, target) in enumerate(zip(refs[:5], held))
@@ -67,41 +68,24 @@
     )
     epoch = lax.broadcasted_iota(jnp.int32, (rows, epochs), 1).astype(F32)
     targets = jnp.where(epoch < lengths, targets_ref[...].astype(F32), jnp.inf)
-    out_ref[:, :width] = embed_ref[...]
-    out_ref[:, width : width + epochs] = fitted.astype(BF16)
+    columns = jnp.concatenate([embed_ref[...], fitted.astype(BF16)], axis=1)
+    columns_ref[...] = columns
+    observed_ref[...] = targets.astype(BF16)
+    out_ref[:, : width + epochs] = columns
     out_ref[:, width + epochs :] = targets.astype(BF16)
 
 
-def fit_chunks(left, right_ref, fields_ref, scale, width, chunk):
-    total = None
-    for at in range(0, fields_ref.shape[0], chunk):
-        kernel = jnp.exp2(nt_dot(left, right_ref[at : at + chunk, :]) * scale).astype(BF16)
-        part = nn_dot(kernel, fields_ref[at : at + chunk, width:])
-        total = part if total is None else total + part
-    return total
-
-
-def block_of(ref, block, rows, mask):
+def observed_kernel(first, own_ref, other_ref, out_ref):
+    out_ref[: own_ref.shape[0], :] = own_ref[...]
+    out_ref[own_ref.shape[0] :, :] = other_ref[:, first:]
+
+
+def block_of(block, rows, mask):
     return pl.ds(pl.multiple_of((lax.axis_index("col") ^ mask) * block, block), rows)
-
-
-def near_kernel(scale, chunk, near_ref, left_ref, right_ref, fit_ref):
-    width = left_ref.shape[1] // 2
-    block = near_ref.shape[0] // lax.axis_size("col")
-    for part in range(left_ref.shape[0] // block):
-        embed = near_ref[block_of(near_ref, block, block, 2 * part), :width]
-        left_ref[part * block : (part + 1) * block, :] = extended(embed)(3, 0)
-    for at in range(0, near_ref.shape[0], chunk):
-        right_ref[at : at + chunk, :] = extended(near_ref[at : at + chunk, :width])(0, 3)
-    fit_ref[...] = fit_chunks(left_ref[...], right_ref, near_ref, scale, width, chunk)
 
 
 def with_ones(embed):
     return jnp.concatenate([embed, jnp.ones_like(embed)], axis=1)
-
-
-def weighted(scale, fields, adjoint, right, left):
-    return (nt_dot(fields, adjoint) * jnp.exp2(nt_dot(right, left) * scale)).astype(BF16)
 
 
 def gradient(factor, summed, embed):
@@ -109,54 +93,86 @@
     return factor * (summed[:, :width] - embed.astype(F32) * summed[:, width:])
 
 
-def column_part(scale, factor, own, adjoint, left, fields_ref, right_ref):
-    width = left.shape[1] // 2
-    block = fields_ref.shape[0] // lax.axis_size("col")
-    picks = [block_of(fields_ref, block, own, mask) for mask in (0, 1)]
-    fields = jnp.concatenate([fields_ref[pick, width:] for pick in picks], axis=0)
-    right = jnp.concatenate([right_ref[pick, :] for pick in picks], axis=0)
-    weight = weighted(scale, fields, adjoint, right, left)
-    return gradient(factor, nn_dot(weight, with_ones(left[:, :width])), right[:, :width])
-
-
-def far_kernel(scale, factor, chunk, parts, own, run, *refs):
-    far_ref, left_ref, fit_ref, targets_ref, right_ref, adjoint_ref, col_ref = refs
+def slot_runs(ref, own, block):
+    return jnp.concatenate(
+        [ref[at : at + own, :] for at in range(0, ref.shape[0], block)], axis=0
+    )
+
+
+def fit_part(scale, chunk, own, columns_ref, left_ref, right_ref, slots_ref, picks_ref):
     width = left_ref.shape[1] // 2
-    held = left_ref.shape[0]
-    for at in range(0, far_ref.shape[0], chunk):
-        right_ref[at : at + chunk, :] = extended(far_ref[at : at + chunk, :width])(0, 3)
     left = left_ref[...]
-    fit = fit_ref[...] + fit_chunks(left, right_ref, far_ref, scale, width, chunk)
-    for at in range(0, held, run):
-        part, piece = divmod(at, held // parts)
-        first = piece * parts + part * run
-        targets = targets_ref[first : first + run, :].astype(F32)
-        adjoint = jnp.where(targets == jnp.inf, 0.0, targets - fit[at : at + run])
-        adjoint_ref[at : at + run, :] = adjoint.astype(BF16)
-    col_ref[...] = column_part(scale, factor, own, adjoint_ref[...], left, far_ref, right_ref)
-
-
-def last_kernel(scale, factor, chunk, parts, own, *refs):
-    near_ref, far_ref, left_ref, right_near_ref, right_far_ref, adjoint_ref = refs[:6]
-    ids_refs, (col_ref, row_ref) = refs[6 : 6 + parts], refs[6 + parts :]
+    slots_left = slot_runs(left_ref, own, chunk)
+    total = None
+    for at in range(0, columns_ref.shape[0], chunk):
+        span = slice(at, at + chunk)
+        right = extended(columns_ref[span, :width])(0, 3)
+        right_ref[span, :] = right
+        kernel = jnp.exp2(nt_dot(left, right) * scale).astype(BF16)
+        part = nn_dot(kernel, columns_ref[span, width:])
+        total = part if total is None else total + part
+        slots_ref[:, span] = jnp.exp2(nt_dot(slots_left, right) * scale)
+    for mask in (0, 1):
+        right = right_ref[block_of(chunk, own, mask), :]
+        picks_ref[mask * own : (mask + 1) * own, :] = jnp.exp2(nt_dot(right, left) * scale)
+    return total
+
+
+def near_kernel(scale, chunk, own, near_ref, left_ref, fit_ref, slots_ref, picks_ref, right_ref):
     width = left_ref.shape[1] // 2
-    block = left_ref.shape[0] // parts
-    col_ref[...] = column_part(
-        scale, factor, own, adjoint_ref[...], left_ref[...], near_ref, right_near_ref
-    )
-    starts = range(0, parts * block, block)
-    slots_left = jnp.concatenate([left_ref[at : at + own, :] for at in starts], axis=0)
-    slots_adjoint = jnp.concatenate([adjoint_ref[at : at + own, :] for at in starts], axis=0)
+    for part in range(left_ref.shape[0] // chunk):
+        embed = near_ref[block_of(chunk, chunk, 2 * part), :width]
+        left_ref[part * chunk : (part + 1) * chunk, :] = extended(embed)(3, 0)
+    fit_ref[...] = fit_part(
+        scale, chunk, own, near_ref, left_ref, right_ref, slots_ref, picks_ref
+    )
+
+
+def far_kernel(scale, chunk, own, far_ref, left_ref, near_fit_ref, fit_ref, slots_ref, picks_ref, right_ref):
+    fit_ref[...] = near_fit_ref[...] + fit_part(
+        scale, chunk, own, far_ref, left_ref, right_ref, slots_ref, picks_ref
+    )
+
+
+def column_part(factor, own, block, adjoint, embed, columns_ref, kernel_ref):
+    width = embed.shape[1]
+    columns = jnp.concatenate(
+        [columns_ref[block_of(block, own, mask), :] for mask in (0, 1)], axis=0
+    )
+    weight = (nt_dot(columns[:, width:], adjoint) * kernel_ref[...]).astype(BF16)
+    return gradient(factor, nn_dot(weight, with_ones(embed)), columns[:, :width])
+
+
+def adjoint_kernel(factor, own, far_ref, left_ref, fit_ref, kernel_ref, *refs):
+    targets_refs, (adjoint_ref, col_ref) = refs[:-2], refs[-2:]
+    width = left_ref.shape[1] // 2
+    block = targets_refs[0].shape[0]
+    for part, targets_ref in enumerate(targets_refs):
+        span = slice(part * block, (part + 1) * block)
+        targets = targets_ref[...].astype(F32)
+        adjoint = jnp.where(targets == jnp.inf, 0.0, targets - fit_ref[span, :])
+        adjoint_ref[span, :] = adjoint.astype(BF16)
+    embed = left_ref[:, :width]
+    col_ref[...] = column_part(factor, own, block, adjoint_ref[...], embed, far_ref, kernel_ref)
+
+
+def last_kernel(factor, chunk, parts, own, *refs):
+    near_ref, far_ref, left_ref, adjoint_ref, near_slots_ref, picks_ref, far_slots_ref = refs[:7]
+    ids_refs, (col_ref, row_ref) = refs[7 : 7 + parts], refs[7 + parts :]
+    width = left_ref.shape[1] // 2
+    embed = left_ref[:, :width]
+    col_ref[...] = column_part(factor, own, chunk, adjoint_ref[...], embed, near_ref, picks_ref)
+    slots_embed = slot_runs(left_ref, own, chunk)[:, :width]
+    slots_adjoint = slot_runs(adjoint_ref, own, chunk)
     summed = None
-    for fields_ref, right_ref in ((near_ref, right_near_ref), (far_ref, right_far_ref)):
-        for at in range(0, fields_ref.shape[0], chunk):
+    for columns_ref, kernel_ref in ((near_ref, near_slots_ref), (far_ref, far_slots_ref)):
+        for at in range(0, columns_ref.shape[0], chunk):
             span = slice(at, at + chunk)
-            weight = weighted(
-                scale, slots_adjoint, fields_ref[span, width:], slots_left, right_ref[span, :]
-            )
-            part = nn_dot(weight, with_ones(fields_ref[span, :width]))
+            link = nt_dot(slots_adjoint, columns_ref[span, width:])
+            weight = (link * kernel_ref[:, span]).astype(BF16)
+            part = nn_dot(weight, with_ones(columns_ref[span, :width]))
             summed = part if summed is None else summed + part
-    slot_rows = gradient(factor, summed, slots_left[:, :width])
+    slot_rows = gradient(factor, summed, slots_embed)
     ids = jnp.concatenate([jnp.broadcast_to(ref[...], (own, own)) for ref in ids_refs], axis=1)
     wanted = lax.broadcasted_iota(jnp.int32, ids.shape, 0)
     first = lax.axis_index("row") * lax.axis_size("col")
@@ -186,79 +202,96 @@
     shape = jax.ShapeDtypeStruct
 
     arrays = (curve_embed, solution, targets, lengths.reshape(1, own), epoch_kernel)
-    packed = pl.pallas_call(
+    packed, columns, observed = pl.pallas_call(
         functools.partial(head_kernel, width),
-        out_shape=shape((own, width + 2 * epochs), BF16),
+        out_shape=(
+            shape((own, width + 2 * epochs), BF16),
+            shape((own, width + epochs), BF16),
+            shape((own, epochs), BF16),
+        ),
         in_specs=[pl.BlockSpec(memory_space=pltpu.HBM)] * 5,
-        out_specs=VMEM,
+        out_specs=[VMEM] * 3,
         scratch_shapes=[
             *(pltpu.VMEM(array.shape, array.dtype) for array in arrays),
             pltpu.SemaphoreType.DMA((5,)),
         ],
     )(*arrays)
-    columns, observed = packed[:, : width + epochs], packed[:, width + epochs :]
-    ids = [slot_curve.reshape(1, own)]
-    step = 2
-    if step < rows_axis:
+    ids, halves = [slot_curve.reshape(1, own)], [observed]
+    step = rows_axis // 2
+    if step > 1:
         other = swap(packed, "row", step)
         columns = jnp.concatenate([columns, other[:, : width + epochs]], axis=0)
-        observed = jnp.concatenate([observed, other[:, width + epochs :]], axis=0)
-        step *= 2
-    run = observed.shape[0]
+        observed = pl.pallas_call(
+            functools.partial(observed_kernel, width + epochs),
+            out_shape=shape((2 * own, epochs), BF16),
+            in_specs=[VMEM] * 2,
+            out_specs=VMEM,
+            compiler_params=PARAMS,
+            cost_estimate=pl.CostEstimate(
+                flops=1 << 30, bytes_accessed=other.nbytes, transcendentals=0
+            ),
+        )(observed, other)
+        halves, step = [observed], step // 2
     turn = 2
     while turn < cols_axis:
-        observed = joined(observed, "col", turn)
         ids += [swap(array, "col", turn) for array in ids]
         turn *= 2
-    observed, ids = lax.optimization_barrier((observed, ids))
-    while step < rows_axis:
-        columns, observed = joined(columns, "row", step), joined(observed, "row", step)
-        step *= 2
+    while step > 1:
+        columns, halves = joined(columns, "row", step), [observed, swap(observed, "row", step)]
+        step //= 2
+        if step > 1:
+            observed = jnp.concatenate(halves, axis=0)
     near = lax.all_gather(columns, "col", axis=0, tiled=True)
-    near, observed = lax.optimization_barrier((near, observed))
+    near, halves, ids = lax.optimization_barrier((near, halves, ids))
+    observed = jnp.concatenate(halves, axis=0)
     far = swap(near, "row", 1)
-    parts, held, half = len(ids), observed.shape[0], near.shape[0]
-    chunk = columns.shape[0]
-    left, right_near, fit = pl.pallas_call(
-        functools.partial(near_kernel, scale, chunk),
-        out_shape=(
-            shape((held, 2 * width), BF16),
-            shape((half, 2 * width), BF16),
-            shape((held, epochs), F32),
-        ),
+    observed = [observed]
+    turn = 2
+    while turn < cols_axis:
+        observed += [swap(array, "col", turn) for array in observed]
+        turn *= 2
+    parts, half, chunk = len(ids), near.shape[0], columns.shape[0]
+    held = parts * chunk
+    cost = pl.CostEstimate(
+        flops=2 * held * half * (2 * width + epochs),
+        bytes_accessed=2 << 20,
+        transcendentals=held * half,
+    )
+    kernels = (shape((parts * own, half), F32), shape((2 * own, held), F32))
+    left, fit, *near_kernels = pl.pallas_call(
+        functools.partial(near_kernel, scale, chunk, own),
+        out_shape=(shape((held, 2 * width), BF16), shape((held, epochs), F32), *kernels),
         in_specs=[VMEM],
+        out_specs=[VMEM] * 4,
+        scratch_shapes=[pltpu.VMEM((half, 2 * width), BF16)],
+        compiler_params=PARAMS,
+        cost_estimate=cost,
+    )(near)
+    fit, *far_kernels = pl.pallas_call(
+        functools.partial(far_kernel, scale, chunk, own),
+        out_shape=(shape((held, epochs), F32), *kernels),
+        in_specs=[VMEM] * 3,
         out_specs=[VMEM] * 3,
+        scratch_shapes=[pltpu.VMEM((half, 2 * width), BF16)],
         compiler_params=PARAMS,
-        cost_estimate=pl.CostEstimate(
-            flops=2 * held * half * (2 * width + epochs),
-            bytes_accessed=2 << 20,
-            transcendentals=held * half,
-        ),
-    )(near)
-    right_far, adjoint, col_far = pl.pallas_call(
-        functools.partial(far_kernel, scale, factor, chunk, parts, own, run),
-        out_shape=(
-            shape((half, 2 * width), BF16),
-            shape((held, epochs), BF16),
-            shape((2 * own, width), F32),
-        ),
-        in_specs=[VMEM] * 4,
-        out_specs=[VMEM] * 3,
+        cost_estimate=cost,
+    )(far, left, fit)
+    adjoint, col_far = pl.pallas_call(
+        functools.partial(adjoint_kernel, factor, own),
+        out_shape=(shape((held, epochs), BF16), shape((2 * own, width), F32)),
+        in_specs=[VMEM] * (4 + parts),
+        out_specs=[VMEM] * 2,
         compiler_params=PARAMS,
-    )(far, left, fit, observed)
+    )(far, left, fit, far_kernels[1], *observed)
     col_other = swap(col_far, "row", 1)
     col_near, row_part = pl.pallas_call(
-        functools.partial(last_kernel, scale, factor, chunk, parts, own),
+        functools.partial(last_kernel, factor, chunk, parts, own),
         out_shape=(shape((2 * own, width), F32),) * 2,
-        in_specs=[VMEM] * (6 + parts),
+        in_specs=[VMEM] * (7 + parts),
         out_specs=[VMEM] * 2,
         compiler_params=PARAMS,
-        cost_estimate=pl.CostEstimate(
-            flops=2 * held * half * (2 * width + epochs),
-            bytes_accessed=2 << 20,
-            transcendentals=held * half,
-        ),
-    )(near, far, left, right_near, right_far, adjoint, *ids)
+        cost_estimate=cost,
+    )(near, far, left, adjoint, *near_kernels, far_kernels[0], *ids)
     col_part = col_near + col_other
     other = swap(jnp.concatenate([col_part[own:], row_part[own:]], axis=0), "col", 1)
     return row_part[:own] + other[own:], col_part[:own] + other[:own]

time: 43.6 us -> 41.8 us (0.959)
  local copies, waits for them, and re-layouts: 1.59 us -> 0.05 us
  starting transfers between devices: 12.4 us -> 10.9 us
  blocking collectives: 11.1 us -> 12.2 us
    slice x3 -> x0, local copies, waits for them, and re-layouts: 1.57 us -> none  [the longest x2 1.56 us: gathered_plan(): columns, observed = (packed[:, :width + epochs], packed[:, width + epochs:])]
    ppermute x8, starting transfers between devices: 12.4 us -> 10.9 us  [swap(): return lax.ppermute(array, axis, pairs)]
    all_gather x1, blocking collectives: 11.1 us -> 12.2 us  [gathered_plan(): near = lax.all_gather(columns, 'col', axis=0, tiled=True)]
    pallas_call x4 -> x6, Pallas kernels: 6.84 us -> 7.21 us  [the longest x1 1.98 us: gathered_plan(): pl.pallas_call(functools.partial(head_kernel, width), out_shape=(shape((o...]
  transfers between devices with their start and end apart: 8 -> 8, of which waited for: 4 -> 4; matrix products, arithmetic and copies ran while one was open for 4% -> 0% of each run, Pallas kernels for 8% -> 12%
where the time goes in v3:
time: 41.8 us; the launch traced here: 41.6 us
  blocking collectives  12.2 us (29%)
  starting transfers between devices  10.9 us (26%)
  waiting for transfers between devices  9.79 us (23%)
  Pallas kernels  7.21 us (17%)
  between operations  0.79 us (2%)
  other arithmetic  0.68 us (2%)
    all_gather x1, blocking collectives, gathered_plan(): near = lax.all_gather(columns, 'col', axis=0, tiled=True)  12.2 us
    ppermute x8, starting transfers between devices, swap(): return lax.ppermute(array, axis, pairs)  10.9 us
    ppermute x8, waiting for transfers between devices, swap(): return lax.ppermute(array, axis, pairs)  9.79 us
    pallas_call x1, Pallas kernels, gathered_plan(): pl.pallas_call(functools.partial(head_kernel, width), out_shape=(shape((o...  1.98 us
    pallas_call x1, Pallas kernels, gathered_plan(): pl.pallas_call(functools.partial(near_kernel, scale, chunk, own), out_sha...  1.73 us
    pallas_call x1, Pallas kernels, gathered_plan(): pl.pallas_call(functools.partial(far_kernel, scale, chunk, own), out_shap...  1.61 us
    pallas_call x1, Pallas kernels, gathered_plan(): pl.pallas_call(functools.partial(last_kernel, factor, chunk, parts, own),...  1.48 us
  transfers between devices with their start and end apart: 8, of which 4 were waited for; matrix products, arithmetic and copies ran while one was open for 0% of the time, Pallas kernels for 12%

profile of v3, /device:TPU:0, one launch (start us, length us, event | category | flops | bytes accessed | tf_op | source)
XLA Modules:
  0.0 41.6 jit_solution(16676234886738844733)
XLA Ops:
  0.6 2.0 %shard_map.77 = (bf16[64,640]{1,0:T(8,128)(2,1)}, bf16[64,384]{1,0:T(8,128)(2,1)}, bf16[64,256]{1,0:T(8,128)(2,1)}) custom-call(bf16[64,128]{1,0:T(8,128)(2,1)} %refs_0_.1, f32[64,256]{1,0:T(8,128)} %refs_1_.1, bf16[64,256]{1,0:T(8,128)(2,1)} %refs_2_.1, s32[1,64]{1,0:T(1,128)} %bitcast.4, f32[256,256]{1,0:T(8,128)} %refs_4_.1), custom_call_target="tpu_custom_call" | custom-call | tf_op jit(solution)/shard_map/pallas_call | solution.py:205
  2.6 0.0 copy-start
  2.6 4.1 %collective-permute-start = (bf16[64,640]{1,0:T(8,128)(2,1)}, bf16[64,640]{1,0:T(8,128)(2,1)S(1)}, u32[]{:S(2)}, u32[]{:S(2)}) collective-permute-start(bf16[64,640]{1,0:T(8,128)(2,1)} %get-tuple-element.22), channel_id=1, source_target_pairs={{0,16},{4,20},{8,24},{12,28},{16,0},{20,4},{24,8},{28,12},{1,17},{... | collective-permute-start | bytes 245768 | tf_op jit(solution)/shard_map/ppermute | solution.py:189
  6.7 0.0 copy-done
  6.7 0.0 copy-start.2
  6.7 1.5 %collective-permute-start.3 = (s32[1,64]{1,0:T(1,128)S(1)}, s32[1,64]{1,0:T(1,128)S(1)}, u32[]{:S(2)}, u32[]{:S(2)}) collective-permute-start(s32[1,64]{1,0:T(1,128)S(1)} %bitcast.2), channel_id=1, source_target_pairs={{0,2},{1,3},{2,0},{3,1},{4,6},{5,7},{6,4},{7,5},{8,10},{9,11},{10,... | collective-permute-start | bytes 776 | tf_op jit(solution)/shard_map/ppermute | solution.py:189
  8.3 2.9 %collective-permute-done.other_ref = bf16[64,640]{1,0:T(8,128)(2,1)S(1)} collective-permute-done((bf16[64,640]{1,0:T(8,128)(2,1)}, bf16[64,640]{1,0:T(8,128)(2,1)S(1)}, u32[]{:S(2)}, u32[]{:S(2)}) %collective-permute-start) | collective-permute-done | bytes 81952 | tf_op jit(solution)/shard_map/ppermute | solution.py:189
  11.1 0.0 copy-done.2
  11.2 0.0 copy-start.1
  11.2 0.9 %collective-permute-start.1 = (bf16[128,384]{1,0:T(8,128)(2,1)S(1)}, bf16[128,384]{1,0:T(8,128)(2,1)S(1)}, u32[]{:S(2)}, u32[]{:S(2)}) collective-permute-start(bf16[128,384]{1,0:T(8,128)(2,1)S(1)} %pad_maximum_fusion.1), channel_id=1, source_target_pairs={{0,8},{4,12},{8,0},{12,4},{16,24},{20,28},{24,16},{28,20},{1,9},{5... | collective-permute-start | bytes 294920 | tf_op jit(solution)/shard_map/ppermute | solution.py:189
  12.1 0.0 copy-done.1
  12.1 1.3 %collective-permute-start.2 = (bf16[128,256]{1,0:T(8,128)(2,1)S(1)}, bf16[128,256]{1,0:T(8,128)(2,1)S(1)}, u32[]{:S(2)}, u32[]{:S(2)}) collective-permute-start(bf16[128,256]{1,0:T(8,128)(2,1)S(1)} %shard_map.78), channel_id=1, source_target_pairs={{0,8},{4,12},{8,0},{12,4},{16,24},{20,28},{24,16},{28,20},{1,9},{5... | collective-permute-start | bytes 196616 | tf_op jit(solution)/shard_map/ppermute | solution.py:189
  13.4 2.7 %collective-permute-done.1 = bf16[128,384]{1,0:T(8,128)(2,1)S(1)} collective-permute-done((bf16[128,384]{1,0:T(8,128)(2,1)S(1)}, bf16[128,384]{1,0:T(8,128)(2,1)S(1)}, u32[]{:S(2)}, u32[]{:S(2)}) %collective-permute-start.1) | collective-permute-done | bytes 98336 | tf_op jit(solution)/shard_map/ppermute | solution.py:189
  16.1 12.2 %all_gather.3.near_ref.refs_0_ = bf16[1024,384]{1,0:T(8,128)(2,1)S(1)} all-gather(bf16[256,384]{1,0:T(8,128)(2,1)S(1)} %pad_maximum_fusion), channel_id=1, replica_groups=mesh['row'=8,'col'=4] {'col'}, dimensions={0}, use_global_device_ids=true | all-gather | bytes 983040 | tf_op jit(solution)/shard_map/all_gather | solution.py:244
  28.3 0.0 collective-permute-done.3.refs_8_
  28.3 0.0 collective-permute-done.2
  28.3 0.1 collective-permute-start.4
  28.4 1.5 %collective-permute-start.5 = (bf16[256,256]{1,0:T(8,128)(2,1)S(1)}, bf16[256,256]{1,0:T(8,128)(2,1)S(1)}, u32[]{:S(2)}, u32[]{:S(2)}) collective-permute-start(bf16[256,256]{1,0:T(8,128)(2,1)S(1)} %constant_dynamic-update-slice_fusion.refs_0_), channel_id=1, source_target_pairs={{0,2},{1,3},{2,0},{3,1},{4,6},{5,7},{6,4},{7,5},{8,10},{9,11},{10,... | collective-permute-start | bytes 393224 | tf_op jit(solution)/shard_map/ppermute | solution.py:189
  29.9 1.7 %shard_map.79 = (bf16[512,256]{1,0:T(8,128)(2,1)S(1)}, f32[512,256]{1,0:T(8,128)S(1)}, f32[128,1024]{1,0:T(8,128)S(1)}, f32[128,512]{1,0:T(8,128)S(1)}) custom-call(bf16[1024,384]{1,0:T(8,128)(2,1)S(1)} %all_gather.3.near_ref.refs_0_), custom_call_target="tpu_custom_call" | custom-call | flops 536870912 | bytes 2097152 | tf_op jit(solution)/shard_map/pallas_call | solution.py:261
  31.6 0.0 collective-permute-done.4.far_ref.refs_1_
  31.6 1.6 %shard_map.80 = (f32[512,256]{1,0:T(8,128)S(1)}, f32[128,1024]{1,0:T(8,128)S(1)}, f32[128,512]{1,0:T(8,128)S(1)}) custom-call(bf16[1024,384]{1,0:T(8,128)(2,1)S(1)} %collective-permute-done.4.far_ref.refs_1_, bf16[512,256]{1,0:T(8,128)(2,1)S(1)} %get-tuple-element.25.left_ref.refs_2_, f32[512,256]{1,0:T(8,128)S(1)} %get-tuple-element.26.near_fit_ref), custom_call_target="tpu_custom_call" | custom-call | flops 536870912 | bytes 2097152 | tf_op jit(solution)/shard_map/pallas_call | solution.py:270
  33.2 1.1 %collective-permute-done.5.refs_1_ = bf16[256,256]{1,0:T(8,128)(2,1)S(1)} collective-permute-done((bf16[256,256]{1,0:T(8,128)(2,1)S(1)}, bf16[256,256]{1,0:T(8,128)(2,1)S(1)}, u32[]{:S(2)}, u32[]{:S(2)}) %collective-permute-start.5) | collective-permute-done | bytes 131104 | tf_op jit(solution)/shard_map/ppermute | solution.py:189
  34.3 0.4 shard_map.81
  34.7 0.1 collective-permute-start.6
  34.8 1.5 %shard_map.82 = (f32[128,128]{1,0:T(8,128)S(1)}, f32[128,128]{1,0:T(8,128)S(1)}) custom-call(bf16[1024,384]{1,0:T(8,128)(2,1)S(1)} %all_gather.3.near_ref.refs_0_, bf16[1024,384]{1,0:T(8,128)(2,1)S(1)} %collective-permute-done.4.far_ref.refs_1_, bf16[512,256]{1,0:T(8,128)(2,1)S(1)} %get-tuple-element.25.left_ref.refs_2_, ...), custom_call_target="tpu_custom_call" | custom-call | flops 536870912 | bytes 2097152 | tf_op jit(solution)/shard_map/pallas_call | solution.py:287
  36.3 0.0 collective-permute-done.6
  36.4 1.5 %collective-permute-start.7 = (f32[128,128]{1,0:T(8,128)S(1)}, f32[128,128]{1,0:T(8,128)S(1)}, u32[]{:S(2)}, u32[]{:S(2)}) collective-permute-start(f32[128,128]{1,0:T(8,128)S(1)} %pad_maximum_fusion.2), channel_id=1, source_target_pairs={{0,1},{1,0},{2,3},{3,2},{4,5},{5,4},{6,7},{7,6},{8,9},{9,8},{10,11... | collective-permute-start | bytes 196616 | tf_op jit(solution)/shard_map/ppermute | solution.py:189
  37.8 3.1 %collective-permute-done.7 = f32[128,128]{1,0:T(8,128)S(1)} collective-permute-done((f32[128,128]{1,0:T(8,128)S(1)}, f32[128,128]{1,0:T(8,128)S(1)}, u32[]{:S(2)}, u32[]{:S(2)}) %collective-permute-start.7) | collective-permute-done | bytes 65568 | tf_op jit(solution)/shard_map/ppermute | solution.py:189
  40.9 0.6 %slice_add_fusion = (f32[64,128]{1,0:T(8,128)}, f32[64,128]{1,0:T(8,128)}) fusion(f32[128,128]{1,0:T(8,128)S(1)} %collective-permute-done.7, f32[128,128]{1,0:T(8,128)S(1)} %add.9, f32[128,128]{1,0:T(8,128)S(1)} %get-tuple-element.37), kind=kLoop, calls=%fused_computation.3 | loop fusion | flops 16384 | bytes 196608 | tf_op jit(solution)/shard_map/add | solution.py:297
  (10 shorter events, 0.1 us)
Async XLA Ops:
  2.6 4.1 %copy-start = (s32[64]{0:T(128)S(1)}, s32[64]{0:T(128)}, u32[]{:S(2)}) copy-start(s32[64]{0:T(128)} %param.10) | copy-start | bytes 772
  2.6 8.5 %collective-permute-start = (bf16[64,640]{1,0:T(8,128)(2,1)}, bf16[64,640]{1,0:T(8,128)(2,1)S(1)}, u32[]{:S(2)}, u32[]{:S(2)}) collective-permute-start(bf16[64,640]{1,0:T(8,128)(2,1)} %get-tuple-element.22), channel_id=1, source_target_pairs={{0,16},{4,20},{8,24},{12,28},{16,0},{20,4},{24,8},{28,12},{1,17},{... | collective-permute-start | bytes 245768 | tf_op jit(solution)/shard_map/ppermute | solution.py:189
  6.7 4.4 %copy-start.2 = (bf16[64,384]{1,0:T(8,128)(2,1)S(1)}, bf16[64,384]{1,0:T(8,128)(2,1)}, u32[]{:S(2)}) copy-start(bf16[64,384]{1,0:T(8,128)(2,1)} %get-tuple-element.21) | copy-start | bytes 147460
  6.7 21.5 %collective-permute-start.3 = (s32[1,64]{1,0:T(1,128)S(1)}, s32[1,64]{1,0:T(1,128)S(1)}, u32[]{:S(2)}, u32[]{:S(2)}) collective-permute-start(s32[1,64]{1,0:T(1,128)S(1)} %bitcast.2), channel_id=1, source_target_pairs={{0,2},{1,3},{2,0},{3,1},{4,6},{5,7},{6,4},{7,5},{8,10},{9,11},{10,... | collective-permute-start | bytes 776 | tf_op jit(solution)/shard_map/ppermute | solution.py:189
  11.2 0.9 %copy-start.1 = (bf16[64,256]{1,0:T(8,128)(2,1)S(1)}, bf16[64,256]{1,0:T(8,128)(2,1)}, u32[]{:S(2)}) copy-start(bf16[64,256]{1,0:T(8,128)(2,1)} %get-tuple-element.23.own_ref) | copy-start | bytes 98308
  11.2 4.9 %collective-permute-start.1 = (bf16[128,384]{1,0:T(8,128)(2,1)S(1)}, bf16[128,384]{1,0:T(8,128)(2,1)S(1)}, u32[]{:S(2)}, u32[]{:S(2)}) collective-permute-start(bf16[128,384]{1,0:T(8,128)(2,1)S(1)} %pad_maximum_fusion.1), channel_id=1, source_target_pairs={{0,8},{4,12},{8,0},{12,4},{16,24},{20,28},{24,16},{28,20},{1,9},{5... | collective-permute-start | bytes 294920 | tf_op jit(solution)/shard_map/ppermute | solution.py:189
  12.1 16.2 %collective-permute-start.2 = (bf16[128,256]{1,0:T(8,128)(2,1)S(1)}, bf16[128,256]{1,0:T(8,128)(2,1)S(1)}, u32[]{:S(2)}, u32[]{:S(2)}) collective-permute-start(bf16[128,256]{1,0:T(8,128)(2,1)S(1)} %shard_map.78), channel_id=1, source_target_pairs={{0,8},{4,12},{8,0},{12,4},{16,24},{20,28},{24,16},{28,20},{1,9},{5... | collective-permute-start | bytes 196616 | tf_op jit(solution)/shard_map/ppermute | solution.py:189
  28.3 3.3 %collective-permute-start.4 = (bf16[1024,384]{1,0:T(8,128)(2,1)S(1)}, bf16[1024,384]{1,0:T(8,128)(2,1)S(1)}, u32[]{:S(2)}, u32[]{:S(2)}) collective-permute-start(bf16[1024,384]{1,0:T(8,128)(2,1)S(1)} %all_gather.3.near_ref.refs_0_), channel_id=1, source_target_pairs={{0,4},{4,0},{8,12},{12,8},{16,20},{20,16},{24,28},{28,24},{1,5},{5... | collective-permute-start | bytes 2359304 | tf_op jit(solution)/shard_map/ppermute | solution.py:189
  28.4 5.9 %collective-permute-start.5 = (bf16[256,256]{1,0:T(8,128)(2,1)S(1)}, bf16[256,256]{1,0:T(8,128)(2,1)S(1)}, u32[]{:S(2)}, u32[]{:S(2)}) collective-permute-start(bf16[256,256]{1,0:T(8,128)(2,1)S(1)} %constant_dynamic-update-slice_fusion.refs_0_), channel_id=1, source_target_pairs={{0,2},{1,3},{2,0},{3,1},{4,6},{5,7},{6,4},{7,5},{8,10},{9,11},{10,... | collective-permute-start | bytes 393224 | tf_op jit(solution)/shard_map/ppermute | solution.py:189
  34.7 1.6 %collective-permute-start.6 = (f32[128,128]{1,0:T(8,128)S(1)}, f32[128,128]{1,0:T(8,128)S(1)}, u32[]{:S(2)}, u32[]{:S(2)}) collective-permute-start(f32[128,128]{1,0:T(8,128)S(1)} %get-tuple-element.39), channel_id=1, source_target_pairs={{0,4},{4,0},{8,12},{12,8},{16,20},{20,16},{24,28},{28,24},{1,5},{5... | collective-permute-start | bytes 196616 | tf_op jit(solution)/shard_map/ppermute | solution.py:189
  36.4 4.6 %collective-permute-start.7 = (f32[128,128]{1,0:T(8,128)S(1)}, f32[128,128]{1,0:T(8,128)S(1)}, u32[]{:S(2)}, u32[]{:S(2)}) collective-permute-start(f32[128,128]{1,0:T(8,128)S(1)} %pad_maximum_fusion.2), channel_id=1, source_target_pairs={{0,1},{1,0},{2,3},{3,2},{4,5},{5,4},{6,7},{7,6},{8,9},{9,8},{10,11... | collective-permute-start | bytes 196616 | tf_op jit(solution)/shard_map/ppermute | solution.py:189

commit v4 on v3

--- a/solution.py
+++ b/solution.py
@@ -80,10 +80,6 @@
     out_ref[own_ref.shape[0] :, :] = other_ref[:, first:]
 
 
-def block_of(block, rows, mask):
-    return pl.ds(pl.multiple_of((lax.axis_index("col") ^ mask) * block, block), rows)
-
-
 def with_ones(embed):
     return jnp.concatenate([embed, jnp.ones_like(embed)], axis=1)
 
@@ -93,85 +89,103 @@
     return factor * (summed[:, :width] - embed.astype(F32) * summed[:, width:])
 
 
-def slot_runs(ref, own, block):
-    return jnp.concatenate(
-        [ref[at : at + own, :] for at in range(0, ref.shape[0], block)], axis=0
-    )
-
-
-def fit_part(scale, chunk, own, columns_ref, left_ref, right_ref, slots_ref, picks_ref):
+def stacked(refs, rows):
+    return jnp.concatenate([ref[:rows, :] for ref in refs], axis=0)
+
+
+def slot_runs(ref, own):
+    half = ref.shape[0] // 2
+    return jnp.concatenate([ref[:own, :], ref[half : half + own, :]], axis=0)
+
+
+def fit_part(scale, own, columns_refs, left_ref, slots_ref, total):
     width = left_ref.shape[1] // 2
     left = left_ref[...]
-    slots_left = slot_runs(left_ref, own, chunk)
-    total = None
-    for at in range(0, columns_ref.shape[0], chunk):
-        span = slice(at, at + chunk)
-        right = extended(columns_ref[span, :width])(0, 3)
-        right_ref[span, :] = right
+    slots_left = slot_runs(left_ref, own)
+    place = 0
+    for ref in columns_refs:
+        block = ref.shape[0]
+        right = extended(ref[:, :width])(0, 3)
         kernel = jnp.exp2(nt_dot(left, right) * scale).astype(BF16)
-        part = nn_dot(kernel, columns_ref[span, width:])
+        part = nn_dot(kernel, ref[:, width:])
         total = part if total is None else total + part
-        slots_ref[:, span] = jnp.exp2(nt_dot(slots_left, right) * scale)
-    for mask in (0, 1):
-        right = right_ref[block_of(chunk, own, mask), :]
-        picks_ref[mask * own : (mask + 1) * own, :] = jnp.exp2(nt_dot(right, left) * scale)
+        slots_ref[:, place : place + block] = jnp.exp2(nt_dot(slots_left, right) * scale)
+        place += block
     return total
 
 
-def near_kernel(scale, chunk, own, near_ref, left_ref, fit_ref, slots_ref, picks_ref, right_ref):
+def pick_kernels(scale, own, first_ref, second_ref, left_ref, picks_ref):
     width = left_ref.shape[1] // 2
-    for part in range(left_ref.shape[0] // chunk):
-        embed = near_ref[block_of(chunk, chunk, 2 * part), :width]
-        left_ref[part * chunk : (part + 1) * chunk, :] = extended(embed)(3, 0)
-    fit_ref[...] = fit_part(
-        scale, chunk, own, near_ref, left_ref, right_ref, slots_ref, picks_ref
-    )
-
-
-def far_kernel(scale, chunk, own, far_ref, left_ref, near_fit_ref, fit_ref, slots_ref, picks_ref, right_ref):
-    fit_ref[...] = near_fit_ref[...] + fit_part(
-        scale, chunk, own, far_ref, left_ref, right_ref, slots_ref, picks_ref
-    )
-
-
-def column_part(factor, own, block, adjoint, embed, columns_ref, kernel_ref):
+    right = extended(stacked((first_ref, second_ref), own)[:, :width])(0, 3)
+    picks_ref[...] = jnp.exp2(nt_dot(right, left_ref[...]) * scale)
+
+
+def near_kernel(scale, own, own_ref, x_ref, y_ref, left_ref, fit_ref, slots_ref, picks_ref):
+    block, width = own_ref.shape[0], left_ref.shape[1] // 2
+    for part, ref in enumerate((own_ref, y_ref)):
+        left_ref[part * block : (part + 1) * block, :] = extended(ref[:, :width])(3, 0)
+    columns = (own_ref, x_ref, y_ref)
+    fit_ref[...] = fit_part(scale, own, columns, left_ref, slots_ref, None)
+    pick_kernels(scale, own, own_ref, x_ref, left_ref, picks_ref)
+
+
+def far_kernel(scale, own, *refs):
+    own_ref, x_ref, y_ref, left_ref, before_ref, fit_ref, slots_ref, picks_ref = refs
+    columns = (own_ref, x_ref, y_ref)
+    fit_ref[...] = fit_part(scale, own, columns, left_ref, slots_ref, before_ref[...])
+    pick_kernels(scale, own, own_ref, x_ref, left_ref, picks_ref)
+
+
+def across_kernel(scale, own, *refs):
+    columns, (left_ref, before_ref, fit_ref, slots_ref) = refs[:2], refs[2:]
+    fit_ref[...] = fit_part(scale, own, columns, left_ref, slots_ref, before_ref[...])
+
+
+def column_part(factor, own, adjoint, embed, refs, kernel_ref):
     width = embed.shape[1]
-    columns = jnp.concatenate(
-        [columns_ref[block_of(block, own, mask), :] for mask in (0, 1)], axis=0
-    )
+    columns = stacked(refs, own)
     weight = (nt_dot(columns[:, width:], adjoint) * kernel_ref[...]).astype(BF16)
     return gradient(factor, nn_dot(weight, with_ones(embed)), columns[:, :width])
 
 
-def adjoint_kernel(factor, own, far_ref, left_ref, fit_ref, kernel_ref, *refs):
-    targets_refs, (adjoint_ref, col_ref) = refs[:-2], refs[-2:]
+def adjoint_kernel(scale, factor, own, *refs):
+    columns, (left_ref, before_ref, own_ref, x_ref, picks_ref) = refs[:2], refs[2:7]
+    targets_refs, (slots_ref, adjoint_ref, col_ref) = refs[7:9], refs[9:]
     width = left_ref.shape[1] // 2
-    block = targets_refs[0].shape[0]
+    block = left_ref.shape[0] // 2
+    fit = fit_part(scale, own, columns, left_ref, slots_ref, before_ref[...])
     for part, targets_ref in enumerate(targets_refs):
         span = slice(part * block, (part + 1) * block)
         targets = targets_ref[...].astype(F32)
-        adjoint = jnp.where(targets == jnp.inf, 0.0, targets - fit_ref[span, :])
+        adjoint = jnp.where(targets == jnp.inf, 0.0, targets - fit[span])
         adjoint_ref[span, :] = adjoint.astype(BF16)
-    embed = left_ref[:, :width]
-    col_ref[...] = column_part(factor, own, block, adjoint_ref[...], embed, far_ref, kernel_ref)
-
-
-def last_kernel(factor, chunk, parts, own, *refs):
-    near_ref, far_ref, left_ref, adjoint_ref, near_slots_ref, picks_ref, far_slots_ref = refs[:7]
-    ids_refs, (col_ref, row_ref) = refs[7 : 7 + parts], refs[7 + parts :]
+    col_ref[...] = column_part(
+        factor, own, adjoint_ref[...], left_ref[:, :width], (own_ref, x_ref), picks_ref
+    )
+
+
+def last_kernel(factor, own, *refs):
+    columns_refs, slots_refs = refs[:10], refs[10:14]
+    left_ref, adjoint_ref, picks_ref = refs[14:17]
+    ids_refs, (col_ref, row_ref) = refs[17:19], refs[19:]
     width = left_ref.shape[1] // 2
-    embed = left_ref[:, :width]
-    col_ref[...] = column_part(factor, own, chunk, adjoint_ref[...], embed, near_ref, picks_ref)
-    slots_embed = slot_runs(left_ref, own, chunk)[:, :width]
-    slots_adjoint = slot_runs(adjoint_ref, own, chunk)
+    col_ref[...] = column_part(
+        factor, own, adjoint_ref[...], left_ref[:, :width], columns_refs[:2], picks_ref
+    )
+    slots_embed = slot_runs(left_ref, own)[:, :width]
+    slots_adjoint = slot_runs(adjoint_ref, own)
+    half = columns_refs[-1].shape[0]
+    places = [(ref, at) for ref in slots_refs for at in range(0, ref.shape[1], half)]
     summed = None
-    for columns_ref, kernel_ref in ((near_ref, near_slots_ref), (far_ref, far_slots_ref)):
-        for at in range(0, columns_ref.shape[0], chunk):
-            span = slice(at, at + chunk)
-            link = nt_dot(slots_adjoint, columns_ref[span, width:])
-            weight = (link * kernel_ref[:, span]).astype(BF16)
-            part = nn_dot(weight, with_ones(columns_ref[span, :width]))
-            summed = part if summed is None else summed + part
+    for ref in columns_refs:
+        link = nt_dot(slots_adjoint, ref[:, width:])
+        kernel = []
+        for _ in range(ref.shape[0] // half):
+            kernel_ref, at = places.pop(0)
+            kernel.append(kernel_ref[:, at : at + half])
+        weight = (link * jnp.concatenate(kernel, axis=1)).astype(BF16)
+        part = nn_dot(weight, with_ones(ref[:, :width]))
+        summed = part if summed is None else summed + part
     slot_rows = gradient(factor, summed, slots_embed)
     ids = jnp.concatenate([jnp.broadcast_to(ref[...], (own, own)) for ref in ids_refs], axis=1)
     wanted = lax.broadcasted_iota(jnp.int32, ids.shape, 0)
@@ -182,6 +196,11 @@
         row_ref[mask * own : (mask + 1) * own, :] = jnp.dot(
             chosen, slot_rows, precision=lax.Precision.HIGHEST, preferred_element_type=F32
         )
+
+
+def observed_kernel(first, own_ref, other_ref, out_ref):
+    out_ref[: own_ref.shape[0], :] = own_ref[...]
+    out_ref[own_ref.shape[0] :, :] = other_ref[:, first:]
 
 
 def swap(array, axis, mask):
@@ -232,66 +251,70 @@
             ),
         )(observed, other)
         halves, step = [observed], step // 2
-    turn = 2
-    while turn < cols_axis:
-        ids += [swap(array, "col", turn) for array in ids]
-        turn *= 2
+    ids.append(swap(ids[0], "col", 2))
     while step > 1:
         columns, halves = joined(columns, "row", step), [observed, swap(observed, "row", step)]
         step //= 2
         if step > 1:
             observed = jnp.concatenate(halves, axis=0)
-    near = lax.all_gather(columns, "col", axis=0, tiled=True)
-    near, halves, ids = lax.optimization_barrier((near, halves, ids))
+    block = columns.shape[0]
+    held, half = 2 * block, block // 2
+    x_block, y_block = swap(columns, "col", 1), swap(columns, "col", 2)
+    across = (swap(x_block[:half], "col", 2), swap(y_block[half:], "col", 1))
+    near = (columns, x_block, y_block)
+    far = tuple(swap(array, "row", 1) for array in near)
+
+    def call(body, outs, *inputs):
+        blocks = 3 if body in (near_kernel, far_kernel) else 1
+        return pl.pallas_call(
+            functools.partial(body, scale, own),
+            out_shape=outs,
+            in_specs=[VMEM] * len(inputs),
+            out_specs=[VMEM] * len(outs),
+            compiler_params=PARAMS,
+            cost_estimate=pl.CostEstimate(
+                flops=2 * held * blocks * block * (2 * width + epochs),
+                bytes_accessed=1 << 20,
+                transcendentals=held * blocks * block,
+            ),
+        )(*inputs)
+
+    fit_shape, picks_shape = shape((held, epochs), F32), shape((2 * own, held), F32)
+    slots = [shape((2 * own, count * block), F32) for count in (3, 1)]
+    left, fit, slots_near, picks_near = call(
+        near_kernel,
+        (shape((held, 2 * width), BF16), fit_shape, slots[0], picks_shape),
+        *near,
+    )
+    fit, halves, ids = lax.optimization_barrier((fit, halves, ids))
     observed = jnp.concatenate(halves, axis=0)
-    far = swap(near, "row", 1)
-    observed = [observed]
-    turn = 2
-    while turn < cols_axis:
-        observed += [swap(array, "col", turn) for array in observed]
-        turn *= 2
-    parts, half, chunk = len(ids), near.shape[0], columns.shape[0]
-    held = parts * chunk
-    cost = pl.CostEstimate(
-        flops=2 * held * half * (2 * width + epochs),
-        bytes_accessed=2 << 20,
-        transcendentals=held * half,
-    )
-    kernels = (shape((parts * own, half), F32), shape((2 * own, held), F32))
-    left, fit, *near_kernels = pl.pallas_call(
-        functools.partial(near_kernel, scale, chunk, own),
-        out_shape=(shape((held, 2 * width), BF16), shape((held, epochs), F32), *kernels),
-        in_specs=[VMEM],
-        out_specs=[VMEM] * 4,
-        scratch_shapes=[pltpu.VMEM((half, 2 * width), BF16)],
+    observed_y = swap(observed, "col", 2)
+    fit, slots_far, picks_far = call(
+        far_kernel, (fit_shape, slots[0], picks_shape), *far, left, fit
+    )
+    across, fit = lax.optimization_barrier((across, fit))
+    far_across = tuple(swap(array, "row", 1) for array in across)
+    fit, slots_across = call(across_kernel, (fit_shape, slots[1]), *across, left, fit)
+    slots_last, adjoint, col_far = pl.pallas_call(
+        functools.partial(adjoint_kernel, scale, factor, own),
+        out_shape=(slots[1], shape((held, epochs), BF16), shape((2 * own, width), F32)),
+        in_specs=[VMEM] * 9,
+        out_specs=[VMEM] * 3,
         compiler_params=PARAMS,
-        cost_estimate=cost,
-    )(near)
-    fit, *far_kernels = pl.pallas_call(
-        functools.partial(far_kernel, scale, chunk, own),
-        out_shape=(shape((held, epochs), F32), *kernels),
-        in_specs=[VMEM] * 3,
-        out_specs=[VMEM] * 3,
-        scratch_shapes=[pltpu.VMEM((half, 2 * width), BF16)],
-        compiler_params=PARAMS,
-        cost_estimate=cost,
-    )(far, left, fit)
-    adjoint, col_far = pl.pallas_call(
-        functools.partial(adjoint_kernel, factor, own),
-        out_shape=(shape((held, epochs), BF16), shape((2 * own, width), F32)),
-        in_specs=[VMEM] * (4 + parts),
+    )(*far_across, left, fit, *far[:2], picks_far, observed, observed_y)
+    col_other = swap(col_far, "row", 1)
+    col_near, row_part = pl.pallas_call(
+        functools.partial(last_kernel, factor, own),
+        out_shape=(shape((2 * own, width), F32),) * 2,
+        in_specs=[VMEM] * 19,
         out_specs=[VMEM] * 2,
         compiler_params=PARAMS,
-    )(far, left, fit, far_kernels[1], *observed)
-    col_other = swap(col_far, "row", 1)
-    col_near, row_part = pl.pallas_call(
-        functools.partial(last_kernel, factor, chunk, parts, own),
-        out_shape=(shape((2 * own, width), F32),) * 2,
-        in_specs=[VMEM] * (7 + parts),
-        out_specs=[VMEM] * 2,
-        compiler_params=PARAMS,
-        cost_estimate=cost,
-    )(near, far, left, adjoint, *near_kernels, far_kernels[0], *ids)
+        cost_estimate=pl.CostEstimate(flops=1 << 29, bytes_accessed=1 << 20, transcendentals=0),
+    )(
+        *(*near, *far, *across, *far_across),
+        *(slots_near, slots_far, slots_across, slots_last),
+        *(left, adjoint, picks_near, *ids),
+    )
     col_part = col_near + col_other
     other = swap(jnp.concatenate([col_part[own:], row_part[own:]], axis=0), "col", 1)
     return row_part[:own] + other[own:], col_part[:own] + other[:own]
@@ -424,7 +447,7 @@
     own, width = curve_embed.shape
     rows_axis, cols_axis = lax.axis_size("row"), lax.axis_size("col")
     gathered = own * rows_axis * cols_axis * (width + solution.shape[1]) * 2
-    if gathered <= GATHER_LIMIT and power_of_two(rows_axis) and power_of_two(cols_axis):
+    if gathered <= GATHER_LIMIT and power_of_two(rows_axis) and cols_axis == 4:
         return gathered_plan(curve_embed, solution, *rest)
     return tiled_plan(curve_embed, solution, *rest)
 

time: 41.8 us -> 40.7 us (0.974)
  blocking collectives: 12.2 us -> 0 us
  waiting for transfers between devices: 9.79 us -> 15.1 us
  starting transfers between devices: 10.9 us -> 15.2 us
  Pallas kernels: 7.21 us -> 8.6 us
    all_gather x1 -> x0, blocking collectives: 12.2 us -> none  [gathered_plan(): near = lax.all_gather(columns, 'col', axis=0, tiled=True)]
    ppermute x8 -> x16, waiting for transfers between devices: 9.79 us -> 15.1 us  [swap(): return lax.ppermute(array, axis, pairs)]
    ppermute x8 -> x16, starting transfers between devices: 10.9 us -> 15.2 us  [swap(): return lax.ppermute(array, axis, pairs)]
    pallas_call x4 -> x5, Pallas kernels: 5.22 us -> 6.62 us  [the longest x3 4.07 us: call(): pl.pallas_call(functools.partial(body, scale, own), out_shape=outs, in_sp...]
  transfers between devices with their start and end apart: 8 -> 16, of which waited for: 4 -> 7; matrix products, arithmetic and copies ran while one was open for 0% -> 0% of each run, Pallas kernels for 12% -> 13%
where the time goes in v4:
time: 40.7 us; the launch traced here: 40.5 us
  starting transfers between devices  15.2 us (37%)
  waiting for transfers between devices  15.1 us (37%)
  Pallas kernels  8.6 us (21%)
  between operations  0.83 us (2%)
  other arithmetic  0.68 us (2%)
    ppermute x16, starting transfers between devices, swap(): return lax.ppermute(array, axis, pairs)  15.2 us
    ppermute x16, waiting for transfers between devices, swap(): return lax.ppermute(array, axis, pairs)  15.1 us
    pallas_call x3, Pallas kernels, call(): pl.pallas_call(functools.partial(body, scale, own), out_shape=outs, in_sp...  4.07 us
    pallas_call x1, Pallas kernels, gathered_plan(): pl.pallas_call(functools.partial(head_kernel, width), out_shape=(shape((o...  1.98 us
    pallas_call x1, Pallas kernels, gathered_plan(): pl.pallas_call(functools.partial(last_kernel, factor, own), out_shape=(sh...  1.29 us
    pallas_call x1, Pallas kernels, gathered_plan(): pl.pallas_call(functools.partial(adjoint_kernel, scale, factor, own), out...  1.26 us
  transfers between devices with their start and end apart: 16, of which 7 were waited for; matrix products, arithmetic and copies ran while one was open for 0% of the time, Pallas kernels for 13%

profile of v4, /device:TPU:0, one launch (start us, length us, event | category | flops | bytes accessed | tf_op | source)
XLA Modules:
  0.0 40.5 jit_solution(3537157261224025527)
XLA Ops:
  0.6 2.0 %shard_map.77 = (bf16[64,640]{1,0:T(8,128)(2,1)}, bf16[64,384]{1,0:T(8,128)(2,1)}, bf16[64,256]{1,0:T(8,128)(2,1)}) custom-call(bf16[64,128]{1,0:T(8,128)(2,1)} %refs_0_.1, f32[64,256]{1,0:T(8,128)} %refs_1_.1, bf16[64,256]{1,0:T(8,128)(2,1)} %refs_2_.1, s32[1,64]{1,0:T(1,128)} %bitcast.4, f32[256,256]{1,0:T(8,128)} %refs_4_.1), custom_call_target="tpu_custom_call" | custom-call | tf_op jit(solution)/shard_map/pallas_call | solution.py:224
  2.6 0.0 copy-start.2
  2.6 4.1 %collective-permute-start = (bf16[64,640]{1,0:T(8,128)(2,1)}, bf16[64,640]{1,0:T(8,128)(2,1)S(1)}, u32[]{:S(2)}, u32[]{:S(2)}) collective-permute-start(bf16[64,640]{1,0:T(8,128)(2,1)} %get-tuple-element.28), channel_id=1, source_target_pairs={{0,16},{4,20},{8,24},{12,28},{16,0},{20,4},{24,8},{28,12},{1,17},{... | collective-permute-start | bytes 245768 | tf_op jit(solution)/shard_map/ppermute | solution.py:208
  6.7 4.4 %collective-permute-done.other_ref = bf16[64,640]{1,0:T(8,128)(2,1)S(1)} collective-permute-done((bf16[64,640]{1,0:T(8,128)(2,1)}, bf16[64,640]{1,0:T(8,128)(2,1)S(1)}, u32[]{:S(2)}, u32[]{:S(2)}) %collective-permute-start) | collective-permute-done | bytes 81952 | tf_op jit(solution)/shard_map/ppermute | solution.py:208
  11.1 0.0 copy-done.2
  11.2 0.0 copy-start.1
  11.2 0.9 %collective-permute-start.1 = (bf16[128,384]{1,0:T(8,128)(2,1)S(1)}, bf16[128,384]{1,0:T(8,128)(2,1)S(1)}, u32[]{:S(2)}, u32[]{:S(2)}) collective-permute-start(bf16[128,384]{1,0:T(8,128)(2,1)S(1)} %pad_maximum_fusion.1), channel_id=1, source_target_pairs={{0,8},{4,12},{8,0},{12,4},{16,24},{20,28},{24,16},{28,20},{1,9},{5... | collective-permute-start | bytes 294920 | tf_op jit(solution)/shard_map/ppermute | solution.py:208
  12.1 3.8 %collective-permute-done.1 = bf16[128,384]{1,0:T(8,128)(2,1)S(1)} collective-permute-done((bf16[128,384]{1,0:T(8,128)(2,1)S(1)}, bf16[128,384]{1,0:T(8,128)(2,1)S(1)}, u32[]{:S(2)}, u32[]{:S(2)}) %collective-permute-start.1) | collective-permute-done | bytes 98336 | tf_op jit(solution)/shard_map/ppermute | solution.py:208
  15.9 1.7 %collective-permute-start.2 = (bf16[256,384]{1,0:T(8,128)(2,1)S(1)}, bf16[256,384]{1,0:T(8,128)(2,1)S(1)}, u32[]{:S(2)}, u32[]{:S(2)}) collective-permute-start(bf16[256,384]{1,0:T(8,128)(2,1)S(1)} %pad_maximum_fusion.own_ref.refs_0_), channel_id=1, source_target_pairs={{0,1},{1,0},{2,3},{3,2},{4,5},{5,4},{6,7},{7,6},{8,9},{9,8},{10,11... | collective-permute-start | bytes 589832 | tf_op jit(solution)/shard_map/ppermute | solution.py:208
  17.6 1.5 %collective-permute-start.3 = (bf16[256,384]{1,0:T(8,128)(2,1)S(1)}, bf16[256,384]{1,0:T(8,128)(2,1)S(1)}, u32[]{:S(2)}, u32[]{:S(2)}) collective-permute-start(bf16[256,384]{1,0:T(8,128)(2,1)S(1)} %pad_maximum_fusion.own_ref.refs_0_), channel_id=1, source_target_pairs={{0,2},{1,3},{2,0},{3,1},{4,6},{5,7},{6,4},{7,5},{8,10},{9,11},{10,... | collective-permute-start | bytes 589832 | tf_op jit(solution)/shard_map/ppermute | solution.py:208
  19.2 0.0 copy-done.1
  19.2 0.0 copy-start
  19.2 0.7 %collective-permute-start.9 = (bf16[128,256]{1,0:T(8,128)(2,1)S(1)}, bf16[128,256]{1,0:T(8,128)(2,1)S(1)}, u32[]{:S(2)}, u32[]{:S(2)}) collective-permute-start(bf16[128,256]{1,0:T(8,128)(2,1)S(1)} %shard_map.79), channel_id=1, source_target_pairs={{0,8},{4,12},{8,0},{12,4},{16,24},{20,28},{24,16},{28,20},{1,9},{5... | collective-permute-start | bytes 196616 | tf_op jit(solution)/shard_map/ppermute | solution.py:208
  19.9 0.0 copy-done
  19.9 0.5 %collective-permute-start.10 = (s32[1,64]{1,0:T(1,128)S(1)}, s32[1,64]{1,0:T(1,128)S(1)}, u32[]{:S(2)}, u32[]{:S(2)}) collective-permute-start(s32[1,64]{1,0:T(1,128)S(1)} %bitcast.2), channel_id=1, source_target_pairs={{0,2},{1,3},{2,0},{3,1},{4,6},{5,7},{6,4},{7,5},{8,10},{9,11},{10,... | collective-permute-start | bytes 776 | tf_op jit(solution)/shard_map/ppermute | solution.py:208
  20.4 0.0 collective-permute-start.4
  20.4 1.2 %collective-permute-done.2.x_ref.refs_1_ = bf16[256,384]{1,0:T(8,128)(2,1)S(1)} collective-permute-done((bf16[256,384]{1,0:T(8,128)(2,1)S(1)}, bf16[256,384]{1,0:T(8,128)(2,1)S(1)}, u32[]{:S(2)}, u32[]{:S(2)}) %collective-permute-start.2) | collective-permute-done | bytes 196640 | tf_op jit(solution)/shard_map/ppermute | solution.py:208
  21.6 1.8 %collective-permute-start.7 = (bf16[128,384]{1,0:T(8,128)(2,1)S(1)}, bf16[128,384]{1,0:T(8,128)(2,1)S(1)}, u32[]{:S(2)}, u32[]{:S(2)}) collective-permute-start(bf16[128,384]{1,0:T(8,128)(2,1)S(1)} %slice.37), channel_id=1, source_target_pairs={{0,2},{1,3},{2,0},{3,1},{4,6},{5,7},{6,4},{7,5},{8,10},{9,11},{10,... | collective-permute-start | bytes 294920 | tf_op jit(solution)/shard_map/ppermute | solution.py:208
  23.4 0.0 collective-permute-done.3.y_ref.refs_2_
  23.4 1.6 %collective-permute-start.8 = (bf16[128,384]{1,0:T(8,128)(2,1)S(1)}, bf16[128,384]{1,0:T(8,128)(2,1)S(1)}, u32[]{:S(2)}, u32[]{:S(2)}) collective-permute-start(bf16[128,384]{1,0:T(8,128)(2,1)S(1)} %slice.38), channel_id=1, source_target_pairs={{0,1},{1,0},{2,3},{3,2},{4,5},{5,4},{6,7},{7,6},{8,9},{9,8},{10,11... | collective-permute-start | bytes 294920 | tf_op jit(solution)/shard_map/ppermute | solution.py:208
  25.0 1.4 %shard_map.78 = (bf16[512,256]{1,0:T(8,128)(2,1)S(1)}, f32[512,256]{1,0:T(8,128)S(1)}, f32[128,768]{1,0:T(8,128)S(1)}, f32[128,512]{1,0:T(8,128)S(1)}) custom-call(bf16[256,384]{1,0:T(8,128)(2,1)S(1)} %pad_maximum_fusion.own_ref.refs_0_, bf16[256,384]{1,0:T(8,128)(2,1)S(1)} %collective-permute-done.2.x_ref.refs_1_, ...), custom_call_target="tpu_custom_call" | custom-call | flops 402653184 | bytes 1048576 | tf_op jit(solution)/shard_map/pallas_call | solution.py:269
  26.4 0.0 collective-permute-done.10.refs_18_
  26.4 0.0 collective-permute-done.9
  26.4 0.1 collective-permute-start.5
  26.5 0.5 %collective-permute-start.6 = (bf16[256,384]{1,0:T(8,128)(2,1)S(1)}, bf16[256,384]{1,0:T(8,128)(2,1)S(1)}, u32[]{:S(2)}, u32[]{:S(2)}) collective-permute-start(bf16[256,384]{1,0:T(8,128)(2,1)S(1)} %collective-permute-done.3.y_ref.refs_2_), channel_id=1, source_target_pairs={{0,4},{4,0},{8,12},{12,8},{16,20},{20,16},{24,28},{28,24},{1,5},{5... | collective-permute-start | bytes 589832 | tf_op jit(solution)/shard_map/ppermute | solution.py:208
  27.0 0.0 collective-permute-done.4.refs_0_.refs_4_.refs_3_
  27.0 0.6 %collective-permute-start.13 = (bf16[256,256]{1,0:T(8,128)(2,1)S(1)}, bf16[256,256]{1,0:T(8,128)(2,1)S(1)}, u32[]{:S(2)}, u32[]{:S(2)}) collective-permute-start(bf16[256,256]{1,0:T(8,128)(2,1)S(1)} %constant_dynamic-update-slice_fusion.refs_7_), channel_id=1, source_target_pairs={{0,2},{1,3},{2,0},{3,1},{4,6},{5,7},{6,4},{7,5},{8,10},{9,11},{10,... | collective-permute-start | bytes 393224 | tf_op jit(solution)/shard_map/ppermute | solution.py:208
  27.6 0.3 collective-permute-done.5.refs_1_.refs_5_.refs_4_
  27.9 0.3 collective-permute-done.6.refs_2_.refs_5_
  28.2 1.7 %shard_map.80 = (f32[512,256]{1,0:T(8,128)S(1)}, f32[128,768]{1,0:T(8,128)S(1)}, f32[128,512]{1,0:T(8,128)S(1)}) custom-call(bf16[256,384]{1,0:T(8,128)(2,1)S(1)} %collective-permute-done.4.refs_0_.refs_4_.refs_3_, bf16[256,384]{1,0:T(8,128)(2,1)S(1)} %collective-permute-done.5.refs_1_.refs_5_.refs_4_, ...), custom_call_target="tpu_custom_call" | custom-call | flops 402653184 | bytes 1048576 | tf_op jit(solution)/shard_map/pallas_call | solution.py:269
  29.9 0.0 collective-permute-done.7.refs_0_.refs_6_
  29.9 0.0 collective-permute-done.8.refs_1_.refs_7_
  29.9 0.3 collective-permute-start.11
  30.2 0.3 collective-permute-start.12
  30.5 1.0 %shard_map.81 = (f32[512,256]{1,0:T(8,128)S(1)}, f32[128,256]{1,0:T(8,128)S(1)}) custom-call(bf16[128,384]{1,0:T(8,128)(2,1)S(1)} %collective-permute-done.7.refs_0_.refs_6_, bf16[128,384]{1,0:T(8,128)(2,1)S(1)} %collective-permute-done.8.refs_1_.refs_7_, bf16[512,256]{1,0:T(8,128)(2,1)S(1)} %get-tuple-element.29.refs_3_.refs_2_.refs_14_, ...), custom_call_target="tpu_custom_call" | custom-call | flops 134217728 | bytes 1048576 | tf_op jit(solution)/shard_map/pallas_call | solution.py:269
  31.5 1.1 %collective-permute-done.13.refs_8_ = bf16[256,256]{1,0:T(8,128)(2,1)S(1)} collective-permute-done((bf16[256,256]{1,0:T(8,128)(2,1)S(1)}, bf16[256,256]{1,0:T(8,128)(2,1)S(1)}, u32[]{:S(2)}, u32[]{:S(2)}) %collective-permute-start.13) | collective-permute-done | bytes 131104 | tf_op jit(solution)/shard_map/ppermute | solution.py:208
  32.6 0.0 collective-permute-done.11.refs_0_.refs_8_
  32.6 0.0 collective-permute-done.12.refs_1_.refs_9_
  32.6 1.3 %shard_map.82 = (f32[128,256]{1,0:T(8,128)S(1)}, bf16[512,256]{1,0:T(8,128)(2,1)S(1)}, f32[128,128]{1,0:T(8,128)S(1)}) custom-call(bf16[128,384]{1,0:T(8,128)(2,1)S(1)} %collective-permute-done.11.refs_0_.refs_8_, bf16[128,384]{1,0:T(8,128)(2,1)S(1)} %collective-permute-done.12.refs_1_.refs_9_, ...), custom_call_target="tpu_custom_call" | custom-call | tf_op jit(solution)/shard_map/pallas_call | solution.py:298
  33.8 0.1 collective-permute-start.14
  33.9 1.3 %shard_map.83 = (f32[128,128]{1,0:T(8,128)S(1)}, f32[128,128]{1,0:T(8,128)S(1)}) custom-call(bf16[256,384]{1,0:T(8,128)(2,1)S(1)} %pad_maximum_fusion.own_ref.refs_0_, bf16[256,384]{1,0:T(8,128)(2,1)S(1)} %collective-permute-done.2.x_ref.refs_1_, bf16[256,384]{1,0:T(8,128)(2,1)S(1)} %collective-permute-done.3.y_ref.refs_2_, ...), custom_call_target="tpu_custom_call" | custom-call | flops 536870912 | bytes 1048576 | tf_op jit(solution)/shard_map/pallas_call | solution.py:306
  35.2 0.0 collective-permute-done.14
  35.3 0.6 %collective-permute-start.15 = (f32[128,128]{1,0:T(8,128)S(1)}, f32[128,128]{1,0:T(8,128)S(1)}, u32[]{:S(2)}, u32[]{:S(2)}) collective-permute-start(f32[128,128]{1,0:T(8,128)S(1)} %pad_maximum_fusion.2), channel_id=1, source_target_pairs={{0,1},{1,0},{2,3},{3,2},{4,5},{5,4},{6,7},{7,6},{8,9},{9,8},{10,11... | collective-permute-start | bytes 196616 | tf_op jit(solution)/shard_map/ppermute | solution.py:208
  35.9 3.9 %collective-permute-done.15 = f32[128,128]{1,0:T(8,128)S(1)} collective-permute-done((f32[128,128]{1,0:T(8,128)S(1)}, f32[128,128]{1,0:T(8,128)S(1)}, u32[]{:S(2)}, u32[]{:S(2)}) %collective-permute-start.15) | collective-permute-done | bytes 65568 | tf_op jit(solution)/shard_map/ppermute | solution.py:208
  39.8 0.6 %slice_add_fusion = (f32[64,128]{1,0:T(8,128)}, f32[64,128]{1,0:T(8,128)}) fusion(f32[128,128]{1,0:T(8,128)S(1)} %collective-permute-done.15, f32[128,128]{1,0:T(8,128)S(1)} %add.9, f32[128,128]{1,0:T(8,128)S(1)} %get-tuple-element.49), kind=kLoop, calls=%fused_computation.3 | loop fusion | flops 16384 | bytes 196608 | tf_op jit(solution)/shard_map/add | solution.py:320
  (12 shorter events, 0.1 us)
Async XLA Ops:
  2.6 8.5 %copy-start.2 = (bf16[64,384]{1,0:T(8,128)(2,1)S(1)}, bf16[64,384]{1,0:T(8,128)(2,1)}, u32[]{:S(2)}) copy-start(bf16[64,384]{1,0:T(8,128)(2,1)} %get-tuple-element.27) | copy-start | bytes 147460
  2.6 8.5 %collective-permute-start = (bf16[64,640]{1,0:T(8,128)(2,1)}, bf16[64,640]{1,0:T(8,128)(2,1)S(1)}, u32[]{:S(2)}, u32[]{:S(2)}) collective-permute-start(bf16[64,640]{1,0:T(8,128)(2,1)} %get-tuple-element.28), channel_id=1, source_target_pairs={{0,16},{4,20},{8,24},{12,28},{16,0},{20,4},{24,8},{28,12},{1,17},{... | collective-permute-start | bytes 245768 | tf_op jit(solution)/shard_map/ppermute | solution.py:208
  11.2 8.0 %copy-start.1 = (bf16[64,256]{1,0:T(8,128)(2,1)S(1)}, bf16[64,256]{1,0:T(8,128)(2,1)}, u32[]{:S(2)}) copy-start(bf16[64,256]{1,0:T(8,128)(2,1)} %get-tuple-element.31.own_ref) | copy-start | bytes 98308
  11.2 4.7 %collective-permute-start.1 = (bf16[128,384]{1,0:T(8,128)(2,1)S(1)}, bf16[128,384]{1,0:T(8,128)(2,1)S(1)}, u32[]{:S(2)}, u32[]{:S(2)}) collective-permute-start(bf16[128,384]{1,0:T(8,128)(2,1)S(1)} %pad_maximum_fusion.1), channel_id=1, source_target_pairs={{0,8},{4,12},{8,0},{12,4},{16,24},{20,28},{24,16},{28,20},{1,9},{5... | collective-permute-start | bytes 294920 | tf_op jit(solution)/shard_map/ppermute | solution.py:208
  15.9 5.7 %collective-permute-start.2 = (bf16[256,384]{1,0:T(8,128)(2,1)S(1)}, bf16[256,384]{1,0:T(8,128)(2,1)S(1)}, u32[]{:S(2)}, u32[]{:S(2)}) collective-permute-start(bf16[256,384]{1,0:T(8,128)(2,1)S(1)} %pad_maximum_fusion.own_ref.refs_0_), channel_id=1, source_target_pairs={{0,1},{1,0},{2,3},{3,2},{4,5},{5,4},{6,7},{7,6},{8,9},{9,8},{10,11... | collective-permute-start | bytes 589832 | tf_op jit(solution)/shard_map/ppermute | solution.py:208
  17.6 5.8 %collective-permute-start.3 = (bf16[256,384]{1,0:T(8,128)(2,1)S(1)}, bf16[256,384]{1,0:T(8,128)(2,1)S(1)}, u32[]{:S(2)}, u32[]{:S(2)}) collective-permute-start(bf16[256,384]{1,0:T(8,128)(2,1)S(1)} %pad_maximum_fusion.own_ref.refs_0_), channel_id=1, source_target_pairs={{0,2},{1,3},{2,0},{3,1},{4,6},{5,7},{6,4},{7,5},{8,10},{9,11},{10,... | collective-permute-start | bytes 589832 | tf_op jit(solution)/shard_map/ppermute | solution.py:208
  19.2 0.7 %copy-start = (s32[64]{0:T(128)S(1)}, s32[64]{0:T(128)}, u32[]{:S(2)}) copy-start(s32[64]{0:T(128)} %param.10) | copy-start | bytes 772
  19.2 7.2 %collective-permute-start.9 = (bf16[128,256]{1,0:T(8,128)(2,1)S(1)}, bf16[128,256]{1,0:T(8,128)(2,1)S(1)}, u32[]{:S(2)}, u32[]{:S(2)}) collective-permute-start(bf16[128,256]{1,0:T(8,128)(2,1)S(1)} %shard_map.79), channel_id=1, source_target_pairs={{0,8},{4,12},{8,0},{12,4},{16,24},{20,28},{24,16},{28,20},{1,9},{5... | collective-permute-start | bytes 196616 | tf_op jit(solution)/shard_map/ppermute | solution.py:208
  19.9 6.5 %collective-permute-start.10 = (s32[1,64]{1,0:T(1,128)S(1)}, s32[1,64]{1,0:T(1,128)S(1)}, u32[]{:S(2)}, u32[]{:S(2)}) collective-permute-start(s32[1,64]{1,0:T(1,128)S(1)} %bitcast.2), channel_id=1, source_target_pairs={{0,2},{1,3},{2,0},{3,1},{4,6},{5,7},{6,4},{7,5},{8,10},{9,11},{10,... | collective-permute-start | bytes 776 | tf_op jit(solution)/shard_map/ppermute | solution.py:208
  20.4 6.6 %collective-permute-start.4 = (bf16[256,384]{1,0:T(8,128)(2,1)S(1)}, bf16[256,384]{1,0:T(8,128)(2,1)S(1)}, u32[]{:S(2)}, u32[]{:S(2)}) collective-permute-start(bf16[256,384]{1,0:T(8,128)(2,1)S(1)} %pad_maximum_fusion.own_ref.refs_0_), channel_id=1, source_target_pairs={{0,4},{4,0},{8,12},{12,8},{16,20},{20,16},{24,28},{28,24},{1,5},{5... | collective-permute-start | bytes 589832 | tf_op jit(solution)/shard_map/ppermute | solution.py:208
  21.6 8.3 %collective-permute-start.7 = (bf16[128,384]{1,0:T(8,128)(2,1)S(1)}, bf16[128,384]{1,0:T(8,128)(2,1)S(1)}, u32[]{:S(2)}, u32[]{:S(2)}) collective-permute-start(bf16[128,384]{1,0:T(8,128)(2,1)S(1)} %slice.37), channel_id=1, source_target_pairs={{0,2},{1,3},{2,0},{3,1},{4,6},{5,7},{6,4},{7,5},{8,10},{9,11},{10,... | collective-permute-start | bytes 294920 | tf_op jit(solution)/shard_map/ppermute | solution.py:208
  23.4 6.5 %collective-permute-start.8 = (bf16[128,384]{1,0:T(8,128)(2,1)S(1)}, bf16[128,384]{1,0:T(8,128)(2,1)S(1)}, u32[]{:S(2)}, u32[]{:S(2)}) collective-permute-start(bf16[128,384]{1,0:T(8,128)(2,1)S(1)} %slice.38), channel_id=1, source_target_pairs={{0,1},{1,0},{2,3},{3,2},{4,5},{5,4},{6,7},{7,6},{8,9},{9,8},{10,11... | collective-permute-start | bytes 294920 | tf_op jit(solution)/shard_map/ppermute | solution.py:208
  26.4 1.5 %collective-permute-start.5 = (bf16[256,384]{1,0:T(8,128)(2,1)S(1)}, bf16[256,384]{1,0:T(8,128)(2,1)S(1)}, u32[]{:S(2)}, u32[]{:S(2)}) collective-permute-start(bf16[256,384]{1,0:T(8,128)(2,1)S(1)} %collective-permute-done.2.x_ref.refs_1_), channel_id=1, source_target_pairs={{0,4},{4,0},{8,12},{12,8},{16,20},{20,16},{24,28},{28,24},{1,5},{5... | collective-permute-start | bytes 589832 | tf_op jit(solution)/shard_map/ppermute | solution.py:208
  26.5 1.7 %collective-permute-start.6 = (bf16[256,384]{1,0:T(8,128)(2,1)S(1)}, bf16[256,384]{1,0:T(8,128)(2,1)S(1)}, u32[]{:S(2)}, u32[]{:S(2)}) collective-permute-start(bf16[256,384]{1,0:T(8,128)(2,1)S(1)} %collective-permute-done.3.y_ref.refs_2_), channel_id=1, source_target_pairs={{0,4},{4,0},{8,12},{12,8},{16,20},{20,16},{24,28},{28,24},{1,5},{5... | collective-permute-start | bytes 589832 | tf_op jit(solution)/shard_map/ppermute | solution.py:208
  27.0 5.5 %collective-permute-start.13 = (bf16[256,256]{1,0:T(8,128)(2,1)S(1)}, bf16[256,256]{1,0:T(8,128)(2,1)S(1)}, u32[]{:S(2)}, u32[]{:S(2)}) collective-permute-start(bf16[256,256]{1,0:T(8,128)(2,1)S(1)} %constant_dynamic-update-slice_fusion.refs_7_), channel_id=1, source_target_pairs={{0,2},{1,3},{2,0},{3,1},{4,6},{5,7},{6,4},{7,5},{8,10},{9,11},{10,... | collective-permute-start | bytes 393224 | tf_op jit(solution)/shard_map/ppermute | solution.py:208
  29.9 2.6 %collective-permute-start.11 = (bf16[128,384]{1,0:T(8,128)(2,1)S(1)}, bf16[128,384]{1,0:T(8,128)(2,1)S(1)}, u32[]{:S(2)}, u32[]{:S(2)}) collective-permute-start(bf16[128,384]{1,0:T(8,128)(2,1)S(1)} %collective-permute-done.7.refs_0_.refs_6_), channel_id=1, source_target_pairs={{0,4},{4,0},{8,12},{12,8},{16,20},{20,16},{24,28},{28,24},{1,5},{5... | collective-permute-start | bytes 294920 | tf_op jit(solution)/shard_map/ppermute | solution.py:208
  30.2 2.4 %collective-permute-start.12 = (bf16[128,384]{1,0:T(8,128)(2,1)S(1)}, bf16[128,384]{1,0:T(8,128)(2,1)S(1)}, u32[]{:S(2)}, u32[]{:S(2)}) collective-permute-start(bf16[128,384]{1,0:T(8,128)(2,1)S(1)} %collective-permute-done.8.refs_1_.refs_7_), channel_id=1, source_target_pairs={{0,4},{4,0},{8,12},{12,8},{16,20},{20,16},{24,28},{28,24},{1,5},{5... | collective-permute-start | bytes 294920 | tf_op jit(solution)/shard_map/ppermute | solution.py:208
  33.8 1.4 %collective-permute-start.14 = (f32[128,128]{1,0:T(8,128)S(1)}, f32[128,128]{1,0:T(8,128)S(1)}, u32[]{:S(2)}, u32[]{:S(2)}) collective-permute-start(f32[128,128]{1,0:T(8,128)S(1)} %get-tuple-element.51), channel_id=1, source_target_pairs={{0,4},{4,0},{8,12},{12,8},{16,20},{20,16},{24,28},{28,24},{1,5},{5... | collective-permute-start | bytes 196616 | tf_op jit(solution)/shard_map/ppermute | solution.py:208
  35.3 4.5 %collective-permute-start.15 = (f32[128,128]{1,0:T(8,128)S(1)}, f32[128,128]{1,0:T(8,128)S(1)}, u32[]{:S(2)}, u32[]{:S(2)}) collective-permute-start(f32[128,128]{1,0:T(8,128)S(1)} %pad_maximum_fusion.2), channel_id=1, source_target_pairs={{0,1},{1,0},{2,3},{3,2},{4,5},{5,4},{6,7},{7,6},{8,9},{9,8},{10,11... | collective-permute-start | bytes 196616 | tf_op jit(solution)/shard_map/ppermute | solution.py:208

commit v5 on v4

--- a/solution.py
+++ b/solution.py
@@ -98,19 +98,25 @@
     return jnp.concatenate([ref[:own, :], ref[half : half + own, :]], axis=0)
 
 
-def fit_part(scale, own, columns_refs, left_ref, slots_ref, total):
+def joint(refs):
+    return jnp.concatenate([ref[...] for ref in refs], axis=0)
+
+
+def fit_part(scale, own, groups, left_ref, slots_ref, total):
     width = left_ref.shape[1] // 2
     left = left_ref[...]
     slots_left = slot_runs(left_ref, own)
     place = 0
-    for ref in columns_refs:
-        block = ref.shape[0]
-        right = extended(ref[:, :width])(0, 3)
+    for group in groups:
+        columns = joint(group)
+        right = extended(columns[:, :width])(0, 3)
         kernel = jnp.exp2(nt_dot(left, right) * scale).astype(BF16)
-        part = nn_dot(kernel, ref[:, width:])
+        part = nn_dot(kernel, columns[:, width:])
         total = part if total is None else total + part
-        slots_ref[:, place : place + block] = jnp.exp2(nt_dot(slots_left, right) * scale)
-        place += block
+        slots_ref[:, place : place + columns.shape[0]] = jnp.exp2(
+            nt_dot(slots_left, right) * scale
+        )
+        place += columns.shape[0]
     return total
 
 
@@ -120,25 +126,20 @@
     picks_ref[...] = jnp.exp2(nt_dot(right, left_ref[...]) * scale)
 
 
-def near_kernel(scale, own, own_ref, x_ref, y_ref, left_ref, fit_ref, slots_ref, picks_ref):
-    block, width = own_ref.shape[0], left_ref.shape[1] // 2
-    for part, ref in enumerate((own_ref, y_ref)):
-        left_ref[part * block : (part + 1) * block, :] = extended(ref[:, :width])(3, 0)
-    columns = (own_ref, x_ref, y_ref)
-    fit_ref[...] = fit_part(scale, own, columns, left_ref, slots_ref, None)
-    pick_kernels(scale, own, own_ref, x_ref, left_ref, picks_ref)
-
-
-def far_kernel(scale, own, *refs):
-    own_ref, x_ref, y_ref, left_ref, before_ref, fit_ref, slots_ref, picks_ref = refs
-    columns = (own_ref, x_ref, y_ref)
-    fit_ref[...] = fit_part(scale, own, columns, left_ref, slots_ref, before_ref[...])
-    pick_kernels(scale, own, own_ref, x_ref, left_ref, picks_ref)
+def main_kernel(scale, own, *refs):
+    near, far = [refs[:2], refs[2:4], refs[4:6]], [(ref,) for ref in refs[6:9]]
+    left_ref, fit_ref, slots_ref, near_picks_ref, far_picks_ref = refs[9:]
+    block, width = left_ref.shape[0] // 2, left_ref.shape[1] // 2
+    for part, group in enumerate((near[0], near[2])):
+        left_ref[part * block : (part + 1) * block, :] = extended(joint(group)[:, :width])(3, 0)
+    fit_ref[...] = fit_part(scale, own, near + far, left_ref, slots_ref, None)
+    pick_kernels(scale, own, refs[0], refs[2], left_ref, near_picks_ref)
+    pick_kernels(scale, own, refs[6], refs[7], left_ref, far_picks_ref)
 
 
 def across_kernel(scale, own, *refs):
-    columns, (left_ref, before_ref, fit_ref, slots_ref) = refs[:2], refs[2:]
-    fit_ref[...] = fit_part(scale, own, columns, left_ref, slots_ref, before_ref[...])
+    group, (left_ref, before_ref, fit_ref, slots_ref) = refs[:2], refs[2:]
+    fit_ref[...] = fit_part(scale, own, (group,), left_ref, slots_ref, before_ref[...])
 
 
 def column_part(factor, own, adjoint, embed, refs, kernel_ref):
@@ -149,15 +150,16 @@
 
 
 def adjoint_kernel(scale, factor, own, *refs):
-    columns, (left_ref, before_ref, own_ref, x_ref, picks_ref) = refs[:2], refs[2:7]
-    targets_refs, (slots_ref, adjoint_ref, col_ref) = refs[7:9], refs[9:]
+    group, (left_ref, before_ref, own_ref, x_ref, picks_ref) = refs[:2], refs[2:7]
+    first_ref, first_y_ref, second_ref, slots_ref, adjoint_ref, col_ref = refs[7:]
     width = left_ref.shape[1] // 2
-    block = left_ref.shape[0] // 2
-    fit = fit_part(scale, own, columns, left_ref, slots_ref, before_ref[...])
-    for part, targets_ref in enumerate(targets_refs):
-        span = slice(part * block, (part + 1) * block)
-        targets = targets_ref[...].astype(F32)
-        adjoint = jnp.where(targets == jnp.inf, 0.0, targets - fit[span])
+    half = first_ref.shape[0]
+    fit = fit_part(scale, own, (group,), left_ref, slots_ref, before_ref[...])
+    targets = (first_ref[...], second_ref[:half, :], first_y_ref[...], second_ref[half:, :])
+    for part, values in enumerate(targets):
+        span = slice(part * half, (part + 1) * half)
+        values = values.astype(F32)
+        adjoint = jnp.where(values == jnp.inf, 0.0, values - fit[span])
         adjoint_ref[span, :] = adjoint.astype(BF16)
     col_ref[...] = column_part(
         factor, own, adjoint_ref[...], left_ref[:, :width], (own_ref, x_ref), picks_ref
@@ -165,26 +167,24 @@
 
 
 def last_kernel(factor, own, *refs):
-    columns_refs, slots_refs = refs[:10], refs[10:14]
-    left_ref, adjoint_ref, picks_ref = refs[14:17]
-    ids_refs, (col_ref, row_ref) = refs[17:19], refs[19:]
+    groups = [refs[at : at + 2] for at in (0, 2, 4)]
+    groups += [refs[at : at + 1] for at in (6, 7, 8)] + [refs[9:11], refs[11:13]]
+    slots_refs, (left_ref, adjoint_ref, picks_ref) = refs[13:16], refs[16:19]
+    ids_refs, (col_ref, row_ref) = refs[19:21], refs[21:]
     width = left_ref.shape[1] // 2
     col_ref[...] = column_part(
-        factor, own, adjoint_ref[...], left_ref[:, :width], columns_refs[:2], picks_ref
+        factor, own, adjoint_ref[...], left_ref[:, :width], (refs[0], refs[2]), picks_ref
     )
     slots_embed = slot_runs(left_ref, own)[:, :width]
     slots_adjoint = slot_runs(adjoint_ref, own)
-    half = columns_refs[-1].shape[0]
-    places = [(ref, at) for ref in slots_refs for at in range(0, ref.shape[1], half)]
+    block = left_ref.shape[0] // 2
+    places = [(ref, at) for ref in slots_refs for at in range(0, ref.shape[1], block)]
     summed = None
-    for ref in columns_refs:
-        link = nt_dot(slots_adjoint, ref[:, width:])
-        kernel = []
-        for _ in range(ref.shape[0] // half):
-            kernel_ref, at = places.pop(0)
-            kernel.append(kernel_ref[:, at : at + half])
-        weight = (link * jnp.concatenate(kernel, axis=1)).astype(BF16)
-        part = nn_dot(weight, with_ones(ref[:, :width]))
+    for group, (kernel_ref, at) in zip(groups, places):
+        columns = joint(group)
+        link = nt_dot(slots_adjoint, columns[:, width:])
+        weight = (link * kernel_ref[:, at : at + block]).astype(BF16)
+        part = nn_dot(weight, with_ones(columns[:, :width]))
         summed = part if summed is None else summed + part
     slot_rows = gradient(factor, summed, slots_embed)
     ids = jnp.concatenate([jnp.broadcast_to(ref[...], (own, own)) for ref in ids_refs], axis=1)
@@ -235,62 +235,53 @@
             pltpu.SemaphoreType.DMA((5,)),
         ],
     )(*arrays)
-    ids, halves = [slot_curve.reshape(1, own)], [observed]
+    ids = slot_curve.reshape(1, own)
     step = rows_axis // 2
-    if step > 1:
-        other = swap(packed, "row", step)
-        columns = jnp.concatenate([columns, other[:, : width + epochs]], axis=0)
-        observed = pl.pallas_call(
-            functools.partial(observed_kernel, width + epochs),
-            out_shape=shape((2 * own, epochs), BF16),
-            in_specs=[VMEM] * 2,
-            out_specs=VMEM,
-            compiler_params=PARAMS,
-            cost_estimate=pl.CostEstimate(
-                flops=1 << 30, bytes_accessed=other.nbytes, transcendentals=0
-            ),
-        )(observed, other)
-        halves, step = [observed], step // 2
-    ids.append(swap(ids[0], "col", 2))
-    while step > 1:
-        columns, halves = joined(columns, "row", step), [observed, swap(observed, "row", step)]
+    other, ids_y = lax.optimization_barrier((swap(packed, "row", step), swap(ids, "col", 2)))
+    columns = jnp.concatenate([columns, other[:, : width + epochs]], axis=0)
+    observed = pl.pallas_call(
+        functools.partial(observed_kernel, width + epochs),
+        out_shape=shape((2 * own, epochs), BF16),
+        in_specs=[VMEM] * 2,
+        out_specs=VMEM,
+        compiler_params=PARAMS,
+        cost_estimate=pl.CostEstimate(
+            flops=1 << 30, bytes_accessed=other.nbytes, transcendentals=0
+        ),
+    )(observed, other)
+    step //= 2
+    while step > 2:
+        columns, observed = joined(columns, "row", step), joined(observed, "row", step)
         step //= 2
-        if step > 1:
-            observed = jnp.concatenate(halves, axis=0)
-    block = columns.shape[0]
-    held, half = 2 * block, block // 2
-    x_block, y_block = swap(columns, "col", 1), swap(columns, "col", 2)
-    across = (swap(x_block[:half], "col", 2), swap(y_block[half:], "col", 1))
-    near = (columns, x_block, y_block)
-    far = tuple(swap(array, "row", 1) for array in near)
+    first, second = columns, swap(columns, "row", 2)
+    x_first, y_first = swap(first, "col", 1), swap(first, "col", 2)
+    y_second, x_second = swap(second, "col", 2), swap(second, "col", 1)
+    near = (first, second, x_first, x_second, y_first, y_second)
+    across = (swap(x_first, "col", 2), swap(y_second, "col", 1))
+    far = tuple(
+        swap(jnp.concatenate(near[at : at + 2], axis=0), "row", 1) for at in (0, 2, 4)
+    )
+    half = first.shape[0]
+    block, held = 2 * half, 4 * half
 
     def call(body, outs, *inputs):
-        blocks = 3 if body in (near_kernel, far_kernel) else 1
         return pl.pallas_call(
             functools.partial(body, scale, own),
             out_shape=outs,
             in_specs=[VMEM] * len(inputs),
             out_specs=[VMEM] * len(outs),
             compiler_params=PARAMS,
-            cost_estimate=pl.CostEstimate(
-                flops=2 * held * blocks * block * (2 * width + epochs),
-                bytes_accessed=1 << 20,
-                transcendentals=held * blocks * block,
-            ),
+            cost_estimate=pl.CostEstimate(flops=1 << 16, bytes_accessed=1 << 10, transcendentals=0),
         )(*inputs)
 
     fit_shape, picks_shape = shape((held, epochs), F32), shape((2 * own, held), F32)
-    slots = [shape((2 * own, count * block), F32) for count in (3, 1)]
-    left, fit, slots_near, picks_near = call(
-        near_kernel,
-        (shape((held, 2 * width), BF16), fit_shape, slots[0], picks_shape),
-        *near,
-    )
-    fit, halves, ids = lax.optimization_barrier((fit, halves, ids))
-    observed = jnp.concatenate(halves, axis=0)
-    observed_y = swap(observed, "col", 2)
-    fit, slots_far, picks_far = call(
-        far_kernel, (fit_shape, slots[0], picks_shape), *far, left, fit
+    slots = [shape((2 * own, count * block), F32) for count in (6, 1)]
+    observed_pair = (observed, swap(observed, "col", 2))
+    observed_z = swap(jnp.concatenate(observed_pair, axis=0), "row", 2)
+    left, fit, slots_main, picks_near, picks_far = call(
+        main_kernel,
+        (shape((held, 2 * width), BF16), fit_shape, slots[0], picks_shape, picks_shape),
+        *(*near, *far),
     )
     across, fit = lax.optimization_barrier((across, fit))
     far_across = tuple(swap(array, "row", 1) for array in across)
@@ -298,22 +289,22 @@
     slots_last, adjoint, col_far = pl.pallas_call(
         functools.partial(adjoint_kernel, scale, factor, own),
         out_shape=(slots[1], shape((held, epochs), BF16), shape((2 * own, width), F32)),
-        in_specs=[VMEM] * 9,
+        in_specs=[VMEM] * 10,
         out_specs=[VMEM] * 3,
         compiler_params=PARAMS,
-    )(*far_across, left, fit, *far[:2], picks_far, observed, observed_y)
+    )(*far_across, left, fit, *far[:2], picks_far, *observed_pair, observed_z)
     col_other = swap(col_far, "row", 1)
     col_near, row_part = pl.pallas_call(
         functools.partial(last_kernel, factor, own),
         out_shape=(shape((2 * own, width), F32),) * 2,
-        in_specs=[VMEM] * 19,
+        in_specs=[VMEM] * 21,
         out_specs=[VMEM] * 2,
         compiler_params=PARAMS,
         cost_estimate=pl.CostEstimate(flops=1 << 29, bytes_accessed=1 << 20, transcendentals=0),
     )(
         *(*near, *far, *across, *far_across),
-        *(slots_near, slots_far, slots_across, slots_last),
-        *(left, adjoint, picks_near, *ids),
+        *(slots_main, slots_across, slots_last),
+        *(left, adjoint, picks_near, ids, ids_y),
     )
     col_part = col_near + col_other
     other = swap(jnp.concatenate([col_part[own:], row_part[own:]], axis=0), "col", 1)
@@ -447,7 +438,7 @@
     own, width = curve_embed.shape
     rows_axis, cols_axis = lax.axis_size("row"), lax.axis_size("col")
     gathered = own * rows_axis * cols_axis * (width + solution.shape[1]) * 2
-    if gathered <= GATHER_LIMIT and power_of_two(rows_axis) and cols_axis == 4:
+    if gathered <= GATHER_LIMIT and rows_axis >= 8 and power_of_two(rows_axis) and cols_axis == 4:
         return gathered_plan(curve_embed, solution, *rest)
     return tiled_plan(curve_embed, solution, *rest)
 

time: 40.7 us -> 38.9 us (0.956)
  waiting for transfers between devices: 15.1 us -> 11 us
  starting transfers between devices: 15.2 us -> 18.5 us
  Pallas kernels: 8.6 us -> 7.6 us
    ppermute x16 -> x18, waiting for transfers between devices: 15.1 us -> 11 us  [swap(): return lax.ppermute(array, axis, pairs)]
    ppermute x16 -> x18, starting transfers between devices: 15.2 us -> 18.5 us  [swap(): return lax.ppermute(array, axis, pairs)]
    pallas_call x3 -> x2, Pallas kernels: 4.07 us -> 3.26 us  [call(): pl.pallas_call(functools.partial(body, scale, own), out_shape=outs, in_sp...]
  transfers between devices with their start and end apart: 16 -> 18, of which waited for: 7 -> 9; matrix products, arithmetic and copies ran while one was open for 0% -> 0% of each run, Pallas kernels for 13% -> 12%
where the time goes in v5:
time: 38.9 us; the launch traced here: 38.7 us
  starting transfers between devices  18.5 us (48%)
  waiting for transfers between devices  11 us (28%)
  Pallas kernels  7.6 us (20%)
  between operations  0.83 us (2%)
  other arithmetic  0.74 us (2%)
    ppermute x18, starting transfers between devices, swap(): return lax.ppermute(array, axis, pairs)  18.5 us
    ppermute x18, waiting for transfers between devices, swap(): return lax.ppermute(array, axis, pairs)  11 us
    pallas_call x2, Pallas kernels, call(): pl.pallas_call(functools.partial(body, scale, own), out_shape=outs, in_sp...  3.26 us
    pallas_call x1, Pallas kernels, gathered_plan(): pl.pallas_call(functools.partial(head_kernel, width), out_shape=(shape((o...  1.98 us
    pallas_call x1, Pallas kernels, gathered_plan(): pl.pallas_call(functools.partial(last_kernel, factor, own), out_shape=(sh...  1.48 us
    pallas_call x1, Pallas kernels, gathered_plan(): pl.pallas_call(functools.partial(adjoint_kernel, scale, factor, own), out...  0.87 us
  transfers between devices with their start and end apart: 18, of which 9 were waited for; matrix products, arithmetic and copies ran while one was open for 0% of the time, Pallas kernels for 12%

profile of v5, /device:TPU:0, one launch (start us, length us, event | category | flops | bytes accessed | tf_op | source)
XLA Modules:
  0.0 38.7 jit_solution(9645426820999051853)
XLA Ops:
  0.6 2.0 %shard_map.77 = (bf16[64,640]{1,0:T(8,128)(2,1)}, bf16[64,384]{1,0:T(8,128)(2,1)}, bf16[64,256]{1,0:T(8,128)(2,1)}) custom-call(bf16[64,128]{1,0:T(8,128)(2,1)} %refs_0_.1, f32[64,256]{1,0:T(8,128)} %refs_1_.1, bf16[64,256]{1,0:T(8,128)(2,1)} %refs_2_.1, s32[1,64]{1,0:T(1,128)} %bitcast.4, f32[256,256]{1,0:T(8,128)} %refs_4_.1), custom_call_target="tpu_custom_call" | custom-call | tf_op jit(solution)/shard_map/pallas_call | solution.py:224
  2.6 0.0 copy-start
  2.6 4.1 %collective-permute-start = (bf16[64,640]{1,0:T(8,128)(2,1)}, bf16[64,640]{1,0:T(8,128)(2,1)S(1)}, u32[]{:S(2)}, u32[]{:S(2)}) collective-permute-start(bf16[64,640]{1,0:T(8,128)(2,1)} %get-tuple-element.23), channel_id=1, source_target_pairs={{0,16},{4,20},{8,24},{12,28},{16,0},{20,4},{24,8},{28,12},{1,17},{... | collective-permute-start | bytes 245768 | tf_op jit(solution)/shard_map/ppermute | solution.py:208
  6.7 0.0 copy-done
  6.7 0.0 copy-start.2
  6.7 1.5 %collective-permute-start.1 = (s32[1,64]{1,0:T(1,128)S(1)}, s32[1,64]{1,0:T(1,128)S(1)}, u32[]{:S(2)}, u32[]{:S(2)}) collective-permute-start(s32[1,64]{1,0:T(1,128)S(1)} %bitcast.2), channel_id=1, source_target_pairs={{0,2},{1,3},{2,0},{3,1},{4,6},{5,7},{6,4},{7,5},{8,10},{9,11},{10,... | collective-permute-start | bytes 776 | tf_op jit(solution)/shard_map/ppermute | solution.py:208
  8.3 2.0 %collective-permute-done.1.refs_20_ = s32[1,64]{1,0:T(1,128)S(1)} collective-permute-done((s32[1,64]{1,0:T(1,128)S(1)}, s32[1,64]{1,0:T(1,128)S(1)}, u32[]{:S(2)}, u32[]{:S(2)}) %collective-permute-start.1) | collective-permute-done | bytes 288 | tf_op jit(solution)/shard_map/ppermute | solution.py:208
  10.3 0.9 %collective-permute-done.other_ref = bf16[64,640]{1,0:T(8,128)(2,1)S(1)} collective-permute-done((bf16[64,640]{1,0:T(8,128)(2,1)}, bf16[64,640]{1,0:T(8,128)(2,1)S(1)}, u32[]{:S(2)}, u32[]{:S(2)}) %collective-permute-start) | collective-permute-done | bytes 81952 | tf_op jit(solution)/shard_map/ppermute | solution.py:208
  11.1 0.0 copy-done.2
  11.2 0.0 copy-start.1
  11.2 0.9 %collective-permute-start.2 = (bf16[128,384]{1,0:T(8,128)(2,1)S(1)}, bf16[128,384]{1,0:T(8,128)(2,1)S(1)}, u32[]{:S(2)}, u32[]{:S(2)}) collective-permute-start(bf16[128,384]{1,0:T(8,128)(2,1)S(1)} %pad_maximum_fusion.4.refs_0_), channel_id=1, source_target_pairs={{0,8},{4,12},{8,0},{12,4},{16,24},{20,28},{24,16},{28,20},{1,9},{5... | collective-permute-start | bytes 294920 | tf_op jit(solution)/shard_map/ppermute | solution.py:208
  12.1 1.5 %collective-permute-start.3 = (bf16[128,384]{1,0:T(8,128)(2,1)S(1)}, bf16[128,384]{1,0:T(8,128)(2,1)S(1)}, u32[]{:S(2)}, u32[]{:S(2)}) collective-permute-start(bf16[128,384]{1,0:T(8,128)(2,1)S(1)} %pad_maximum_fusion.4.refs_0_), channel_id=1, source_target_pairs={{0,1},{1,0},{2,3},{3,2},{4,5},{5,4},{6,7},{7,6},{8,9},{9,8},{10,11... | collective-permute-start | bytes 294920 | tf_op jit(solution)/shard_map/ppermute | solution.py:208
  13.6 1.5 %collective-permute-start.5 = (bf16[128,384]{1,0:T(8,128)(2,1)S(1)}, bf16[128,384]{1,0:T(8,128)(2,1)S(1)}, u32[]{:S(2)}, u32[]{:S(2)}) collective-permute-start(bf16[128,384]{1,0:T(8,128)(2,1)S(1)} %pad_maximum_fusion.4.refs_0_), channel_id=1, source_target_pairs={{0,2},{1,3},{2,0},{3,1},{4,6},{5,7},{6,4},{7,5},{8,10},{9,11},{10,... | collective-permute-start | bytes 294920 | tf_op jit(solution)/shard_map/ppermute | solution.py:208
  15.1 0.0 copy-done.1
  15.1 0.6 %collective-permute-start.14 = (bf16[128,256]{1,0:T(8,128)(2,1)S(1)}, bf16[128,256]{1,0:T(8,128)(2,1)S(1)}, u32[]{:S(2)}, u32[]{:S(2)}) collective-permute-start(bf16[128,256]{1,0:T(8,128)(2,1)S(1)} %shard_map.80.refs_7_), channel_id=1, source_target_pairs={{0,2},{1,3},{2,0},{3,1},{4,6},{5,7},{6,4},{7,5},{8,10},{9,11},{10,... | collective-permute-start | bytes 196616 | tf_op jit(solution)/shard_map/ppermute | solution.py:208
  15.7 0.2 collective-permute-done.2.refs_1_
  15.9 1.7 %collective-permute-start.4 = (bf16[128,384]{1,0:T(8,128)(2,1)S(1)}, bf16[128,384]{1,0:T(8,128)(2,1)S(1)}, u32[]{:S(2)}, u32[]{:S(2)}) collective-permute-start(bf16[128,384]{1,0:T(8,128)(2,1)S(1)} %collective-permute-done.2.refs_1_), channel_id=1, source_target_pairs={{0,1},{1,0},{2,3},{3,2},{4,5},{5,4},{6,7},{7,6},{8,9},{9,8},{10,11... | collective-permute-start | bytes 294920 | tf_op jit(solution)/shard_map/ppermute | solution.py:208
  17.6 0.1 collective-permute-start.7
  17.6 0.0 collective-permute-done.3.refs_2_
  17.7 1.6 %collective-permute-start.6 = (bf16[128,384]{1,0:T(8,128)(2,1)S(1)}, bf16[128,384]{1,0:T(8,128)(2,1)S(1)}, u32[]{:S(2)}, u32[]{:S(2)}) collective-permute-start(bf16[128,384]{1,0:T(8,128)(2,1)S(1)} %collective-permute-done.2.refs_1_), channel_id=1, source_target_pairs={{0,2},{1,3},{2,0},{3,1},{4,6},{5,7},{6,4},{7,5},{8,10},{9,11},{10,... | collective-permute-start | bytes 294920 | tf_op jit(solution)/shard_map/ppermute | solution.py:208
  19.2 1.2 %collective-permute-done.4.refs_3_ = bf16[128,384]{1,0:T(8,128)(2,1)S(1)} collective-permute-done((bf16[128,384]{1,0:T(8,128)(2,1)S(1)}, bf16[128,384]{1,0:T(8,128)(2,1)S(1)}, u32[]{:S(2)}, u32[]{:S(2)}) %collective-permute-start.4) | collective-permute-done | bytes 98336 | tf_op jit(solution)/shard_map/ppermute | solution.py:208
  20.5 0.1 collective-permute-start.8
  20.6 0.0 collective-permute-done.5.refs_4_
  20.6 2.3 %collective-permute-done.6.refs_5_ = bf16[128,384]{1,0:T(8,128)(2,1)S(1)} collective-permute-done((bf16[128,384]{1,0:T(8,128)(2,1)S(1)}, bf16[128,384]{1,0:T(8,128)(2,1)S(1)}, u32[]{:S(2)}, u32[]{:S(2)}) %collective-permute-start.6) | collective-permute-done | bytes 98336 | tf_op jit(solution)/shard_map/ppermute | solution.py:208
  22.9 0.1 collective-permute-start.9
  23.0 1.6 %collective-permute-start.10 = (bf16[128,384]{1,0:T(8,128)(2,1)S(1)}, bf16[128,384]{1,0:T(8,128)(2,1)S(1)}, u32[]{:S(2)}, u32[]{:S(2)}) collective-permute-start(bf16[128,384]{1,0:T(8,128)(2,1)S(1)} %collective-permute-done.3.refs_2_), channel_id=1, source_target_pairs={{0,2},{1,3},{2,0},{3,1},{4,6},{5,7},{6,4},{7,5},{8,10},{9,11},{10,... | collective-permute-start | bytes 294920 | tf_op jit(solution)/shard_map/ppermute | solution.py:208
  24.6 0.0 collective-permute-done.14.refs_8_
  24.6 0.5 %collective-permute-start.11 = (bf16[128,384]{1,0:T(8,128)(2,1)S(1)}, bf16[128,384]{1,0:T(8,128)(2,1)S(1)}, u32[]{:S(2)}, u32[]{:S(2)}) collective-permute-start(bf16[128,384]{1,0:T(8,128)(2,1)S(1)} %collective-permute-done.6.refs_5_), channel_id=1, source_target_pairs={{0,1},{1,0},{2,3},{3,2},{4,5},{5,4},{6,7},{7,6},{8,9},{9,8},{10,11... | collective-permute-start | bytes 294920 | tf_op jit(solution)/shard_map/ppermute | solution.py:208
  25.1 0.0 collective-permute-done.7.refs_6_.refs_4_
  25.1 1.1 %collective-permute-start.15 = (bf16[256,256]{1,0:T(8,128)(2,1)S(1)}, bf16[256,256]{1,0:T(8,128)(2,1)S(1)}, u32[]{:S(2)}, u32[]{:S(2)}) collective-permute-start(bf16[256,256]{1,0:T(8,128)(2,1)S(1)} %pad_maximum_fusion.3), channel_id=1, source_target_pairs={{0,8},{4,12},{8,0},{12,4},{16,24},{20,28},{24,16},{28,20},{1,9},{5... | collective-permute-start | bytes 393224 | tf_op jit(solution)/shard_map/ppermute | solution.py:208
  26.2 0.0 collective-permute-done.8.refs_7_.refs_5_
  26.2 0.0 collective-permute-done.9.refs_8_
  26.2 2.7 %shard_map.78 = (bf16[512,256]{1,0:T(8,128)(2,1)S(1)}, f32[512,256]{1,0:T(8,128)S(1)}, f32[128,1536]{1,0:T(8,128)S(1)}, f32[128,512]{1,0:T(8,128)S(1)}, f32[128,512]{1,0:T(8,128)S(1)}) custom-call(bf16[128,384]{1,0:T(8,128)(2,1)S(1)} %pad_maximum_fusion.4.refs_0_, bf16[128,384]{1,0:T(8,128)(2,1)S(1)} %collective-permute-done.2.refs_1_, ...), custom_call_target="tpu_custom_call" | custom-call | flops 65536 | bytes 1024 | tf_op jit(solution)/shard_map/pallas_call | solution.py:268
  28.9 0.0 collective-permute-done.10.refs_0_.refs_9_
  28.9 0.6 %collective-permute-done.11.refs_1_.refs_10_ = bf16[128,384]{1,0:T(8,128)(2,1)S(1)} collective-permute-done((bf16[128,384]{1,0:T(8,128)(2,1)S(1)}, bf16[128,384]{1,0:T(8,128)(2,1)S(1)}, u32[]{:S(2)}, u32[]{:S(2)}) %collective-permute-start.11) | collective-permute-done | bytes 98336 | tf_op jit(solution)/shard_map/ppermute | solution.py:208
  29.4 0.0 collective-permute-start.12
  29.4 0.5 %collective-permute-start.13 = (bf16[128,384]{1,0:T(8,128)(2,1)S(1)}, bf16[128,384]{1,0:T(8,128)(2,1)S(1)}, u32[]{:S(2)}, u32[]{:S(2)}) collective-permute-start(bf16[128,384]{1,0:T(8,128)(2,1)S(1)} %collective-permute-done.11.refs_1_.refs_10_), channel_id=1, source_target_pairs={{0,4},{4,0},{8,12},{12,8},{16,20},{20,16},{24,28},{28,24},{1,5},{5... | collective-permute-start | bytes 294920 | tf_op jit(solution)/shard_map/ppermute | solution.py:208
  29.9 0.6 %shard_map.79 = (f32[512,256]{1,0:T(8,128)S(1)}, f32[128,256]{1,0:T(8,128)S(1)}) custom-call(bf16[128,384]{1,0:T(8,128)(2,1)S(1)} %collective-permute-done.10.refs_0_.refs_9_, bf16[128,384]{1,0:T(8,128)(2,1)S(1)} %collective-permute-done.11.refs_1_.refs_10_, bf16[512,256]{1,0:T(8,128)(2,1)S(1)} %get-tuple-element.29.refs_2_.refs_16_, ...), custom_call_target="tpu_custom_call" | custom-call | flops 65536 | bytes 1024 | tf_op jit(solution)/shard_map/pallas_call | solution.py:268
  30.5 0.0 collective-permute-done.15.refs_9_
  30.6 0.2 collective-permute-done.12.refs_0_.refs_11_
  30.7 0.2 collective-permute-done.13.refs_1_.refs_12_
  30.9 0.9 %shard_map.81 = (f32[128,256]{1,0:T(8,128)S(1)}, bf16[512,256]{1,0:T(8,128)(2,1)S(1)}, f32[128,128]{1,0:T(8,128)S(1)}) custom-call(bf16[128,384]{1,0:T(8,128)(2,1)S(1)} %collective-permute-done.12.refs_0_.refs_11_, bf16[128,384]{1,0:T(8,128)(2,1)S(1)} %collective-permute-done.13.refs_1_.refs_12_, bf16[512,256]{1,0:T(8,128)(2,1)S(1)} %get-tuple-element.29.refs_2_.refs_16_, ...), custom_call_target="tpu_custom_call" | custom-call | tf_op jit(solution)/shard_map/pallas_call | solution.py:289
  31.8 0.4 %collective-permute-start.16 = (f32[128,128]{1,0:T(8,128)S(1)}, f32[128,128]{1,0:T(8,128)S(1)}, u32[]{:S(2)}, u32[]{:S(2)}) collective-permute-start(f32[128,128]{1,0:T(8,128)S(1)} %get-tuple-element.41), channel_id=1, source_target_pairs={{0,4},{4,0},{8,12},{12,8},{16,20},{20,16},{24,28},{28,24},{1,5},{5... | collective-permute-start | bytes 196616 | tf_op jit(solution)/shard_map/ppermute | solution.py:208
  32.2 1.5 %shard_map.82 = (f32[128,128]{1,0:T(8,128)S(1)}, f32[128,128]{1,0:T(8,128)S(1)}) custom-call(bf16[128,384]{1,0:T(8,128)(2,1)S(1)} %pad_maximum_fusion.4.refs_0_, bf16[128,384]{1,0:T(8,128)(2,1)S(1)} %collective-permute-done.2.refs_1_, bf16[128,384]{1,0:T(8,128)(2,1)S(1)} %collective-permute-done.3.refs_2_, ...), custom_call_target="tpu_custom_call" | custom-call | flops 536870912 | bytes 1048576 | tf_op jit(solution)/shard_map/pallas_call | solution.py:297
  33.7 0.0 collective-permute-done.16
  33.7 0.8 %collective-permute-start.17 = (f32[128,128]{1,0:T(8,128)S(1)}, f32[128,128]{1,0:T(8,128)S(1)}, u32[]{:S(2)}, u32[]{:S(2)}) collective-permute-start(f32[128,128]{1,0:T(8,128)S(1)} %pad_maximum_fusion.5), channel_id=1, source_target_pairs={{0,1},{1,0},{2,3},{3,2},{4,5},{5,4},{6,7},{7,6},{8,9},{9,8},{10,11... | collective-permute-start | bytes 196616 | tf_op jit(solution)/shard_map/ppermute | solution.py:208
  34.6 3.5 %collective-permute-done.17 = f32[128,128]{1,0:T(8,128)S(1)} collective-permute-done((f32[128,128]{1,0:T(8,128)S(1)}, f32[128,128]{1,0:T(8,128)S(1)}, u32[]{:S(2)}, u32[]{:S(2)}) %collective-permute-start.17) | collective-permute-done | bytes 65568 | tf_op jit(solution)/shard_map/ppermute | solution.py:208
  38.1 0.6 %slice_add_fusion = (f32[64,128]{1,0:T(8,128)}, f32[64,128]{1,0:T(8,128)}) fusion(f32[128,128]{1,0:T(8,128)S(1)} %collective-permute-done.17, f32[128,128]{1,0:T(8,128)S(1)} %add.9, f32[128,128]{1,0:T(8,128)S(1)} %get-tuple-element.39), kind=kLoop, calls=%fused_computation.6 | loop fusion | flops 16384 | bytes 196608 | tf_op jit(solution)/shard_map/add | solution.py:311
  (11 shorter events, 0.1 us)
Async XLA Ops:
  2.6 4.1 %copy-start = (s32[64]{0:T(128)S(1)}, s32[64]{0:T(128)}, u32[]{:S(2)}) copy-start(s32[64]{0:T(128)} %param.10) | copy-start | bytes 772
  2.6 8.5 %collective-permute-start = (bf16[64,640]{1,0:T(8,128)(2,1)}, bf16[64,640]{1,0:T(8,128)(2,1)S(1)}, u32[]{:S(2)}, u32[]{:S(2)}) collective-permute-start(bf16[64,640]{1,0:T(8,128)(2,1)} %get-tuple-element.23), channel_id=1, source_target_pairs={{0,16},{4,20},{8,24},{12,28},{16,0},{20,4},{24,8},{28,12},{1,17},{... | collective-permute-start | bytes 245768 | tf_op jit(solution)/shard_map/ppermute | solution.py:208
  6.7 4.4 %copy-start.2 = (bf16[64,384]{1,0:T(8,128)(2,1)S(1)}, bf16[64,384]{1,0:T(8,128)(2,1)}, u32[]{:S(2)}) copy-start(bf16[64,384]{1,0:T(8,128)(2,1)} %get-tuple-element.22) | copy-start | bytes 147460
  6.7 3.5 %collective-permute-start.1 = (s32[1,64]{1,0:T(1,128)S(1)}, s32[1,64]{1,0:T(1,128)S(1)}, u32[]{:S(2)}, u32[]{:S(2)}) collective-permute-start(s32[1,64]{1,0:T(1,128)S(1)} %bitcast.2), channel_id=1, source_target_pairs={{0,2},{1,3},{2,0},{3,1},{4,6},{5,7},{6,4},{7,5},{8,10},{9,11},{10,... | collective-permute-start | bytes 776 | tf_op jit(solution)/shard_map/ppermute | solution.py:208
  11.2 3.9 %copy-start.1 = (bf16[64,256]{1,0:T(8,128)(2,1)S(1)}, bf16[64,256]{1,0:T(8,128)(2,1)}, u32[]{:S(2)}) copy-start(bf16[64,256]{1,0:T(8,128)(2,1)} %get-tuple-element.34.own_ref) | copy-start | bytes 98308
  11.2 4.7 %collective-permute-start.2 = (bf16[128,384]{1,0:T(8,128)(2,1)S(1)}, bf16[128,384]{1,0:T(8,128)(2,1)S(1)}, u32[]{:S(2)}, u32[]{:S(2)}) collective-permute-start(bf16[128,384]{1,0:T(8,128)(2,1)S(1)} %pad_maximum_fusion.4.refs_0_), channel_id=1, source_target_pairs={{0,8},{4,12},{8,0},{12,4},{16,24},{20,28},{24,16},{28,20},{1,9},{5... | collective-permute-start | bytes 294920 | tf_op jit(solution)/shard_map/ppermute | solution.py:208
  12.1 5.6 %collective-permute-start.3 = (bf16[128,384]{1,0:T(8,128)(2,1)S(1)}, bf16[128,384]{1,0:T(8,128)(2,1)S(1)}, u32[]{:S(2)}, u32[]{:S(2)}) collective-permute-start(bf16[128,384]{1,0:T(8,128)(2,1)S(1)} %pad_maximum_fusion.4.refs_0_), channel_id=1, source_target_pairs={{0,1},{1,0},{2,3},{3,2},{4,5},{5,4},{6,7},{7,6},{8,9},{9,8},{10,11... | collective-permute-start | bytes 294920 | tf_op jit(solution)/shard_map/ppermute | solution.py:208
  13.6 7.0 %collective-permute-start.5 = (bf16[128,384]{1,0:T(8,128)(2,1)S(1)}, bf16[128,384]{1,0:T(8,128)(2,1)S(1)}, u32[]{:S(2)}, u32[]{:S(2)}) collective-permute-start(bf16[128,384]{1,0:T(8,128)(2,1)S(1)} %pad_maximum_fusion.4.refs_0_), channel_id=1, source_target_pairs={{0,2},{1,3},{2,0},{3,1},{4,6},{5,7},{6,4},{7,5},{8,10},{9,11},{10,... | collective-permute-start | bytes 294920 | tf_op jit(solution)/shard_map/ppermute | solution.py:208
  15.1 9.5 %collective-permute-start.14 = (bf16[128,256]{1,0:T(8,128)(2,1)S(1)}, bf16[128,256]{1,0:T(8,128)(2,1)S(1)}, u32[]{:S(2)}, u32[]{:S(2)}) collective-permute-start(bf16[128,256]{1,0:T(8,128)(2,1)S(1)} %shard_map.80.refs_7_), channel_id=1, source_target_pairs={{0,2},{1,3},{2,0},{3,1},{4,6},{5,7},{6,4},{7,5},{8,10},{9,11},{10,... | collective-permute-start | bytes 196616 | tf_op jit(solution)/shard_map/ppermute | solution.py:208
  15.9 4.6 %collective-permute-start.4 = (bf16[128,384]{1,0:T(8,128)(2,1)S(1)}, bf16[128,384]{1,0:T(8,128)(2,1)S(1)}, u32[]{:S(2)}, u32[]{:S(2)}) collective-permute-start(bf16[128,384]{1,0:T(8,128)(2,1)S(1)} %collective-permute-done.2.refs_1_), channel_id=1, source_target_pairs={{0,1},{1,0},{2,3},{3,2},{4,5},{5,4},{6,7},{7,6},{8,9},{9,8},{10,11... | collective-permute-start | bytes 294920 | tf_op jit(solution)/shard_map/ppermute | solution.py:208
  17.6 7.5 %collective-permute-start.7 = (bf16[256,384]{1,0:T(8,128)(2,1)S(1)}, bf16[256,384]{1,0:T(8,128)(2,1)S(1)}, u32[]{:S(2)}, u32[]{:S(2)}) collective-permute-start(bf16[256,384]{1,0:T(8,128)(2,1)S(1)} %pad_maximum_fusion), channel_id=1, source_target_pairs={{0,4},{4,0},{8,12},{12,8},{16,20},{20,16},{24,28},{28,24},{1,5},{5... | collective-permute-start | bytes 589832 | tf_op jit(solution)/shard_map/ppermute | solution.py:208
  17.7 5.2 %collective-permute-start.6 = (bf16[128,384]{1,0:T(8,128)(2,1)S(1)}, bf16[128,384]{1,0:T(8,128)(2,1)S(1)}, u32[]{:S(2)}, u32[]{:S(2)}) collective-permute-start(bf16[128,384]{1,0:T(8,128)(2,1)S(1)} %collective-permute-done.2.refs_1_), channel_id=1, source_target_pairs={{0,2},{1,3},{2,0},{3,1},{4,6},{5,7},{6,4},{7,5},{8,10},{9,11},{10,... | collective-permute-start | bytes 294920 | tf_op jit(solution)/shard_map/ppermute | solution.py:208
  20.5 5.7 %collective-permute-start.8 = (bf16[256,384]{1,0:T(8,128)(2,1)S(1)}, bf16[256,384]{1,0:T(8,128)(2,1)S(1)}, u32[]{:S(2)}, u32[]{:S(2)}) collective-permute-start(bf16[256,384]{1,0:T(8,128)(2,1)S(1)} %pad_maximum_fusion.1), channel_id=1, source_target_pairs={{0,4},{4,0},{8,12},{12,8},{16,20},{20,16},{24,28},{28,24},{1,5},{5... | collective-permute-start | bytes 589832 | tf_op jit(solution)/shard_map/ppermute | solution.py:208
  22.9 3.3 %collective-permute-start.9 = (bf16[256,384]{1,0:T(8,128)(2,1)S(1)}, bf16[256,384]{1,0:T(8,128)(2,1)S(1)}, u32[]{:S(2)}, u32[]{:S(2)}) collective-permute-start(bf16[256,384]{1,0:T(8,128)(2,1)S(1)} %pad_maximum_fusion.2), channel_id=1, source_target_pairs={{0,4},{4,0},{8,12},{12,8},{16,20},{20,16},{24,28},{28,24},{1,5},{5... | collective-permute-start | bytes 589832 | tf_op jit(solution)/shard_map/ppermute | solution.py:208
  23.0 5.9 %collective-permute-start.10 = (bf16[128,384]{1,0:T(8,128)(2,1)S(1)}, bf16[128,384]{1,0:T(8,128)(2,1)S(1)}, u32[]{:S(2)}, u32[]{:S(2)}) collective-permute-start(bf16[128,384]{1,0:T(8,128)(2,1)S(1)} %collective-permute-done.3.refs_2_), channel_id=1, source_target_pairs={{0,2},{1,3},{2,0},{3,1},{4,6},{5,7},{6,4},{7,5},{8,10},{9,11},{10,... | collective-permute-start | bytes 294920 | tf_op jit(solution)/shard_map/ppermute | solution.py:208
  24.6 4.9 %collective-permute-start.11 = (bf16[128,384]{1,0:T(8,128)(2,1)S(1)}, bf16[128,384]{1,0:T(8,128)(2,1)S(1)}, u32[]{:S(2)}, u32[]{:S(2)}) collective-permute-start(bf16[128,384]{1,0:T(8,128)(2,1)S(1)} %collective-permute-done.6.refs_5_), channel_id=1, source_target_pairs={{0,1},{1,0},{2,3},{3,2},{4,5},{5,4},{6,7},{7,6},{8,9},{9,8},{10,11... | collective-permute-start | bytes 294920 | tf_op jit(solution)/shard_map/ppermute | solution.py:208
  25.1 5.4 %collective-permute-start.15 = (bf16[256,256]{1,0:T(8,128)(2,1)S(1)}, bf16[256,256]{1,0:T(8,128)(2,1)S(1)}, u32[]{:S(2)}, u32[]{:S(2)}) collective-permute-start(bf16[256,256]{1,0:T(8,128)(2,1)S(1)} %pad_maximum_fusion.3), channel_id=1, source_target_pairs={{0,8},{4,12},{8,0},{12,4},{16,24},{20,28},{24,16},{28,20},{1,9},{5... | collective-permute-start | bytes 393224 | tf_op jit(solution)/shard_map/ppermute | solution.py:208
  29.4 1.3 %collective-permute-start.12 = (bf16[128,384]{1,0:T(8,128)(2,1)S(1)}, bf16[128,384]{1,0:T(8,128)(2,1)S(1)}, u32[]{:S(2)}, u32[]{:S(2)}) collective-permute-start(bf16[128,384]{1,0:T(8,128)(2,1)S(1)} %collective-permute-done.10.refs_0_.refs_9_), channel_id=1, source_target_pairs={{0,4},{4,0},{8,12},{12,8},{16,20},{20,16},{24,28},{28,24},{1,5},{5... | collective-permute-start | bytes 294920 | tf_op jit(solution)/shard_map/ppermute | solution.py:208
  29.4 1.5 %collective-permute-start.13 = (bf16[128,384]{1,0:T(8,128)(2,1)S(1)}, bf16[128,384]{1,0:T(8,128)(2,1)S(1)}, u32[]{:S(2)}, u32[]{:S(2)}) collective-permute-start(bf16[128,384]{1,0:T(8,128)(2,1)S(1)} %collective-permute-done.11.refs_1_.refs_10_), channel_id=1, source_target_pairs={{0,4},{4,0},{8,12},{12,8},{16,20},{20,16},{24,28},{28,24},{1,5},{5... | collective-permute-start | bytes 294920 | tf_op jit(solution)/shard_map/ppermute | solution.py:208
  31.8 1.9 %collective-permute-start.16 = (f32[128,128]{1,0:T(8,128)S(1)}, f32[128,128]{1,0:T(8,128)S(1)}, u32[]{:S(2)}, u32[]{:S(2)}) collective-permute-start(f32[128,128]{1,0:T(8,128)S(1)} %get-tuple-element.41), channel_id=1, source_target_pairs={{0,4},{4,0},{8,12},{12,8},{16,20},{20,16},{24,28},{28,24},{1,5},{5... | collective-permute-start | bytes 196616 | tf_op jit(solution)/shard_map/ppermute | solution.py:208
  33.7 4.3 %collective-permute-start.17 = (f32[128,128]{1,0:T(8,128)S(1)}, f32[128,128]{1,0:T(8,128)S(1)}, u32[]{:S(2)}, u32[]{:S(2)}) collective-permute-start(f32[128,128]{1,0:T(8,128)S(1)} %pad_maximum_fusion.5), channel_id=1, source_target_pairs={{0,1},{1,0},{2,3},{3,2},{4,5},{5,4},{6,7},{7,6},{8,9},{9,8},{10,11... | collective-permute-start | bytes 196616 | tf_op jit(solution)/shard_map/ppermute | solution.py:208

commit v6 on v5

--- a/solution.py
+++ b/solution.py
@@ -9,6 +9,7 @@
 from jax.sharding import PartitionSpec as P
 
 GATHER_LIMIT = 4 << 20
+DIGIT = 256
 BF16, F32 = jnp.bfloat16, jnp.float32
 VMEM = pl.BlockSpec(memory_space=pltpu.VMEM)
 SMEM = pl.BlockSpec(memory_space=pltpu.SMEM)
@@ -45,22 +46,33 @@
     return lanes
 
 
-def head_kernel(width, *refs):
-    out_ref, columns_ref, observed_ref = refs[5:8]
-    held, semaphores = refs[8:13], refs[13]
+def fetch(sources, held, semaphores):
     copies = [
         pltpu.make_async_copy(source, target, semaphores.at[index])
-        for index, (source, target) in enumerate(zip(refs[:5], held))
+        for index, (source, target) in enumerate(zip(sources, held))
     ]
     for copy in copies:
         copy.start()
     for copy in copies:
         copy.wait()
-    embed_ref, solution_ref, targets_ref, lengths_ref, epoch_ref = held
-    rows, epochs = solution_ref.shape
+
+
+def head_kernel(width, *refs):
+    sources, columns_ref, held, semaphores = refs[:3], refs[3], refs[4:7], refs[7]
+    fetch(sources, held, semaphores)
+    embed_ref, solution_ref, epoch_ref = held
     fitted = jnp.dot(
         solution_ref[...], epoch_ref[...], precision=lax.Precision.HIGHEST, preferred_element_type=F32
     )
+    columns_ref[...] = jnp.concatenate([embed_ref[...], fitted.astype(BF16)], axis=1)
+
+
+def targets_kernel(*refs):
+    sources, (observed_ref, digits_ref) = refs[:3], refs[4:6]
+    held, semaphores = refs[6:9], refs[9]
+    fetch(sources, held, semaphores)
+    targets_ref, lengths_ref, ids_ref = held
+    rows, epochs = targets_ref.shape
     row = lax.broadcasted_iota(jnp.int32, (rows, rows), 0)
     column = lax.broadcasted_iota(jnp.int32, (rows, rows), 1)
     lengths = jnp.sum(
@@ -68,16 +80,12 @@
     )
     epoch = lax.broadcasted_iota(jnp.int32, (rows, epochs), 1).astype(F32)
     targets = jnp.where(epoch < lengths, targets_ref[...].astype(F32), jnp.inf)
-    columns = jnp.concatenate([embed_ref[...], fitted.astype(BF16)], axis=1)
-    columns_ref[...] = columns
     observed_ref[...] = targets.astype(BF16)
-    out_ref[:, : width + epochs] = columns
-    out_ref[:, width + epochs :] = targets.astype(BF16)
-
-
-def observed_kernel(first, own_ref, other_ref, out_ref):
-    out_ref[: own_ref.shape[0], :] = own_ref[...]
-    out_ref[own_ref.shape[0] :, :] = other_ref[:, first:]
+    ids = ids_ref[...]
+    place = lax.broadcasted_iota(jnp.int32, (digits_ref.shape[0], rows), 0)
+    digits = jnp.where(place == 0, ids // DIGIT, jnp.where(place == 1, ids % DIGIT, 0))
+    digits_ref[...] = jnp.zeros(digits_ref.shape, BF16)
+    digits_ref[:, :rows] = digits.astype(F32).astype(BF16)
 
 
 def with_ones(embed):
@@ -127,18 +135,18 @@
 
 
 def main_kernel(scale, own, *refs):
-    near, far = [refs[:2], refs[2:4], refs[4:6]], [(ref,) for ref in refs[6:9]]
-    left_ref, fit_ref, slots_ref, near_picks_ref, far_picks_ref = refs[9:]
+    groups = [(ref,) for ref in refs[:6]]
+    left_ref, fit_ref, slots_ref, near_picks_ref, far_picks_ref = refs[6:]
     block, width = left_ref.shape[0] // 2, left_ref.shape[1] // 2
-    for part, group in enumerate((near[0], near[2])):
+    for part, group in enumerate((groups[0], groups[2])):
         left_ref[part * block : (part + 1) * block, :] = extended(joint(group)[:, :width])(3, 0)
-    fit_ref[...] = fit_part(scale, own, near + far, left_ref, slots_ref, None)
-    pick_kernels(scale, own, refs[0], refs[2], left_ref, near_picks_ref)
-    pick_kernels(scale, own, refs[6], refs[7], left_ref, far_picks_ref)
+    fit_ref[...] = fit_part(scale, own, groups, left_ref, slots_ref, None)
+    pick_kernels(scale, own, refs[0], refs[1], left_ref, near_picks_ref)
+    pick_kernels(scale, own, refs[3], refs[4], left_ref, far_picks_ref)
 
 
 def across_kernel(scale, own, *refs):
-    group, (left_ref, before_ref, fit_ref, slots_ref) = refs[:2], refs[2:]
+    group, (left_ref, before_ref, fit_ref, slots_ref) = refs[:1], refs[1:]
     fit_ref[...] = fit_part(scale, own, (group,), left_ref, slots_ref, before_ref[...])
 
 
@@ -150,30 +158,29 @@
 
 
 def adjoint_kernel(scale, factor, own, *refs):
-    group, (left_ref, before_ref, own_ref, x_ref, picks_ref) = refs[:2], refs[2:7]
-    first_ref, first_y_ref, second_ref, slots_ref, adjoint_ref, col_ref = refs[7:]
+    group, (left_ref, before_ref, own_ref, x_ref, picks_ref) = refs[:1], refs[1:6]
+    targets_refs, (slots_ref, adjoint_ref, col_ref) = refs[6:8], refs[8:]
     width = left_ref.shape[1] // 2
-    half = first_ref.shape[0]
     fit = fit_part(scale, own, (group,), left_ref, slots_ref, before_ref[...])
-    targets = (first_ref[...], second_ref[:half, :], first_y_ref[...], second_ref[half:, :])
-    for part, values in enumerate(targets):
-        span = slice(part * half, (part + 1) * half)
-        values = values.astype(F32)
-        adjoint = jnp.where(values == jnp.inf, 0.0, values - fit[span])
-        adjoint_ref[span, :] = adjoint.astype(BF16)
+    block, run = fit.shape[0] // 2, targets_refs[0].shape[0]
+    for at in range(0, fit.shape[0], own):
+        part, piece = divmod(at // own, block // own)
+        which, first = divmod((2 * piece + part) * own, run)
+        values = targets_refs[which][first : first + own, :].astype(F32)
+        adjoint = jnp.where(values == jnp.inf, 0.0, values - fit[at : at + own])
+        adjoint_ref[at : at + own, :] = adjoint.astype(BF16)
     col_ref[...] = column_part(
         factor, own, adjoint_ref[...], left_ref[:, :width], (own_ref, x_ref), picks_ref
     )
 
 
 def last_kernel(factor, own, *refs):
-    groups = [refs[at : at + 2] for at in (0, 2, 4)]
-    groups += [refs[at : at + 1] for at in (6, 7, 8)] + [refs[9:11], refs[11:13]]
-    slots_refs, (left_ref, adjoint_ref, picks_ref) = refs[13:16], refs[16:19]
-    ids_refs, (col_ref, row_ref) = refs[19:21], refs[21:]
+    groups = [refs[at : at + 1] for at in range(8)]
+    slots_refs, (left_ref, adjoint_ref, picks_ref) = refs[8:11], refs[11:14]
+    ids_refs, (col_ref, row_ref) = refs[14:16], refs[16:]
     width = left_ref.shape[1] // 2
     col_ref[...] = column_part(
-        factor, own, adjoint_ref[...], left_ref[:, :width], (refs[0], refs[2]), picks_ref
+        factor, own, adjoint_ref[...], left_ref[:, :width], refs[:2], picks_ref
     )
     slots_embed = slot_runs(left_ref, own)[:, :width]
     slots_adjoint = slot_runs(adjoint_ref, own)
@@ -187,7 +194,12 @@
         part = nn_dot(weight, with_ones(columns[:, :width]))
         summed = part if summed is None else summed + part
     slot_rows = gradient(factor, summed, slots_embed)
-    ids = jnp.concatenate([jnp.broadcast_to(ref[...], (own, own)) for ref in ids_refs], axis=1)
+    ids = []
+    for ref in ids_refs:
+        digits = ref[ref.shape[0] - 16 :, :own].astype(F32)
+        values = (digits[0:1] * DIGIT + digits[1:2]).astype(jnp.int32)
+        ids.append(jnp.broadcast_to(values, (own, own)))
+    ids = jnp.concatenate(ids, axis=1)
     wanted = lax.broadcasted_iota(jnp.int32, ids.shape, 0)
     first = lax.axis_index("row") * lax.axis_size("col")
     for mask in (0, 1):
@@ -198,11 +210,6 @@
         )
 
 
-def observed_kernel(first, own_ref, other_ref, out_ref):
-    out_ref[: own_ref.shape[0], :] = own_ref[...]
-    out_ref[own_ref.shape[0] :, :] = other_ref[:, first:]
-
-
 def swap(array, axis, mask):
     pairs = [(index, index ^ mask) for index in range(lax.axis_size(axis))]
     return lax.ppermute(array, axis, pairs)
@@ -220,49 +227,47 @@
     factor = 2.0 / width
     shape = jax.ShapeDtypeStruct
 
-    arrays = (curve_embed, solution, targets, lengths.reshape(1, own), epoch_kernel)
-    packed, columns, observed = pl.pallas_call(
+    hbm = pl.BlockSpec(memory_space=pltpu.HBM)
+
+    def scratch(arrays):
+        buffers = [pltpu.VMEM(array.shape, array.dtype) for array in arrays]
+        return [*buffers, pltpu.SemaphoreType.DMA((len(arrays),))]
+
+    arrays = (curve_embed, solution, epoch_kernel)
+    columns = pl.pallas_call(
         functools.partial(head_kernel, width),
+        out_shape=shape((own, width + epochs), BF16),
+        in_specs=[hbm] * 3,
+        out_specs=VMEM,
+        scratch_shapes=scratch(arrays),
+    )(*arrays)
+    arrays = (targets, lengths.reshape(1, own), slot_curve.reshape(1, own))
+    observed, digits = pl.pallas_call(
+        targets_kernel,
         out_shape=(
-            shape((own, width + 2 * epochs), BF16),
-            shape((own, width + epochs), BF16),
             shape((own, epochs), BF16),
+            shape((16, epochs), BF16),
         ),
-        in_specs=[pl.BlockSpec(memory_space=pltpu.HBM)] * 5,
-        out_specs=[VMEM] * 3,
-        scratch_shapes=[
-            *(pltpu.VMEM(array.shape, array.dtype) for array in arrays),
-            pltpu.SemaphoreType.DMA((5,)),
-        ],
-    )(*arrays)
-    ids = slot_curve.reshape(1, own)
+        in_specs=[hbm] * 4,
+        out_specs=[VMEM] * 2,
+        scratch_shapes=scratch(arrays),
+        cost_estimate=pl.CostEstimate(flops=1 << 30, bytes_accessed=1 << 16, transcendentals=0),
+    )(*arrays, columns)
     step = rows_axis // 2
-    other, ids_y = lax.optimization_barrier((swap(packed, "row", step), swap(ids, "col", 2)))
-    columns = jnp.concatenate([columns, other[:, : width + epochs]], axis=0)
-    observed = pl.pallas_call(
-        functools.partial(observed_kernel, width + epochs),
-        out_shape=shape((2 * own, epochs), BF16),
-        in_specs=[VMEM] * 2,
-        out_specs=VMEM,
-        compiler_params=PARAMS,
-        cost_estimate=pl.CostEstimate(
-            flops=1 << 30, bytes_accessed=other.nbytes, transcendentals=0
-        ),
-    )(observed, other)
-    step //= 2
+    labelled = jnp.concatenate([observed, digits], axis=0)
+    received, _ = lax.optimization_barrier((swap(columns, "row", step), observed))
+    columns = jnp.concatenate([columns, received], axis=0)
+    labelled_y = swap(labelled, "col", 2)
+    observed = jnp.concatenate([observed, labelled_y[:own]], axis=0)
     while step > 2:
-        columns, observed = joined(columns, "row", step), joined(observed, "row", step)
+        observed = joined(observed, "row", step)
         step //= 2
-    first, second = columns, swap(columns, "row", 2)
-    x_first, y_first = swap(first, "col", 1), swap(first, "col", 2)
-    y_second, x_second = swap(second, "col", 2), swap(second, "col", 1)
-    near = (first, second, x_first, x_second, y_first, y_second)
-    across = (swap(x_first, "col", 2), swap(y_second, "col", 1))
-    far = tuple(
-        swap(jnp.concatenate(near[at : at + 2], axis=0), "row", 1) for at in (0, 2, 4)
-    )
-    half = first.shape[0]
-    block, held = 2 * half, 4 * half
+        columns = joined(columns, "row", step)
+    x_block, y_block = swap(columns, "col", 1), swap(columns, "col", 2)
+    across = swap(x_block, "col", 2)
+    near = (columns, x_block, y_block)
+    far = tuple(swap(array, "row", 1) for array in near)
+    block, held = columns.shape[0], 2 * columns.shape[0]
 
     def call(body, outs, *inputs):
         return pl.pallas_call(
@@ -276,35 +281,34 @@
 
     fit_shape, picks_shape = shape((held, epochs), F32), shape((2 * own, held), F32)
     slots = [shape((2 * own, count * block), F32) for count in (6, 1)]
-    observed_pair = (observed, swap(observed, "col", 2))
-    observed_z = swap(jnp.concatenate(observed_pair, axis=0), "row", 2)
+    observed_z = swap(observed, "row", 2)
     left, fit, slots_main, picks_near, picks_far = call(
         main_kernel,
         (shape((held, 2 * width), BF16), fit_shape, slots[0], picks_shape, picks_shape),
         *(*near, *far),
     )
-    across, fit = lax.optimization_barrier((across, fit))
-    far_across = tuple(swap(array, "row", 1) for array in across)
-    fit, slots_across = call(across_kernel, (fit_shape, slots[1]), *across, left, fit)
+    across, fit, observed_z = lax.optimization_barrier((across, fit, observed_z))
+    far_across = swap(across, "row", 1)
+    fit, slots_across = call(across_kernel, (fit_shape, slots[1]), across, left, fit)
     slots_last, adjoint, col_far = pl.pallas_call(
         functools.partial(adjoint_kernel, scale, factor, own),
         out_shape=(slots[1], shape((held, epochs), BF16), shape((2 * own, width), F32)),
-        in_specs=[VMEM] * 10,
+        in_specs=[VMEM] * 8,
         out_specs=[VMEM] * 3,
         compiler_params=PARAMS,
-    )(*far_across, left, fit, *far[:2], picks_far, *observed_pair, observed_z)
+    )(far_across, left, fit, *far[:2], picks_far, observed, observed_z)
     col_other = swap(col_far, "row", 1)
     col_near, row_part = pl.pallas_call(
         functools.partial(last_kernel, factor, own),
         out_shape=(shape((2 * own, width), F32),) * 2,
-        in_specs=[VMEM] * 21,
+        in_specs=[VMEM] * 16,
         out_specs=[VMEM] * 2,
         compiler_params=PARAMS,
         cost_estimate=pl.CostEstimate(flops=1 << 29, bytes_accessed=1 << 20, transcendentals=0),
     )(
-        *(*near, *far, *across, *far_across),
+        *(*near, *far, across, far_across),
         *(slots_main, slots_across, slots_last),
-        *(left, adjoint, picks_near, ids, ids_y),
+        *(left, adjoint, picks_near, digits, labelled_y),
     )
     col_part = col_near + col_other
     other = swap(jnp.concatenate([col_part[own:], row_part[own:]], axis=0), "col", 1)
@@ -438,7 +442,7 @@
     own, width = curve_embed.shape
     rows_axis, cols_axis = lax.axis_size("row"), lax.axis_size("col")
     gathered = own * rows_axis * cols_axis * (width + solution.shape[1]) * 2
-    if gathered <= GATHER_LIMIT and rows_axis >= 8 and power_of_two(rows_axis) and cols_axis == 4:
+    if gathered <= GATHER_LIMIT and rows_axis >= 8 and own <= solution.shape[1] and power_of_two(rows_axis) and cols_axis == 4:
         return gathered_plan(curve_embed, solution, *rest)
     return tiled_plan(curve_embed, solution, *rest)
 

time: 38.9 us -> 37.4 us (0.961)
  waiting for transfers between devices: 11 us -> 8.5 us
  Pallas kernels: 7.6 us -> 8.97 us
  starting transfers between devices: 18.5 us -> 17.9 us
    ppermute x18 -> x14, waiting for transfers between devices: 11 us -> 8.5 us  [swap(): return lax.ppermute(array, axis, pairs)]
    pallas_call x2, Pallas kernels: 1.99 us -> 3.37 us  [the longest x1 1.87 us: gathered_plan(): pl.pallas_call(functools.partial(head_kernel, width), out_shape=shape((ow...]
    ppermute x18 -> x14, starting transfers between devices: 18.5 us -> 17.9 us  [swap(): return lax.ppermute(array, axis, pairs)]
  transfers between devices with their start and end apart: 18 -> 14, of which waited for: 9 -> 7; matrix products, arithmetic and copies ran while one was open for 0% -> 0% of each run, Pallas kernels for 12% -> 17%
where the time goes in v6:
time: 37.4 us; the launch traced here: 36.9 us
  starting transfers between devices  17.9 us (48%)
  Pallas kernels  8.97 us (24%)
  waiting for transfers between devices  8.5 us (23%)
  between operations  0.75 us (2%)
  other arithmetic  0.7 us (2%)
    ppermute x14, starting transfers between devices, swap(): return lax.ppermute(array, axis, pairs)  17.9 us
    ppermute x14, waiting for transfers between devices, swap(): return lax.ppermute(array, axis, pairs)  8.5 us
    pallas_call x2, Pallas kernels, call(): pl.pallas_call(functools.partial(body, scale, own), out_shape=outs, in_sp...  3.26 us
    pallas_call x1, Pallas kernels, gathered_plan(): pl.pallas_call(functools.partial(head_kernel, width), out_shape=shape((ow...  1.87 us
    pallas_call x1, Pallas kernels, gathered_plan(): pl.pallas_call(targets_kernel, out_shape=(shape((own, epochs), BF16), sha...  1.5 us
    pallas_call x1, Pallas kernels, gathered_plan(): pl.pallas_call(functools.partial(last_kernel, factor, own), out_shape=(sh...  1.48 us
    pallas_call x1, Pallas kernels, gathered_plan(): pl.pallas_call(functools.partial(adjoint_kernel, scale, factor, own), out...  0.86 us
  transfers between devices with their start and end apart: 14, of which 7 were waited for; matrix products, arithmetic and copies ran while one was open for 0% of the time, Pallas kernels for 17%

profile of v6, /device:TPU:0, one launch (start us, length us, event | category | flops | bytes accessed | tf_op | source)
XLA Modules:
  0.0 36.9 jit_solution(278241139099696671)
XLA Ops:
  0.6 1.9 %shard_map.77.refs_3_ = bf16[64,384]{1,0:T(8,128)(2,1)} custom-call(bf16[64,128]{1,0:T(8,128)(2,1)} %refs_0_.2, f32[64,256]{1,0:T(8,128)} %refs_1_.1, f32[256,256]{1,0:T(8,128)} %refs_2_.1), custom_call_target="tpu_custom_call" | custom-call | tf_op jit(solution)/shard_map/pallas_call | solution.py:237
  2.5 4.1 %collective-permute-start = (bf16[64,384]{1,0:T(8,128)(2,1)}, bf16[64,384]{1,0:T(8,128)(2,1)S(1)}, u32[]{:S(2)}, u32[]{:S(2)}) collective-permute-start(bf16[64,384]{1,0:T(8,128)(2,1)} %shard_map.77.refs_3_), channel_id=1, source_target_pairs={{0,16},{4,20},{8,24},{12,28},{16,0},{20,4},{24,8},{28,12},{1,17},{... | collective-permute-start | bytes 147464 | tf_op jit(solution)/shard_map/ppermute | solution.py:215
  6.6 0.0 copy-start.1
  6.6 1.5 %shard_map.78 = (bf16[64,256]{1,0:T(8,128)(2,1)}, bf16[16,256]{1,0:T(8,128)(2,1)}) custom-call(bf16[64,256]{1,0:T(8,128)(2,1)} %refs_0_.3, s32[1,64]{1,0:T(1,128)} %bitcast.2, s32[1,64]{1,0:T(1,128)} %bitcast.3, bf16[64,384]{1,0:T(8,128)(2,1)} %shard_map.77.refs_3_), custom_call_target="tpu_custom_call" | custom-call | flops 1073741824 | bytes 65536 | tf_op jit(solution)/shard_map/pallas_call | solution.py:245
  8.1 1.3 %collective-permute-done = bf16[64,384]{1,0:T(8,128)(2,1)S(1)} collective-permute-done((bf16[64,384]{1,0:T(8,128)(2,1)}, bf16[64,384]{1,0:T(8,128)(2,1)S(1)}, u32[]{:S(2)}, u32[]{:S(2)}) %collective-permute-start) | collective-permute-done | bytes 49184 | tf_op jit(solution)/shard_map/ppermute | solution.py:215
  9.4 0.0 copy-done.1
  9.4 0.0 copy-start
  9.4 0.0 copy-start.2
  9.4 1.4 %collective-permute-start.1 = (bf16[128,384]{1,0:T(8,128)(2,1)S(1)}, bf16[128,384]{1,0:T(8,128)(2,1)S(1)}, u32[]{:S(2)}, u32[]{:S(2)}) collective-permute-start(bf16[128,384]{1,0:T(8,128)(2,1)S(1)} %pad_maximum_fusion.2), channel_id=1, source_target_pairs={{0,8},{4,12},{8,0},{12,4},{16,24},{20,28},{24,16},{28,20},{1,9},{5... | collective-permute-start | bytes 294920 | tf_op jit(solution)/shard_map/ppermute | solution.py:215
  10.9 0.0 copy-done
  10.9 0.0 copy-done.2
  10.9 1.6 %collective-permute-start.8 = (bf16[80,256]{1,0:T(8,128)(2,1)S(1)}, bf16[80,256]{1,0:T(8,128)(2,1)S(1)}, u32[]{:S(2)}, u32[]{:S(2)}) collective-permute-start(bf16[80,256]{1,0:T(8,128)(2,1)S(1)} %pad_maximum_fusion.5), channel_id=1, source_target_pairs={{0,2},{1,3},{2,0},{3,1},{4,6},{5,7},{6,4},{7,5},{8,10},{9,11},{10,... | collective-permute-start | bytes 122888 | tf_op jit(solution)/shard_map/ppermute | solution.py:215
  12.5 1.6 %collective-permute-done.1 = bf16[128,384]{1,0:T(8,128)(2,1)S(1)} collective-permute-done((bf16[128,384]{1,0:T(8,128)(2,1)S(1)}, bf16[128,384]{1,0:T(8,128)(2,1)S(1)}, u32[]{:S(2)}, u32[]{:S(2)}) %collective-permute-start.1) | collective-permute-done | bytes 98336 | tf_op jit(solution)/shard_map/ppermute | solution.py:215
  14.1 1.8 %collective-permute-start.2 = (bf16[256,384]{1,0:T(8,128)(2,1)S(1)}, bf16[256,384]{1,0:T(8,128)(2,1)S(1)}, u32[]{:S(2)}, u32[]{:S(2)}) collective-permute-start(bf16[256,384]{1,0:T(8,128)(2,1)S(1)} %pad_maximum_fusion.refs_0_), channel_id=1, source_target_pairs={{0,1},{1,0},{2,3},{3,2},{4,5},{5,4},{6,7},{7,6},{8,9},{9,8},{10,11... | collective-permute-start | bytes 589832 | tf_op jit(solution)/shard_map/ppermute | solution.py:215
  15.9 1.5 %collective-permute-start.3 = (bf16[256,384]{1,0:T(8,128)(2,1)S(1)}, bf16[256,384]{1,0:T(8,128)(2,1)S(1)}, u32[]{:S(2)}, u32[]{:S(2)}) collective-permute-start(bf16[256,384]{1,0:T(8,128)(2,1)S(1)} %pad_maximum_fusion.refs_0_), channel_id=1, source_target_pairs={{0,2},{1,3},{2,0},{3,1},{4,6},{5,7},{6,4},{7,5},{8,10},{9,11},{10,... | collective-permute-start | bytes 589832 | tf_op jit(solution)/shard_map/ppermute | solution.py:215
  17.4 0.0 collective-permute-done.8.refs_15_
  17.4 2.3 %collective-permute-start.9 = (bf16[128,256]{1,0:T(8,128)(2,1)S(1)}, bf16[128,256]{1,0:T(8,128)(2,1)S(1)}, u32[]{:S(2)}, u32[]{:S(2)}) collective-permute-start(bf16[128,256]{1,0:T(8,128)(2,1)S(1)} %pad_maximum_fusion.3), channel_id=1, source_target_pairs={{0,16},{4,20},{8,24},{12,28},{16,0},{20,4},{24,8},{28,12},{1,17},{... | collective-permute-start | bytes 196616 | tf_op jit(solution)/shard_map/ppermute | solution.py:215
  19.7 0.0 collective-permute-start.4
  19.7 0.1 collective-permute-done.2.refs_1_
  19.9 1.7 %collective-permute-start.7 = (bf16[256,384]{1,0:T(8,128)(2,1)S(1)}, bf16[256,384]{1,0:T(8,128)(2,1)S(1)}, u32[]{:S(2)}, u32[]{:S(2)}) collective-permute-start(bf16[256,384]{1,0:T(8,128)(2,1)S(1)} %collective-permute-done.2.refs_1_), channel_id=1, source_target_pairs={{0,2},{1,3},{2,0},{3,1},{4,6},{5,7},{6,4},{7,5},{8,10},{9,11},{10,... | collective-permute-start | bytes 589832 | tf_op jit(solution)/shard_map/ppermute | solution.py:215
  21.6 0.0 collective-permute-start.5
  21.6 0.0 collective-permute-done.3.refs_2_
  21.6 0.5 %collective-permute-start.6 = (bf16[256,384]{1,0:T(8,128)(2,1)S(1)}, bf16[256,384]{1,0:T(8,128)(2,1)S(1)}, u32[]{:S(2)}, u32[]{:S(2)}) collective-permute-start(bf16[256,384]{1,0:T(8,128)(2,1)S(1)} %collective-permute-done.3.refs_2_), channel_id=1, source_target_pairs={{0,4},{4,0},{8,12},{12,8},{16,20},{20,16},{24,28},{28,24},{1,5},{5... | collective-permute-start | bytes 589832 | tf_op jit(solution)/shard_map/ppermute | solution.py:215
  22.1 0.6 %collective-permute-done.9 = bf16[128,256]{1,0:T(8,128)(2,1)S(1)} collective-permute-done((bf16[128,256]{1,0:T(8,128)(2,1)S(1)}, bf16[128,256]{1,0:T(8,128)(2,1)S(1)}, u32[]{:S(2)}, u32[]{:S(2)}) %collective-permute-start.9) | collective-permute-done | bytes 65568 | tf_op jit(solution)/shard_map/ppermute | solution.py:215
  22.7 1.3 %collective-permute-start.10 = (bf16[256,256]{1,0:T(8,128)(2,1)S(1)}, bf16[256,256]{1,0:T(8,128)(2,1)S(1)}, u32[]{:S(2)}, u32[]{:S(2)}) collective-permute-start(bf16[256,256]{1,0:T(8,128)(2,1)S(1)} %pad_maximum_fusion.1.refs_6_), channel_id=1, source_target_pairs={{0,8},{4,12},{8,0},{12,4},{16,24},{20,28},{24,16},{28,20},{1,9},{5... | collective-permute-start | bytes 393224 | tf_op jit(solution)/shard_map/ppermute | solution.py:215
  24.0 0.0 collective-permute-done.4.refs_3_
  24.0 0.0 collective-permute-done.6.refs_5_
  24.0 0.0 collective-permute-done.5.refs_4_
  24.0 2.7 %shard_map.79 = (bf16[512,256]{1,0:T(8,128)(2,1)S(1)}, f32[512,256]{1,0:T(8,128)S(1)}, f32[128,1536]{1,0:T(8,128)S(1)}, f32[128,512]{1,0:T(8,128)S(1)}, f32[128,512]{1,0:T(8,128)S(1)}) custom-call(bf16[256,384]{1,0:T(8,128)(2,1)S(1)} %pad_maximum_fusion.refs_0_, bf16[256,384]{1,0:T(8,128)(2,1)S(1)} %collective-permute-done.2.refs_1_, ...), custom_call_target="tpu_custom_call" | custom-call | flops 65536 | bytes 1024 | tf_op jit(solution)/shard_map/pallas_call | solution.py:273
  26.7 1.0 %collective-permute-done.10.refs_7_ = bf16[256,256]{1,0:T(8,128)(2,1)S(1)} collective-permute-done((bf16[256,256]{1,0:T(8,128)(2,1)S(1)}, bf16[256,256]{1,0:T(8,128)(2,1)S(1)}, u32[]{:S(2)}, u32[]{:S(2)}) %collective-permute-start.10) | collective-permute-done | bytes 131104 | tf_op jit(solution)/shard_map/ppermute | solution.py:215
  27.7 0.0 collective-permute-done.7.refs_0_.refs_6_
  27.7 0.0 collective-permute-start.11
  27.7 0.6 %shard_map.80 = (f32[512,256]{1,0:T(8,128)S(1)}, f32[128,256]{1,0:T(8,128)S(1)}) custom-call(bf16[256,384]{1,0:T(8,128)(2,1)S(1)} %collective-permute-done.7.refs_0_.refs_6_, bf16[512,256]{1,0:T(8,128)(2,1)S(1)} %get-tuple-element.26.refs_1_.refs_11_, f32[512,256]{1,0:T(8,128)S(1)} %get-tuple-element.27.refs_2_), custom_call_target="tpu_custom_call" | custom-call | flops 65536 | bytes 1024 | tf_op jit(solution)/shard_map/pallas_call | solution.py:273
  28.3 0.8 %collective-permute-done.11.refs_0_.refs_7_ = bf16[256,384]{1,0:T(8,128)(2,1)S(1)} collective-permute-done((bf16[256,384]{1,0:T(8,128)(2,1)S(1)}, bf16[256,384]{1,0:T(8,128)(2,1)S(1)}, u32[]{:S(2)}, u32[]{:S(2)}) %collective-permute-start.11) | collective-permute-done | bytes 196640 | tf_op jit(solution)/shard_map/ppermute | solution.py:215
  29.2 0.9 %shard_map.81 = (f32[128,256]{1,0:T(8,128)S(1)}, bf16[512,256]{1,0:T(8,128)(2,1)S(1)}, f32[128,128]{1,0:T(8,128)S(1)}) custom-call(bf16[256,384]{1,0:T(8,128)(2,1)S(1)} %collective-permute-done.11.refs_0_.refs_7_, bf16[512,256]{1,0:T(8,128)(2,1)S(1)} %get-tuple-element.26.refs_1_.refs_11_, f32[512,256]{1,0:T(8,128)S(1)} %get-tuple-element.29.refs_2_, ...), custom_call_target="tpu_custom_call" | custom-call | tf_op jit(solution)/shard_map/pallas_call | solution.py:293
  30.1 0.2 collective-permute-start.12
  30.3 1.5 %shard_map.82 = (f32[128,128]{1,0:T(8,128)S(1)}, f32[128,128]{1,0:T(8,128)S(1)}) custom-call(bf16[256,384]{1,0:T(8,128)(2,1)S(1)} %pad_maximum_fusion.refs_0_, bf16[256,384]{1,0:T(8,128)(2,1)S(1)} %collective-permute-done.2.refs_1_, bf16[256,384]{1,0:T(8,128)(2,1)S(1)} %collective-permute-done.3.refs_2_, ...), custom_call_target="tpu_custom_call" | custom-call | flops 536870912 | bytes 1048576 | tf_op jit(solution)/shard_map/pallas_call | solution.py:301
  31.7 0.0 collective-permute-done.12
  31.8 1.5 %collective-permute-start.13 = (f32[128,128]{1,0:T(8,128)S(1)}, f32[128,128]{1,0:T(8,128)S(1)}, u32[]{:S(2)}, u32[]{:S(2)}) collective-permute-start(f32[128,128]{1,0:T(8,128)S(1)} %pad_maximum_fusion.4), channel_id=1, source_target_pairs={{0,1},{1,0},{2,3},{3,2},{4,5},{5,4},{6,7},{7,6},{8,9},{9,8},{10,11... | collective-permute-start | bytes 196616 | tf_op jit(solution)/shard_map/ppermute | solution.py:215
  33.3 3.0 %collective-permute-done.13 = f32[128,128]{1,0:T(8,128)S(1)} collective-permute-done((f32[128,128]{1,0:T(8,128)S(1)}, f32[128,128]{1,0:T(8,128)S(1)}, u32[]{:S(2)}, u32[]{:S(2)}) %collective-permute-start.13) | collective-permute-done | bytes 65568 | tf_op jit(solution)/shard_map/ppermute | solution.py:215
  36.2 0.6 %slice_add_fusion = (f32[64,128]{1,0:T(8,128)}, f32[64,128]{1,0:T(8,128)}) fusion(f32[128,128]{1,0:T(8,128)S(1)} %collective-permute-done.13, f32[128,128]{1,0:T(8,128)S(1)} %add.9, f32[128,128]{1,0:T(8,128)S(1)} %get-tuple-element.35), kind=kLoop, calls=%fused_computation.6 | loop fusion | flops 16384 | bytes 196608 | tf_op jit(solution)/shard_map/add | solution.py:315
  (10 shorter events, 0.1 us)
Async XLA Ops:
  2.5 6.9 %collective-permute-start = (bf16[64,384]{1,0:T(8,128)(2,1)}, bf16[64,384]{1,0:T(8,128)(2,1)S(1)}, u32[]{:S(2)}, u32[]{:S(2)}) collective-permute-start(bf16[64,384]{1,0:T(8,128)(2,1)} %shard_map.77.refs_3_), channel_id=1, source_target_pairs={{0,16},{4,20},{8,24},{12,28},{16,0},{20,4},{24,8},{28,12},{1,17},{... | collective-permute-start | bytes 147464 | tf_op jit(solution)/shard_map/ppermute | solution.py:215
  6.6 2.8 %copy-start.1 = (bf16[64,384]{1,0:T(8,128)(2,1)S(1)}, bf16[64,384]{1,0:T(8,128)(2,1)}, u32[]{:S(2)}) copy-start(bf16[64,384]{1,0:T(8,128)(2,1)} %shard_map.77.refs_3_) | copy-start | bytes 147460
  9.4 1.5 %copy-start = (bf16[16,256]{1,0:T(8,128)(2,1)S(1)}, bf16[16,256]{1,0:T(8,128)(2,1)}, u32[]{:S(2)}) copy-start(bf16[16,256]{1,0:T(8,128)(2,1)} %get-tuple-element.23.refs_14_) | copy-start | bytes 24580
  9.4 1.5 %copy-start.2 = (bf16[64,256]{1,0:T(8,128)(2,1)S(1)}, bf16[64,256]{1,0:T(8,128)(2,1)}, u32[]{:S(2)}) copy-start(bf16[64,256]{1,0:T(8,128)(2,1)} %get-tuple-element.20) | copy-start | bytes 98308
  9.4 4.7 %collective-permute-start.1 = (bf16[128,384]{1,0:T(8,128)(2,1)S(1)}, bf16[128,384]{1,0:T(8,128)(2,1)S(1)}, u32[]{:S(2)}, u32[]{:S(2)}) collective-permute-start(bf16[128,384]{1,0:T(8,128)(2,1)S(1)} %pad_maximum_fusion.2), channel_id=1, source_target_pairs={{0,8},{4,12},{8,0},{12,4},{16,24},{20,28},{24,16},{28,20},{1,9},{5... | collective-permute-start | bytes 294920 | tf_op jit(solution)/shard_map/ppermute | solution.py:215
  10.9 6.5 %collective-permute-start.8 = (bf16[80,256]{1,0:T(8,128)(2,1)S(1)}, bf16[80,256]{1,0:T(8,128)(2,1)S(1)}, u32[]{:S(2)}, u32[]{:S(2)}) collective-permute-start(bf16[80,256]{1,0:T(8,128)(2,1)S(1)} %pad_maximum_fusion.5), channel_id=1, source_target_pairs={{0,2},{1,3},{2,0},{3,1},{4,6},{5,7},{6,4},{7,5},{8,10},{9,11},{10,... | collective-permute-start | bytes 122888 | tf_op jit(solution)/shard_map/ppermute | solution.py:215
  14.1 5.7 %collective-permute-start.2 = (bf16[256,384]{1,0:T(8,128)(2,1)S(1)}, bf16[256,384]{1,0:T(8,128)(2,1)S(1)}, u32[]{:S(2)}, u32[]{:S(2)}) collective-permute-start(bf16[256,384]{1,0:T(8,128)(2,1)S(1)} %pad_maximum_fusion.refs_0_), channel_id=1, source_target_pairs={{0,1},{1,0},{2,3},{3,2},{4,5},{5,4},{6,7},{7,6},{8,9},{9,8},{10,11... | collective-permute-start | bytes 589832 | tf_op jit(solution)/shard_map/ppermute | solution.py:215
  15.9 5.7 %collective-permute-start.3 = (bf16[256,384]{1,0:T(8,128)(2,1)S(1)}, bf16[256,384]{1,0:T(8,128)(2,1)S(1)}, u32[]{:S(2)}, u32[]{:S(2)}) collective-permute-start(bf16[256,384]{1,0:T(8,128)(2,1)S(1)} %pad_maximum_fusion.refs_0_), channel_id=1, source_target_pairs={{0,2},{1,3},{2,0},{3,1},{4,6},{5,7},{6,4},{7,5},{8,10},{9,11},{10,... | collective-permute-start | bytes 589832 | tf_op jit(solution)/shard_map/ppermute | solution.py:215
  17.4 5.2 %collective-permute-start.9 = (bf16[128,256]{1,0:T(8,128)(2,1)S(1)}, bf16[128,256]{1,0:T(8,128)(2,1)S(1)}, u32[]{:S(2)}, u32[]{:S(2)}) collective-permute-start(bf16[128,256]{1,0:T(8,128)(2,1)S(1)} %pad_maximum_fusion.3), channel_id=1, source_target_pairs={{0,16},{4,20},{8,24},{12,28},{16,0},{20,4},{24,8},{28,12},{1,17},{... | collective-permute-start | bytes 196616 | tf_op jit(solution)/shard_map/ppermute | solution.py:215
  19.7 4.3 %collective-permute-start.4 = (bf16[256,384]{1,0:T(8,128)(2,1)S(1)}, bf16[256,384]{1,0:T(8,128)(2,1)S(1)}, u32[]{:S(2)}, u32[]{:S(2)}) collective-permute-start(bf16[256,384]{1,0:T(8,128)(2,1)S(1)} %pad_maximum_fusion.refs_0_), channel_id=1, source_target_pairs={{0,4},{4,0},{8,12},{12,8},{16,20},{20,16},{24,28},{28,24},{1,5},{5... | collective-permute-start | bytes 589832 | tf_op jit(solution)/shard_map/ppermute | solution.py:215
  19.9 7.9 %collective-permute-start.7 = (bf16[256,384]{1,0:T(8,128)(2,1)S(1)}, bf16[256,384]{1,0:T(8,128)(2,1)S(1)}, u32[]{:S(2)}, u32[]{:S(2)}) collective-permute-start(bf16[256,384]{1,0:T(8,128)(2,1)S(1)} %collective-permute-done.2.refs_1_), channel_id=1, source_target_pairs={{0,2},{1,3},{2,0},{3,1},{4,6},{5,7},{6,4},{7,5},{8,10},{9,11},{10,... | collective-permute-start | bytes 589832 | tf_op jit(solution)/shard_map/ppermute | solution.py:215
  21.6 2.4 %collective-permute-start.5 = (bf16[256,384]{1,0:T(8,128)(2,1)S(1)}, bf16[256,384]{1,0:T(8,128)(2,1)S(1)}, u32[]{:S(2)}, u32[]{:S(2)}) collective-permute-start(bf16[256,384]{1,0:T(8,128)(2,1)S(1)} %collective-permute-done.2.refs_1_), channel_id=1, source_target_pairs={{0,4},{4,0},{8,12},{12,8},{16,20},{20,16},{24,28},{28,24},{1,5},{5... | collective-permute-start | bytes 589832 | tf_op jit(solution)/shard_map/ppermute | solution.py:215
  21.6 2.4 %collective-permute-start.6 = (bf16[256,384]{1,0:T(8,128)(2,1)S(1)}, bf16[256,384]{1,0:T(8,128)(2,1)S(1)}, u32[]{:S(2)}, u32[]{:S(2)}) collective-permute-start(bf16[256,384]{1,0:T(8,128)(2,1)S(1)} %collective-permute-done.3.refs_2_), channel_id=1, source_target_pairs={{0,4},{4,0},{8,12},{12,8},{16,20},{20,16},{24,28},{28,24},{1,5},{5... | collective-permute-start | bytes 589832 | tf_op jit(solution)/shard_map/ppermute | solution.py:215
  22.7 5.0 %collective-permute-start.10 = (bf16[256,256]{1,0:T(8,128)(2,1)S(1)}, bf16[256,256]{1,0:T(8,128)(2,1)S(1)}, u32[]{:S(2)}, u32[]{:S(2)}) collective-permute-start(bf16[256,256]{1,0:T(8,128)(2,1)S(1)} %pad_maximum_fusion.1.refs_6_), channel_id=1, source_target_pairs={{0,8},{4,12},{8,0},{12,4},{16,24},{20,28},{24,16},{28,20},{1,9},{5... | collective-permute-start | bytes 393224 | tf_op jit(solution)/shard_map/ppermute | solution.py:215
  27.7 1.4 %collective-permute-start.11 = (bf16[256,384]{1,0:T(8,128)(2,1)S(1)}, bf16[256,384]{1,0:T(8,128)(2,1)S(1)}, u32[]{:S(2)}, u32[]{:S(2)}) collective-permute-start(bf16[256,384]{1,0:T(8,128)(2,1)S(1)} %collective-permute-done.7.refs_0_.refs_6_), channel_id=1, source_target_pairs={{0,4},{4,0},{8,12},{12,8},{16,20},{20,16},{24,28},{28,24},{1,5},{5... | collective-permute-start | bytes 589832 | tf_op jit(solution)/shard_map/ppermute | solution.py:215
  30.1 1.7 %collective-permute-start.12 = (f32[128,128]{1,0:T(8,128)S(1)}, f32[128,128]{1,0:T(8,128)S(1)}, u32[]{:S(2)}, u32[]{:S(2)}) collective-permute-start(f32[128,128]{1,0:T(8,128)S(1)} %get-tuple-element.37), channel_id=1, source_target_pairs={{0,4},{4,0},{8,12},{12,8},{16,20},{20,16},{24,28},{28,24},{1,5},{5... | collective-permute-start | bytes 196616 | tf_op jit(solution)/shard_map/ppermute | solution.py:215
  31.8 4.4 %collective-permute-start.13 = (f32[128,128]{1,0:T(8,128)S(1)}, f32[128,128]{1,0:T(8,128)S(1)}, u32[]{:S(2)}, u32[]{:S(2)}) collective-permute-start(f32[128,128]{1,0:T(8,128)S(1)} %pad_maximum_fusion.4), channel_id=1, source_target_pairs={{0,1},{1,0},{2,3},{3,2},{4,5},{5,4},{6,7},{7,6},{8,9},{9,8},{10,11... | collective-permute-start | bytes 196616 | tf_op jit(solution)/shard_map/ppermute | solution.py:215

commit v7 on v6

--- a/solution.py
+++ b/solution.py
@@ -106,48 +106,40 @@
     return jnp.concatenate([ref[:own, :], ref[half : half + own, :]], axis=0)
 
 
-def joint(refs):
-    return jnp.concatenate([ref[...] for ref in refs], axis=0)
-
-
-def fit_part(scale, own, groups, left_ref, slots_ref, total):
+def fit_part(scale, own, columns, rights, left, slots_ref, total):
+    width, half, place = left.shape[1] // 2, left.shape[0] // 2, 0
+    for values, right in zip(columns, rights):
+        kernel = jnp.exp2(nt_dot(left, right) * scale)
+        slots_ref[:, place : place + right.shape[0]] = jnp.concatenate(
+            [kernel[:own], kernel[half : half + own]], axis=0
+        )
+        part = nn_dot(kernel.astype(BF16), values[:, width:])
+        total = part if total is None else total + part
+        place += right.shape[0]
+    return total
+
+
+def main_kernel(scale, own, *refs):
+    columns, (left_ref, fit_ref, slots_ref, *picks_refs) = [ref[...] for ref in refs[:6]], refs[6:]
     width = left_ref.shape[1] // 2
-    left = left_ref[...]
-    slots_left = slot_runs(left_ref, own)
-    place = 0
-    for group in groups:
-        columns = joint(group)
-        right = extended(columns[:, :width])(0, 3)
-        kernel = jnp.exp2(nt_dot(left, right) * scale).astype(BF16)
-        part = nn_dot(kernel, columns[:, width:])
-        total = part if total is None else total + part
-        slots_ref[:, place : place + columns.shape[0]] = jnp.exp2(
-            nt_dot(slots_left, right) * scale
-        )
-        place += columns.shape[0]
-    return total
-
-
-def pick_kernels(scale, own, first_ref, second_ref, left_ref, picks_ref):
-    width = left_ref.shape[1] // 2
-    right = extended(stacked((first_ref, second_ref), own)[:, :width])(0, 3)
-    picks_ref[...] = jnp.exp2(nt_dot(right, left_ref[...]) * scale)
-
-
-def main_kernel(scale, own, *refs):
-    groups = [(ref,) for ref in refs[:6]]
-    left_ref, fit_ref, slots_ref, near_picks_ref, far_picks_ref = refs[6:]
-    block, width = left_ref.shape[0] // 2, left_ref.shape[1] // 2
-    for part, group in enumerate((groups[0], groups[2])):
-        left_ref[part * block : (part + 1) * block, :] = extended(joint(group)[:, :width])(3, 0)
-    fit_ref[...] = fit_part(scale, own, groups, left_ref, slots_ref, None)
-    pick_kernels(scale, own, refs[0], refs[1], left_ref, near_picks_ref)
-    pick_kernels(scale, own, refs[3], refs[4], left_ref, far_picks_ref)
-
-
-def across_kernel(scale, own, *refs):
-    group, (left_ref, before_ref, fit_ref, slots_ref) = refs[:1], refs[1:]
-    fit_ref[...] = fit_part(scale, own, (group,), left_ref, slots_ref, before_ref[...])
+    forms = [extended(values[:, :width]) for values in columns]
+    left = jnp.concatenate([forms[0](3, 0), forms[2](3, 0)], axis=0)
+    left_ref[...] = left
+    rights = [form(0, 3) for form in forms]
+    fit_ref[...] = fit_part(scale, own, columns, rights, left, slots_ref, None)
+    for picks_ref, first in zip(picks_refs, (0, 3)):
+        picked = jnp.concatenate([rights[first][:own], rights[first + 1][:own]], axis=0)
+        picks_ref[...] = jnp.exp2(nt_dot(picked, left) * scale)
+
+
+def across_part(scale, own, columns_ref, left_ref, before_ref, slots_ref):
+    columns, width = columns_ref[...], left_ref.shape[1] // 2
+    right = extended(columns[:, :width])(0, 3)
+    return fit_part(scale, own, [columns], [right], left_ref[...], slots_ref, before_ref[...])
+
+
+def across_kernel(scale, own, columns_ref, left_ref, before_ref, fit_ref, slots_ref):
+    fit_ref[...] = across_part(scale, own, columns_ref, left_ref, before_ref, slots_ref)
 
 
 def column_part(factor, own, adjoint, embed, refs, kernel_ref):
@@ -158,10 +150,10 @@
 
 
 def adjoint_kernel(scale, factor, own, *refs):
-    group, (left_ref, before_ref, own_ref, x_ref, picks_ref) = refs[:1], refs[1:6]
+    across_ref, left_ref, before_ref, own_ref, x_ref, picks_ref = refs[:6]
     targets_refs, (slots_ref, adjoint_ref, col_ref) = refs[6:8], refs[8:]
     width = left_ref.shape[1] // 2
-    fit = fit_part(scale, own, (group,), left_ref, slots_ref, before_ref[...])
+    fit = across_part(scale, own, across_ref, left_ref, before_ref, slots_ref)
     block, run = fit.shape[0] // 2, targets_refs[0].shape[0]
     for at in range(0, fit.shape[0], own):
         part, piece = divmod(at // own, block // own)
@@ -175,7 +167,7 @@
 
 
 def last_kernel(factor, own, *refs):
-    groups = [refs[at : at + 1] for at in range(8)]
+    columns_refs = refs[:8]
     slots_refs, (left_ref, adjoint_ref, picks_ref) = refs[8:11], refs[11:14]
     ids_refs, (col_ref, row_ref) = refs[14:16], refs[16:]
     width = left_ref.shape[1] // 2
@@ -187,8 +179,8 @@
     block = left_ref.shape[0] // 2
     places = [(ref, at) for ref in slots_refs for at in range(0, ref.shape[1], block)]
     summed = None
-    for group, (kernel_ref, at) in zip(groups, places):
-        columns = joint(group)
+    for columns_ref, (kernel_ref, at) in zip(columns_refs, places):
+        columns = columns_ref[...]
         link = nt_dot(slots_adjoint, columns[:, width:])
         weight = (link * kernel_ref[:, at : at + block]).astype(BF16)
         part = nn_dot(weight, with_ones(columns[:, :width]))
@@ -198,16 +190,19 @@
     for ref in ids_refs:
         digits = ref[ref.shape[0] - 16 :, :own].astype(F32)
         values = (digits[0:1] * DIGIT + digits[1:2]).astype(jnp.int32)
-        ids.append(jnp.broadcast_to(values, (own, own)))
+        ids.append(jnp.broadcast_to(values, (2 * own, own)))
     ids = jnp.concatenate(ids, axis=1)
     wanted = lax.broadcasted_iota(jnp.int32, ids.shape, 0)
     first = lax.axis_index("row") * lax.axis_size("col")
-    for mask in (0, 1):
-        base = (first + (lax.axis_index("col") ^ mask)) * own
-        chosen = (ids == wanted + base).astype(F32)
-        row_ref[mask * own : (mask + 1) * own, :] = jnp.dot(
-            chosen, slot_rows, precision=lax.Precision.HIGHEST, preferred_element_type=F32
-        )
+    bases = [(first + (lax.axis_index("col") ^ mask)) * own for mask in (0, 1)]
+    wanted += jnp.where(wanted < own, bases[0], bases[1] - own)
+    chosen = jnp.where(ids == wanted, 1.0, 0.0).astype(BF16)
+    high = slot_rows.astype(BF16)
+    rest = slot_rows - high.astype(F32)
+    middle = rest.astype(BF16)
+    low = (rest - middle.astype(F32)).astype(BF16)
+    terms = nn_dot(chosen, jnp.concatenate([high, middle, low], axis=1))
+    row_ref[...] = terms[:, :width] + terms[:, width : 2 * width] + terms[:, 2 * width :]
 
 
 def swap(array, axis, mask):

time: 37.4 us -> 37.2 us (level)
  Pallas kernels: 8.97 us -> 7.57 us
  waiting for transfers between devices: 8.5 us -> 9.72 us
    ppermute x14, waiting for transfers between devices: 8.5 us -> 9.72 us  [swap(): return lax.ppermute(array, axis, pairs)]
    pallas_call x2, Pallas kernels: 3.26 us -> 2.05 us  [call(): pl.pallas_call(functools.partial(body, scale, own), out_shape=outs, in_sp...]
  transfers between devices with their start and end apart: 14 -> 14, of which waited for: 7 -> 7; matrix products, arithmetic and copies ran while one was open for 0% -> 0% of each run, Pallas kernels for 17% -> 13%
where the time goes in v7:
time: 37.2 us; the launch traced here: 36.7 us
  starting transfers between devices  17.9 us (48%)
  waiting for transfers between devices  9.72 us (26%)
  Pallas kernels  7.57 us (20%)
  between operations  0.75 us (2%)
  other arithmetic  0.7 us (2%)
    ppermute x14, starting transfers between devices, swap(): return lax.ppermute(array, axis, pairs)  17.9 us
    ppermute x14, waiting for transfers between devices, swap(): return lax.ppermute(array, axis, pairs)  9.72 us
    pallas_call x2, Pallas kernels, call(): pl.pallas_call(functools.partial(body, scale, own), out_shape=outs, in_sp...  2.05 us
    pallas_call x1, Pallas kernels, gathered_plan(): pl.pallas_call(functools.partial(head_kernel, width), out_shape=shape((ow...  1.87 us
    pallas_call x1, Pallas kernels, gathered_plan(): pl.pallas_call(targets_kernel, out_shape=(shape((own, epochs), BF16), sha...  1.5 us
    pallas_call x1, Pallas kernels, gathered_plan(): pl.pallas_call(functools.partial(last_kernel, factor, own), out_shape=(sh...  1.29 us
    pallas_call x1, Pallas kernels, gathered_plan(): pl.pallas_call(functools.partial(adjoint_kernel, scale, factor, own), out...  0.86 us
  transfers between devices with their start and end apart: 14, of which 7 were waited for; matrix products, arithmetic and copies ran while one was open for 0% of the time, Pallas kernels for 13%

profile of v7, /device:TPU:0, one launch (start us, length us, event | category | flops | bytes accessed | tf_op | source)
XLA Modules:
  0.0 36.7 jit_solution(2392027753037444276)
XLA Ops:
  0.6 1.9 %shard_map.77.refs_3_ = bf16[64,384]{1,0:T(8,128)(2,1)} custom-call(bf16[64,128]{1,0:T(8,128)(2,1)} %refs_0_.2, f32[64,256]{1,0:T(8,128)} %refs_1_.1, f32[256,256]{1,0:T(8,128)} %refs_2_.1), custom_call_target="tpu_custom_call" | custom-call | tf_op jit(solution)/shard_map/pallas_call | solution.py:232
  2.5 4.1 %collective-permute-start = (bf16[64,384]{1,0:T(8,128)(2,1)}, bf16[64,384]{1,0:T(8,128)(2,1)S(1)}, u32[]{:S(2)}, u32[]{:S(2)}) collective-permute-start(bf16[64,384]{1,0:T(8,128)(2,1)} %shard_map.77.refs_3_), channel_id=1, source_target_pairs={{0,16},{4,20},{8,24},{12,28},{16,0},{20,4},{24,8},{28,12},{1,17},{... | collective-permute-start | bytes 147464 | tf_op jit(solution)/shard_map/ppermute | solution.py:210
  6.6 0.0 copy-start.1
  6.6 1.5 %shard_map.78 = (bf16[64,256]{1,0:T(8,128)(2,1)}, bf16[16,256]{1,0:T(8,128)(2,1)}) custom-call(bf16[64,256]{1,0:T(8,128)(2,1)} %refs_0_.3, s32[1,64]{1,0:T(1,128)} %bitcast.2, s32[1,64]{1,0:T(1,128)} %bitcast.3, bf16[64,384]{1,0:T(8,128)(2,1)} %shard_map.77.refs_3_), custom_call_target="tpu_custom_call" | custom-call | flops 1073741824 | bytes 65536 | tf_op jit(solution)/shard_map/pallas_call | solution.py:240
  8.1 1.3 %collective-permute-done = bf16[64,384]{1,0:T(8,128)(2,1)S(1)} collective-permute-done((bf16[64,384]{1,0:T(8,128)(2,1)}, bf16[64,384]{1,0:T(8,128)(2,1)S(1)}, u32[]{:S(2)}, u32[]{:S(2)}) %collective-permute-start) | collective-permute-done | bytes 49184 | tf_op jit(solution)/shard_map/ppermute | solution.py:210
  9.4 0.0 copy-done.1
  9.4 0.0 copy-start
  9.4 0.0 copy-start.2
  9.4 1.4 %collective-permute-start.1 = (bf16[128,384]{1,0:T(8,128)(2,1)S(1)}, bf16[128,384]{1,0:T(8,128)(2,1)S(1)}, u32[]{:S(2)}, u32[]{:S(2)}) collective-permute-start(bf16[128,384]{1,0:T(8,128)(2,1)S(1)} %pad_maximum_fusion.2), channel_id=1, source_target_pairs={{0,8},{4,12},{8,0},{12,4},{16,24},{20,28},{24,16},{28,20},{1,9},{5... | collective-permute-start | bytes 294920 | tf_op jit(solution)/shard_map/ppermute | solution.py:210
  10.9 0.0 copy-done
  10.9 0.0 copy-done.2
  10.9 1.6 %collective-permute-start.8 = (bf16[80,256]{1,0:T(8,128)(2,1)S(1)}, bf16[80,256]{1,0:T(8,128)(2,1)S(1)}, u32[]{:S(2)}, u32[]{:S(2)}) collective-permute-start(bf16[80,256]{1,0:T(8,128)(2,1)S(1)} %pad_maximum_fusion.5), channel_id=1, source_target_pairs={{0,2},{1,3},{2,0},{3,1},{4,6},{5,7},{6,4},{7,5},{8,10},{9,11},{10,... | collective-permute-start | bytes 122888 | tf_op jit(solution)/shard_map/ppermute | solution.py:210
  12.5 1.6 %collective-permute-done.1 = bf16[128,384]{1,0:T(8,128)(2,1)S(1)} collective-permute-done((bf16[128,384]{1,0:T(8,128)(2,1)S(1)}, bf16[128,384]{1,0:T(8,128)(2,1)S(1)}, u32[]{:S(2)}, u32[]{:S(2)}) %collective-permute-start.1) | collective-permute-done | bytes 98336 | tf_op jit(solution)/shard_map/ppermute | solution.py:210
  14.1 1.8 %collective-permute-start.2 = (bf16[256,384]{1,0:T(8,128)(2,1)S(1)}, bf16[256,384]{1,0:T(8,128)(2,1)S(1)}, u32[]{:S(2)}, u32[]{:S(2)}) collective-permute-start(bf16[256,384]{1,0:T(8,128)(2,1)S(1)} %pad_maximum_fusion.refs_0_), channel_id=1, source_target_pairs={{0,1},{1,0},{2,3},{3,2},{4,5},{5,4},{6,7},{7,6},{8,9},{9,8},{10,11... | collective-permute-start | bytes 589832 | tf_op jit(solution)/shard_map/ppermute | solution.py:210
  15.9 1.5 %collective-permute-start.3 = (bf16[256,384]{1,0:T(8,128)(2,1)S(1)}, bf16[256,384]{1,0:T(8,128)(2,1)S(1)}, u32[]{:S(2)}, u32[]{:S(2)}) collective-permute-start(bf16[256,384]{1,0:T(8,128)(2,1)S(1)} %pad_maximum_fusion.refs_0_), channel_id=1, source_target_pairs={{0,2},{1,3},{2,0},{3,1},{4,6},{5,7},{6,4},{7,5},{8,10},{9,11},{10,... | collective-permute-start | bytes 589832 | tf_op jit(solution)/shard_map/ppermute | solution.py:210
  17.4 0.0 collective-permute-done.8.refs_15_
  17.4 2.3 %collective-permute-start.9 = (bf16[128,256]{1,0:T(8,128)(2,1)S(1)}, bf16[128,256]{1,0:T(8,128)(2,1)S(1)}, u32[]{:S(2)}, u32[]{:S(2)}) collective-permute-start(bf16[128,256]{1,0:T(8,128)(2,1)S(1)} %pad_maximum_fusion.3), channel_id=1, source_target_pairs={{0,16},{4,20},{8,24},{12,28},{16,0},{20,4},{24,8},{28,12},{1,17},{... | collective-permute-start | bytes 196616 | tf_op jit(solution)/shard_map/ppermute | solution.py:210
  19.7 0.0 collective-permute-start.4
  19.7 0.1 collective-permute-done.2.refs_1_
  19.9 1.7 %collective-permute-start.7 = (bf16[256,384]{1,0:T(8,128)(2,1)S(1)}, bf16[256,384]{1,0:T(8,128)(2,1)S(1)}, u32[]{:S(2)}, u32[]{:S(2)}) collective-permute-start(bf16[256,384]{1,0:T(8,128)(2,1)S(1)} %collective-permute-done.2.refs_1_), channel_id=1, source_target_pairs={{0,2},{1,3},{2,0},{3,1},{4,6},{5,7},{6,4},{7,5},{8,10},{9,11},{10,... | collective-permute-start | bytes 589832 | tf_op jit(solution)/shard_map/ppermute | solution.py:210
  21.6 0.0 collective-permute-start.5
  21.6 0.0 collective-permute-done.3.refs_2_
  21.6 0.5 %collective-permute-start.6 = (bf16[256,384]{1,0:T(8,128)(2,1)S(1)}, bf16[256,384]{1,0:T(8,128)(2,1)S(1)}, u32[]{:S(2)}, u32[]{:S(2)}) collective-permute-start(bf16[256,384]{1,0:T(8,128)(2,1)S(1)} %collective-permute-done.3.refs_2_), channel_id=1, source_target_pairs={{0,4},{4,0},{8,12},{12,8},{16,20},{20,16},{24,28},{28,24},{1,5},{5... | collective-permute-start | bytes 589832 | tf_op jit(solution)/shard_map/ppermute | solution.py:210
  22.1 0.6 %collective-permute-done.9 = bf16[128,256]{1,0:T(8,128)(2,1)S(1)} collective-permute-done((bf16[128,256]{1,0:T(8,128)(2,1)S(1)}, bf16[128,256]{1,0:T(8,128)(2,1)S(1)}, u32[]{:S(2)}, u32[]{:S(2)}) %collective-permute-start.9) | collective-permute-done | bytes 65568 | tf_op jit(solution)/shard_map/ppermute | solution.py:210
  22.7 1.3 %collective-permute-start.10 = (bf16[256,256]{1,0:T(8,128)(2,1)S(1)}, bf16[256,256]{1,0:T(8,128)(2,1)S(1)}, u32[]{:S(2)}, u32[]{:S(2)}) collective-permute-start(bf16[256,256]{1,0:T(8,128)(2,1)S(1)} %pad_maximum_fusion.1.refs_6_), channel_id=1, source_target_pairs={{0,8},{4,12},{8,0},{12,4},{16,24},{20,28},{24,16},{28,20},{1,9},{5... | collective-permute-start | bytes 393224 | tf_op jit(solution)/shard_map/ppermute | solution.py:210
  24.0 0.0 collective-permute-done.4.refs_3_
  24.0 0.0 collective-permute-done.6.refs_5_
  24.0 0.0 collective-permute-done.5.refs_4_
  24.0 1.5 %shard_map.79 = (bf16[512,256]{1,0:T(8,128)(2,1)S(1)}, f32[512,256]{1,0:T(8,128)S(1)}, f32[128,1536]{1,0:T(8,128)S(1)}, f32[128,512]{1,0:T(8,128)S(1)}, f32[128,512]{1,0:T(8,128)S(1)}) custom-call(bf16[256,384]{1,0:T(8,128)(2,1)S(1)} %pad_maximum_fusion.refs_0_, bf16[256,384]{1,0:T(8,128)(2,1)S(1)} %collective-permute-done.2.refs_1_, ...), custom_call_target="tpu_custom_call" | custom-call | flops 65536 | bytes 1024 | tf_op jit(solution)/shard_map/pallas_call | solution.py:268
  25.5 2.2 %collective-permute-done.10.refs_7_ = bf16[256,256]{1,0:T(8,128)(2,1)S(1)} collective-permute-done((bf16[256,256]{1,0:T(8,128)(2,1)S(1)}, bf16[256,256]{1,0:T(8,128)(2,1)S(1)}, u32[]{:S(2)}, u32[]{:S(2)}) %collective-permute-start.10) | collective-permute-done | bytes 131104 | tf_op jit(solution)/shard_map/ppermute | solution.py:210
  27.7 0.0 collective-permute-done.7.columns_ref.refs_6_
  27.7 0.0 collective-permute-start.11
  27.7 0.6 %shard_map.80 = (f32[512,256]{1,0:T(8,128)S(1)}, f32[128,256]{1,0:T(8,128)S(1)}) custom-call(bf16[256,384]{1,0:T(8,128)(2,1)S(1)} %collective-permute-done.7.columns_ref.refs_6_, bf16[512,256]{1,0:T(8,128)(2,1)S(1)} %get-tuple-element.26.left_ref.refs_1_.refs_11_, f32[512,256]{1,0:T(8,128)S(1)} %get-tuple-element.27.before_ref), custom_call_target="tpu_custom_call" | custom-call | flops 65536 | bytes 1024 | tf_op jit(solution)/shard_map/pallas_call | solution.py:268
  28.3 0.8 %collective-permute-done.11.refs_0_.refs_7_ = bf16[256,384]{1,0:T(8,128)(2,1)S(1)} collective-permute-done((bf16[256,384]{1,0:T(8,128)(2,1)S(1)}, bf16[256,384]{1,0:T(8,128)(2,1)S(1)}, u32[]{:S(2)}, u32[]{:S(2)}) %collective-permute-start.11) | collective-permute-done | bytes 196640 | tf_op jit(solution)/shard_map/ppermute | solution.py:210
  29.2 0.9 %shard_map.81 = (f32[128,256]{1,0:T(8,128)S(1)}, bf16[512,256]{1,0:T(8,128)(2,1)S(1)}, f32[128,128]{1,0:T(8,128)S(1)}) custom-call(bf16[256,384]{1,0:T(8,128)(2,1)S(1)} %collective-permute-done.11.refs_0_.refs_7_, bf16[512,256]{1,0:T(8,128)(2,1)S(1)} %get-tuple-element.26.left_ref.refs_1_.refs_11_, f32[512,256]{1,0:T(8,128)S(1)} %get-tuple-element.29.refs_2_, ...), custom_call_target="tpu_custom_call" | custom-call | tf_op jit(solution)/shard_map/pallas_call | solution.py:288
  30.1 0.2 collective-permute-start.12
  30.3 1.3 %shard_map.82 = (f32[128,128]{1,0:T(8,128)S(1)}, f32[128,128]{1,0:T(8,128)S(1)}) custom-call(bf16[256,384]{1,0:T(8,128)(2,1)S(1)} %pad_maximum_fusion.refs_0_, bf16[256,384]{1,0:T(8,128)(2,1)S(1)} %collective-permute-done.2.refs_1_, bf16[256,384]{1,0:T(8,128)(2,1)S(1)} %collective-permute-done.3.refs_2_, ...), custom_call_target="tpu_custom_call" | custom-call | flops 536870912 | bytes 1048576 | tf_op jit(solution)/shard_map/pallas_call | solution.py:296
  31.6 0.0 collective-permute-done.12
  31.6 1.5 %collective-permute-start.13 = (f32[128,128]{1,0:T(8,128)S(1)}, f32[128,128]{1,0:T(8,128)S(1)}, u32[]{:S(2)}, u32[]{:S(2)}) collective-permute-start(f32[128,128]{1,0:T(8,128)S(1)} %pad_maximum_fusion.4), channel_id=1, source_target_pairs={{0,1},{1,0},{2,3},{3,2},{4,5},{5,4},{6,7},{7,6},{8,9},{9,8},{10,11... | collective-permute-start | bytes 196616 | tf_op jit(solution)/shard_map/ppermute | solution.py:210
  33.1 3.0 %collective-permute-done.13 = f32[128,128]{1,0:T(8,128)S(1)} collective-permute-done((f32[128,128]{1,0:T(8,128)S(1)}, f32[128,128]{1,0:T(8,128)S(1)}, u32[]{:S(2)}, u32[]{:S(2)}) %collective-permute-start.13) | collective-permute-done | bytes 65568 | tf_op jit(solution)/shard_map/ppermute | solution.py:210
  36.1 0.6 %slice_add_fusion = (f32[64,128]{1,0:T(8,128)}, f32[64,128]{1,0:T(8,128)}) fusion(f32[128,128]{1,0:T(8,128)S(1)} %collective-permute-done.13, f32[128,128]{1,0:T(8,128)S(1)} %add.9, f32[128,128]{1,0:T(8,128)S(1)} %get-tuple-element.35), kind=kLoop, calls=%fused_computation.6 | loop fusion | flops 16384 | bytes 196608 | tf_op jit(solution)/shard_map/add | solution.py:310
  (10 shorter events, 0.1 us)
Async XLA Ops:
  2.5 6.9 %collective-permute-start = (bf16[64,384]{1,0:T(8,128)(2,1)}, bf16[64,384]{1,0:T(8,128)(2,1)S(1)}, u32[]{:S(2)}, u32[]{:S(2)}) collective-permute-start(bf16[64,384]{1,0:T(8,128)(2,1)} %shard_map.77.refs_3_), channel_id=1, source_target_pairs={{0,16},{4,20},{8,24},{12,28},{16,0},{20,4},{24,8},{28,12},{1,17},{... | collective-permute-start | bytes 147464 | tf_op jit(solution)/shard_map/ppermute | solution.py:210
  6.6 2.8 %copy-start.1 = (bf16[64,384]{1,0:T(8,128)(2,1)S(1)}, bf16[64,384]{1,0:T(8,128)(2,1)}, u32[]{:S(2)}) copy-start(bf16[64,384]{1,0:T(8,128)(2,1)} %shard_map.77.refs_3_) | copy-start | bytes 147460
  9.4 1.5 %copy-start = (bf16[16,256]{1,0:T(8,128)(2,1)S(1)}, bf16[16,256]{1,0:T(8,128)(2,1)}, u32[]{:S(2)}) copy-start(bf16[16,256]{1,0:T(8,128)(2,1)} %get-tuple-element.23.refs_14_) | copy-start | bytes 24580
  9.4 1.5 %copy-start.2 = (bf16[64,256]{1,0:T(8,128)(2,1)S(1)}, bf16[64,256]{1,0:T(8,128)(2,1)}, u32[]{:S(2)}) copy-start(bf16[64,256]{1,0:T(8,128)(2,1)} %get-tuple-element.20) | copy-start | bytes 98308
  9.4 4.7 %collective-permute-start.1 = (bf16[128,384]{1,0:T(8,128)(2,1)S(1)}, bf16[128,384]{1,0:T(8,128)(2,1)S(1)}, u32[]{:S(2)}, u32[]{:S(2)}) collective-permute-start(bf16[128,384]{1,0:T(8,128)(2,1)S(1)} %pad_maximum_fusion.2), channel_id=1, source_target_pairs={{0,8},{4,12},{8,0},{12,4},{16,24},{20,28},{24,16},{28,20},{1,9},{5... | collective-permute-start | bytes 294920 | tf_op jit(solution)/shard_map/ppermute | solution.py:210
  10.9 6.5 %collective-permute-start.8 = (bf16[80,256]{1,0:T(8,128)(2,1)S(1)}, bf16[80,256]{1,0:T(8,128)(2,1)S(1)}, u32[]{:S(2)}, u32[]{:S(2)}) collective-permute-start(bf16[80,256]{1,0:T(8,128)(2,1)S(1)} %pad_maximum_fusion.5), channel_id=1, source_target_pairs={{0,2},{1,3},{2,0},{3,1},{4,6},{5,7},{6,4},{7,5},{8,10},{9,11},{10,... | collective-permute-start | bytes 122888 | tf_op jit(solution)/shard_map/ppermute | solution.py:210
  14.1 5.7 %collective-permute-start.2 = (bf16[256,384]{1,0:T(8,128)(2,1)S(1)}, bf16[256,384]{1,0:T(8,128)(2,1)S(1)}, u32[]{:S(2)}, u32[]{:S(2)}) collective-permute-start(bf16[256,384]{1,0:T(8,128)(2,1)S(1)} %pad_maximum_fusion.refs_0_), channel_id=1, source_target_pairs={{0,1},{1,0},{2,3},{3,2},{4,5},{5,4},{6,7},{7,6},{8,9},{9,8},{10,11... | collective-permute-start | bytes 589832 | tf_op jit(solution)/shard_map/ppermute | solution.py:210
  15.9 5.7 %collective-permute-start.3 = (bf16[256,384]{1,0:T(8,128)(2,1)S(1)}, bf16[256,384]{1,0:T(8,128)(2,1)S(1)}, u32[]{:S(2)}, u32[]{:S(2)}) collective-permute-start(bf16[256,384]{1,0:T(8,128)(2,1)S(1)} %pad_maximum_fusion.refs_0_), channel_id=1, source_target_pairs={{0,2},{1,3},{2,0},{3,1},{4,6},{5,7},{6,4},{7,5},{8,10},{9,11},{10,... | collective-permute-start | bytes 589832 | tf_op jit(solution)/shard_map/ppermute | solution.py:210
  17.4 5.2 %collective-permute-start.9 = (bf16[128,256]{1,0:T(8,128)(2,1)S(1)}, bf16[128,256]{1,0:T(8,128)(2,1)S(1)}, u32[]{:S(2)}, u32[]{:S(2)}) collective-permute-start(bf16[128,256]{1,0:T(8,128)(2,1)S(1)} %pad_maximum_fusion.3), channel_id=1, source_target_pairs={{0,16},{4,20},{8,24},{12,28},{16,0},{20,4},{24,8},{28,12},{1,17},{... | collective-permute-start | bytes 196616 | tf_op jit(solution)/shard_map/ppermute | solution.py:210
  19.7 4.3 %collective-permute-start.4 = (bf16[256,384]{1,0:T(8,128)(2,1)S(1)}, bf16[256,384]{1,0:T(8,128)(2,1)S(1)}, u32[]{:S(2)}, u32[]{:S(2)}) collective-permute-start(bf16[256,384]{1,0:T(8,128)(2,1)S(1)} %pad_maximum_fusion.refs_0_), channel_id=1, source_target_pairs={{0,4},{4,0},{8,12},{12,8},{16,20},{20,16},{24,28},{28,24},{1,5},{5... | collective-permute-start | bytes 589832 | tf_op jit(solution)/shard_map/ppermute | solution.py:210
  19.9 7.9 %collective-permute-start.7 = (bf16[256,384]{1,0:T(8,128)(2,1)S(1)}, bf16[256,384]{1,0:T(8,128)(2,1)S(1)}, u32[]{:S(2)}, u32[]{:S(2)}) collective-permute-start(bf16[256,384]{1,0:T(8,128)(2,1)S(1)} %collective-permute-done.2.refs_1_), channel_id=1, source_target_pairs={{0,2},{1,3},{2,0},{3,1},{4,6},{5,7},{6,4},{7,5},{8,10},{9,11},{10,... | collective-permute-start | bytes 589832 | tf_op jit(solution)/shard_map/ppermute | solution.py:210
  21.6 2.4 %collective-permute-start.5 = (bf16[256,384]{1,0:T(8,128)(2,1)S(1)}, bf16[256,384]{1,0:T(8,128)(2,1)S(1)}, u32[]{:S(2)}, u32[]{:S(2)}) collective-permute-start(bf16[256,384]{1,0:T(8,128)(2,1)S(1)} %collective-permute-done.2.refs_1_), channel_id=1, source_target_pairs={{0,4},{4,0},{8,12},{12,8},{16,20},{20,16},{24,28},{28,24},{1,5},{5... | collective-permute-start | bytes 589832 | tf_op jit(solution)/shard_map/ppermute | solution.py:210
  21.6 2.4 %collective-permute-start.6 = (bf16[256,384]{1,0:T(8,128)(2,1)S(1)}, bf16[256,384]{1,0:T(8,128)(2,1)S(1)}, u32[]{:S(2)}, u32[]{:S(2)}) collective-permute-start(bf16[256,384]{1,0:T(8,128)(2,1)S(1)} %collective-permute-done.3.refs_2_), channel_id=1, source_target_pairs={{0,4},{4,0},{8,12},{12,8},{16,20},{20,16},{24,28},{28,24},{1,5},{5... | collective-permute-start | bytes 589832 | tf_op jit(solution)/shard_map/ppermute | solution.py:210
  22.7 5.0 %collective-permute-start.10 = (bf16[256,256]{1,0:T(8,128)(2,1)S(1)}, bf16[256,256]{1,0:T(8,128)(2,1)S(1)}, u32[]{:S(2)}, u32[]{:S(2)}) collective-permute-start(bf16[256,256]{1,0:T(8,128)(2,1)S(1)} %pad_maximum_fusion.1.refs_6_), channel_id=1, source_target_pairs={{0,8},{4,12},{8,0},{12,4},{16,24},{20,28},{24,16},{28,20},{1,9},{5... | collective-permute-start | bytes 393224 | tf_op jit(solution)/shard_map/ppermute | solution.py:210
  27.7 1.4 %collective-permute-start.11 = (bf16[256,384]{1,0:T(8,128)(2,1)S(1)}, bf16[256,384]{1,0:T(8,128)(2,1)S(1)}, u32[]{:S(2)}, u32[]{:S(2)}) collective-permute-start(bf16[256,384]{1,0:T(8,128)(2,1)S(1)} %collective-permute-done.7.columns_ref.refs_6_), channel_id=1, source_target_pairs={{0,4},{4,0},{8,12},{12,8},{16,20},{20,16},{24,28},{28,24},{1,5},{5... | collective-permute-start | bytes 589832 | tf_op jit(solution)/shard_map/ppermute | solution.py:210
  30.1 1.5 %collective-permute-start.12 = (f32[128,128]{1,0:T(8,128)S(1)}, f32[128,128]{1,0:T(8,128)S(1)}, u32[]{:S(2)}, u32[]{:S(2)}) collective-permute-start(f32[128,128]{1,0:T(8,128)S(1)} %get-tuple-element.37), channel_id=1, source_target_pairs={{0,4},{4,0},{8,12},{12,8},{16,20},{20,16},{24,28},{28,24},{1,5},{5... | collective-permute-start | bytes 196616 | tf_op jit(solution)/shard_map/ppermute | solution.py:210
  31.6 4.4 %collective-permute-start.13 = (f32[128,128]{1,0:T(8,128)S(1)}, f32[128,128]{1,0:T(8,128)S(1)}, u32[]{:S(2)}, u32[]{:S(2)}) collective-permute-start(f32[128,128]{1,0:T(8,128)S(1)} %pad_maximum_fusion.4), channel_id=1, source_target_pairs={{0,1},{1,0},{2,3},{3,2},{4,5},{5,4},{6,7},{7,6},{8,9},{9,8},{10,11... | collective-permute-start | bytes 196616 | tf_op jit(solution)/shard_map/ppermute | solution.py:210

commit v8 on v7

--- a/solution.py
+++ b/solution.py
@@ -282,8 +282,8 @@
         (shape((held, 2 * width), BF16), fit_shape, slots[0], picks_shape, picks_shape),
         *(*near, *far),
     )
-    across, fit, observed_z = lax.optimization_barrier((across, fit, observed_z))
-    far_across = swap(across, "row", 1)
+    sent, _, observed_z = lax.optimization_barrier((across, fit, observed_z))
+    far_across = swap(sent, "row", 1)
     fit, slots_across = call(across_kernel, (fit_shape, slots[1]), across, left, fit)
     slots_last, adjoint, col_far = pl.pallas_call(
         functools.partial(adjoint_kernel, scale, factor, own),

time: 37.2 us -> 36.9 us (level)
  no operation moved by 1% of the time
where the time goes in v8:
time: 36.9 us; the launch traced here: 36.7 us
  starting transfers between devices  17.6 us (48%)
  waiting for transfers between devices  10 us (27%)
  Pallas kernels  7.57 us (21%)
  between operations  0.75 us (2%)
  other arithmetic  0.7 us (2%)
    ppermute x14, starting transfers between devices, swap(): return lax.ppermute(array, axis, pairs)  17.6 us
    ppermute x14, waiting for transfers between devices, swap(): return lax.ppermute(array, axis, pairs)  10 us
    pallas_call x2, Pallas kernels, call(): pl.pallas_call(functools.partial(body, scale, own), out_shape=outs, in_sp...  2.05 us
    pallas_call x1, Pallas kernels, gathered_plan(): pl.pallas_call(functools.partial(head_kernel, width), out_shape=shape((ow...  1.87 us
    pallas_call x1, Pallas kernels, gathered_plan(): pl.pallas_call(targets_kernel, out_shape=(shape((own, epochs), BF16), sha...  1.5 us
    pallas_call x1, Pallas kernels, gathered_plan(): pl.pallas_call(functools.partial(last_kernel, factor, own), out_shape=(sh...  1.29 us
    pallas_call x1, Pallas kernels, gathered_plan(): pl.pallas_call(functools.partial(adjoint_kernel, scale, factor, own), out...  0.86 us
  transfers between devices with their start and end apart: 14, of which 7 were waited for; matrix products, arithmetic and copies ran while one was open for 0% of the time, Pallas kernels for 13%

profile of v8, /device:TPU:0, one launch (start us, length us, event | category | flops | bytes accessed | tf_op | source)
XLA Modules:
  0.0 36.7 jit_solution(5232257518466082310)
XLA Ops:
  0.6 1.9 %shard_map.77.refs_3_ = bf16[64,384]{1,0:T(8,128)(2,1)} custom-call(bf16[64,128]{1,0:T(8,128)(2,1)} %refs_0_.2, f32[64,256]{1,0:T(8,128)} %refs_1_.1, f32[256,256]{1,0:T(8,128)} %refs_2_.1), custom_call_target="tpu_custom_call" | custom-call | tf_op jit(solution)/shard_map/pallas_call | solution.py:232
  2.5 4.1 %collective-permute-start = (bf16[64,384]{1,0:T(8,128)(2,1)}, bf16[64,384]{1,0:T(8,128)(2,1)S(1)}, u32[]{:S(2)}, u32[]{:S(2)}) collective-permute-start(bf16[64,384]{1,0:T(8,128)(2,1)} %shard_map.77.refs_3_), channel_id=1, source_target_pairs={{0,16},{4,20},{8,24},{12,28},{16,0},{20,4},{24,8},{28,12},{1,17},{... | collective-permute-start | bytes 147464 | tf_op jit(solution)/shard_map/ppermute | solution.py:210
  6.6 0.0 copy-start.1
  6.6 1.5 %shard_map.78 = (bf16[64,256]{1,0:T(8,128)(2,1)}, bf16[16,256]{1,0:T(8,128)(2,1)}) custom-call(bf16[64,256]{1,0:T(8,128)(2,1)} %refs_0_.3, s32[1,64]{1,0:T(1,128)} %bitcast.2, s32[1,64]{1,0:T(1,128)} %bitcast.3, bf16[64,384]{1,0:T(8,128)(2,1)} %shard_map.77.refs_3_), custom_call_target="tpu_custom_call" | custom-call | flops 1073741824 | bytes 65536 | tf_op jit(solution)/shard_map/pallas_call | solution.py:240
  8.1 1.3 %collective-permute-done = bf16[64,384]{1,0:T(8,128)(2,1)S(1)} collective-permute-done((bf16[64,384]{1,0:T(8,128)(2,1)}, bf16[64,384]{1,0:T(8,128)(2,1)S(1)}, u32[]{:S(2)}, u32[]{:S(2)}) %collective-permute-start) | collective-permute-done | bytes 49184 | tf_op jit(solution)/shard_map/ppermute | solution.py:210
  9.4 0.0 copy-done.1
  9.4 0.0 copy-start
  9.4 0.0 copy-start.2
  9.4 1.4 %collective-permute-start.1 = (bf16[128,384]{1,0:T(8,128)(2,1)S(1)}, bf16[128,384]{1,0:T(8,128)(2,1)S(1)}, u32[]{:S(2)}, u32[]{:S(2)}) collective-permute-start(bf16[128,384]{1,0:T(8,128)(2,1)S(1)} %pad_maximum_fusion.2), channel_id=1, source_target_pairs={{0,8},{4,12},{8,0},{12,4},{16,24},{20,28},{24,16},{28,20},{1,9},{5... | collective-permute-start | bytes 294920 | tf_op jit(solution)/shard_map/ppermute | solution.py:210
  10.9 0.0 copy-done
  10.9 0.0 copy-done.2
  10.9 1.6 %collective-permute-start.8 = (bf16[80,256]{1,0:T(8,128)(2,1)S(1)}, bf16[80,256]{1,0:T(8,128)(2,1)S(1)}, u32[]{:S(2)}, u32[]{:S(2)}) collective-permute-start(bf16[80,256]{1,0:T(8,128)(2,1)S(1)} %pad_maximum_fusion.5), channel_id=1, source_target_pairs={{0,2},{1,3},{2,0},{3,1},{4,6},{5,7},{6,4},{7,5},{8,10},{9,11},{10,... | collective-permute-start | bytes 122888 | tf_op jit(solution)/shard_map/ppermute | solution.py:210
  12.5 1.6 %collective-permute-done.1 = bf16[128,384]{1,0:T(8,128)(2,1)S(1)} collective-permute-done((bf16[128,384]{1,0:T(8,128)(2,1)S(1)}, bf16[128,384]{1,0:T(8,128)(2,1)S(1)}, u32[]{:S(2)}, u32[]{:S(2)}) %collective-permute-start.1) | collective-permute-done | bytes 98336 | tf_op jit(solution)/shard_map/ppermute | solution.py:210
  14.1 1.8 %collective-permute-start.2 = (bf16[256,384]{1,0:T(8,128)(2,1)S(1)}, bf16[256,384]{1,0:T(8,128)(2,1)S(1)}, u32[]{:S(2)}, u32[]{:S(2)}) collective-permute-start(bf16[256,384]{1,0:T(8,128)(2,1)S(1)} %pad_maximum_fusion.refs_0_), channel_id=1, source_target_pairs={{0,1},{1,0},{2,3},{3,2},{4,5},{5,4},{6,7},{7,6},{8,9},{9,8},{10,11... | collective-permute-start | bytes 589832 | tf_op jit(solution)/shard_map/ppermute | solution.py:210
  15.9 1.5 %collective-permute-start.3 = (bf16[256,384]{1,0:T(8,128)(2,1)S(1)}, bf16[256,384]{1,0:T(8,128)(2,1)S(1)}, u32[]{:S(2)}, u32[]{:S(2)}) collective-permute-start(bf16[256,384]{1,0:T(8,128)(2,1)S(1)} %pad_maximum_fusion.refs_0_), channel_id=1, source_target_pairs={{0,2},{1,3},{2,0},{3,1},{4,6},{5,7},{6,4},{7,5},{8,10},{9,11},{10,... | collective-permute-start | bytes 589832 | tf_op jit(solution)/shard_map/ppermute | solution.py:210
  17.4 0.0 collective-permute-done.8.refs_15_
  17.4 2.3 %collective-permute-start.9 = (bf16[128,256]{1,0:T(8,128)(2,1)S(1)}, bf16[128,256]{1,0:T(8,128)(2,1)S(1)}, u32[]{:S(2)}, u32[]{:S(2)}) collective-permute-start(bf16[128,256]{1,0:T(8,128)(2,1)S(1)} %pad_maximum_fusion.3), channel_id=1, source_target_pairs={{0,16},{4,20},{8,24},{12,28},{16,0},{20,4},{24,8},{28,12},{1,17},{... | collective-permute-start | bytes 196616 | tf_op jit(solution)/shard_map/ppermute | solution.py:210
  19.7 0.0 collective-permute-start.4
  19.7 0.1 collective-permute-done.2.refs_1_
  19.9 0.4 %collective-permute-start.5 = (bf16[256,384]{1,0:T(8,128)(2,1)S(1)}, bf16[256,384]{1,0:T(8,128)(2,1)S(1)}, u32[]{:S(2)}, u32[]{:S(2)}) collective-permute-start(bf16[256,384]{1,0:T(8,128)(2,1)S(1)} %collective-permute-done.2.refs_1_), channel_id=1, source_target_pairs={{0,4},{4,0},{8,12},{12,8},{16,20},{20,16},{24,28},{28,24},{1,5},{5... | collective-permute-start | bytes 589832 | tf_op jit(solution)/shard_map/ppermute | solution.py:210
  20.3 1.4 %collective-permute-start.7 = (bf16[256,384]{1,0:T(8,128)(2,1)S(1)}, bf16[256,384]{1,0:T(8,128)(2,1)S(1)}, u32[]{:S(2)}, u32[]{:S(2)}) collective-permute-start(bf16[256,384]{1,0:T(8,128)(2,1)S(1)} %collective-permute-done.2.refs_1_), channel_id=1, source_target_pairs={{0,2},{1,3},{2,0},{3,1},{4,6},{5,7},{6,4},{7,5},{8,10},{9,11},{10,... | collective-permute-start | bytes 589832 | tf_op jit(solution)/shard_map/ppermute | solution.py:210
  21.6 0.0 collective-permute-done.3.refs_2_
  21.6 0.2 collective-permute-start.6
  21.8 0.8 %collective-permute-done.9 = bf16[128,256]{1,0:T(8,128)(2,1)S(1)} collective-permute-done((bf16[128,256]{1,0:T(8,128)(2,1)S(1)}, bf16[128,256]{1,0:T(8,128)(2,1)S(1)}, u32[]{:S(2)}, u32[]{:S(2)}) %collective-permute-start.9) | collective-permute-done | bytes 65568 | tf_op jit(solution)/shard_map/ppermute | solution.py:210
  22.7 1.3 %collective-permute-start.10 = (bf16[256,256]{1,0:T(8,128)(2,1)S(1)}, bf16[256,256]{1,0:T(8,128)(2,1)S(1)}, u32[]{:S(2)}, u32[]{:S(2)}) collective-permute-start(bf16[256,256]{1,0:T(8,128)(2,1)S(1)} %pad_maximum_fusion.1.refs_6_), channel_id=1, source_target_pairs={{0,8},{4,12},{8,0},{12,4},{16,24},{20,28},{24,16},{28,20},{1,9},{5... | collective-permute-start | bytes 393224 | tf_op jit(solution)/shard_map/ppermute | solution.py:210
  24.0 0.0 collective-permute-done.4.refs_3_
  24.0 0.0 collective-permute-done.5.refs_4_
  24.0 0.0 collective-permute-done.6.refs_5_
  24.0 1.5 %shard_map.79 = (bf16[512,256]{1,0:T(8,128)(2,1)S(1)}, f32[512,256]{1,0:T(8,128)S(1)}, f32[128,1536]{1,0:T(8,128)S(1)}, f32[128,512]{1,0:T(8,128)S(1)}, f32[128,512]{1,0:T(8,128)S(1)}) custom-call(bf16[256,384]{1,0:T(8,128)(2,1)S(1)} %pad_maximum_fusion.refs_0_, bf16[256,384]{1,0:T(8,128)(2,1)S(1)} %collective-permute-done.2.refs_1_, ...), custom_call_target="tpu_custom_call" | custom-call | flops 65536 | bytes 1024 | tf_op jit(solution)/shard_map/pallas_call | solution.py:268
  25.5 2.2 %collective-permute-done.10.refs_7_ = bf16[256,256]{1,0:T(8,128)(2,1)S(1)} collective-permute-done((bf16[256,256]{1,0:T(8,128)(2,1)S(1)}, bf16[256,256]{1,0:T(8,128)(2,1)S(1)}, u32[]{:S(2)}, u32[]{:S(2)}) %collective-permute-start.10) | collective-permute-done | bytes 131104 | tf_op jit(solution)/shard_map/ppermute | solution.py:210
  27.7 0.0 collective-permute-done.7.columns_ref.refs_6_
  27.7 0.0 collective-permute-start.11
  27.7 0.6 %shard_map.80 = (f32[512,256]{1,0:T(8,128)S(1)}, f32[128,256]{1,0:T(8,128)S(1)}) custom-call(bf16[256,384]{1,0:T(8,128)(2,1)S(1)} %collective-permute-done.7.columns_ref.refs_6_, bf16[512,256]{1,0:T(8,128)(2,1)S(1)} %get-tuple-element.25.left_ref.refs_1_.refs_11_, f32[512,256]{1,0:T(8,128)S(1)} %get-tuple-element.21.before_ref), custom_call_target="tpu_custom_call" | custom-call | flops 65536 | bytes 1024 | tf_op jit(solution)/shard_map/pallas_call | solution.py:268
  28.3 0.8 %collective-permute-done.11.refs_0_.refs_7_ = bf16[256,384]{1,0:T(8,128)(2,1)S(1)} collective-permute-done((bf16[256,384]{1,0:T(8,128)(2,1)S(1)}, bf16[256,384]{1,0:T(8,128)(2,1)S(1)}, u32[]{:S(2)}, u32[]{:S(2)}) %collective-permute-start.11) | collective-permute-done | bytes 196640 | tf_op jit(solution)/shard_map/ppermute | solution.py:210
  29.2 0.9 %shard_map.81 = (f32[128,256]{1,0:T(8,128)S(1)}, bf16[512,256]{1,0:T(8,128)(2,1)S(1)}, f32[128,128]{1,0:T(8,128)S(1)}) custom-call(bf16[256,384]{1,0:T(8,128)(2,1)S(1)} %collective-permute-done.11.refs_0_.refs_7_, bf16[512,256]{1,0:T(8,128)(2,1)S(1)} %get-tuple-element.25.left_ref.refs_1_.refs_11_, f32[512,256]{1,0:T(8,128)S(1)} %get-tuple-element.27.refs_2_, ...), custom_call_target="tpu_custom_call" | custom-call | tf_op jit(solution)/shard_map/pallas_call | solution.py:288
  30.1 0.2 collective-permute-start.12
  30.3 1.3 %shard_map.82 = (f32[128,128]{1,0:T(8,128)S(1)}, f32[128,128]{1,0:T(8,128)S(1)}) custom-call(bf16[256,384]{1,0:T(8,128)(2,1)S(1)} %pad_maximum_fusion.refs_0_, bf16[256,384]{1,0:T(8,128)(2,1)S(1)} %collective-permute-done.2.refs_1_, bf16[256,384]{1,0:T(8,128)(2,1)S(1)} %collective-permute-done.3.refs_2_, ...), custom_call_target="tpu_custom_call" | custom-call | flops 536870912 | bytes 1048576 | tf_op jit(solution)/shard_map/pallas_call | solution.py:296
  31.6 0.0 collective-permute-done.12
  31.6 1.4 %collective-permute-start.13 = (f32[128,128]{1,0:T(8,128)S(1)}, f32[128,128]{1,0:T(8,128)S(1)}, u32[]{:S(2)}, u32[]{:S(2)}) collective-permute-start(f32[128,128]{1,0:T(8,128)S(1)} %pad_maximum_fusion.4), channel_id=1, source_target_pairs={{0,1},{1,0},{2,3},{3,2},{4,5},{5,4},{6,7},{7,6},{8,9},{9,8},{10,11... | collective-permute-start | bytes 196616 | tf_op jit(solution)/shard_map/ppermute | solution.py:210
  33.1 3.0 %collective-permute-done.13 = f32[128,128]{1,0:T(8,128)S(1)} collective-permute-done((f32[128,128]{1,0:T(8,128)S(1)}, f32[128,128]{1,0:T(8,128)S(1)}, u32[]{:S(2)}, u32[]{:S(2)}) %collective-permute-start.13) | collective-permute-done | bytes 65568 | tf_op jit(solution)/shard_map/ppermute | solution.py:210
  36.1 0.6 %slice_add_fusion = (f32[64,128]{1,0:T(8,128)}, f32[64,128]{1,0:T(8,128)}) fusion(f32[128,128]{1,0:T(8,128)S(1)} %collective-permute-done.13, f32[128,128]{1,0:T(8,128)S(1)} %add.9, f32[128,128]{1,0:T(8,128)S(1)} %get-tuple-element.33), kind=kLoop, calls=%fused_computation.6 | loop fusion | flops 16384 | bytes 196608 | tf_op jit(solution)/shard_map/add | solution.py:310
  (10 shorter events, 0.1 us)
Async XLA Ops:
  2.5 6.9 %collective-permute-start = (bf16[64,384]{1,0:T(8,128)(2,1)}, bf16[64,384]{1,0:T(8,128)(2,1)S(1)}, u32[]{:S(2)}, u32[]{:S(2)}) collective-permute-start(bf16[64,384]{1,0:T(8,128)(2,1)} %shard_map.77.refs_3_), channel_id=1, source_target_pairs={{0,16},{4,20},{8,24},{12,28},{16,0},{20,4},{24,8},{28,12},{1,17},{... | collective-permute-start | bytes 147464 | tf_op jit(solution)/shard_map/ppermute | solution.py:210
  6.6 2.8 %copy-start.1 = (bf16[64,384]{1,0:T(8,128)(2,1)S(1)}, bf16[64,384]{1,0:T(8,128)(2,1)}, u32[]{:S(2)}) copy-start(bf16[64,384]{1,0:T(8,128)(2,1)} %shard_map.77.refs_3_) | copy-start | bytes 147460
  9.4 1.5 %copy-start = (bf16[16,256]{1,0:T(8,128)(2,1)S(1)}, bf16[16,256]{1,0:T(8,128)(2,1)}, u32[]{:S(2)}) copy-start(bf16[16,256]{1,0:T(8,128)(2,1)} %get-tuple-element.22.refs_14_) | copy-start | bytes 24580
  9.4 1.5 %copy-start.2 = (bf16[64,256]{1,0:T(8,128)(2,1)S(1)}, bf16[64,256]{1,0:T(8,128)(2,1)}, u32[]{:S(2)}) copy-start(bf16[64,256]{1,0:T(8,128)(2,1)} %get-tuple-element.19) | copy-start | bytes 98308
  9.4 4.7 %collective-permute-start.1 = (bf16[128,384]{1,0:T(8,128)(2,1)S(1)}, bf16[128,384]{1,0:T(8,128)(2,1)S(1)}, u32[]{:S(2)}, u32[]{:S(2)}) collective-permute-start(bf16[128,384]{1,0:T(8,128)(2,1)S(1)} %pad_maximum_fusion.2), channel_id=1, source_target_pairs={{0,8},{4,12},{8,0},{12,4},{16,24},{20,28},{24,16},{28,20},{1,9},{5... | collective-permute-start | bytes 294920 | tf_op jit(solution)/shard_map/ppermute | solution.py:210
  10.9 6.5 %collective-permute-start.8 = (bf16[80,256]{1,0:T(8,128)(2,1)S(1)}, bf16[80,256]{1,0:T(8,128)(2,1)S(1)}, u32[]{:S(2)}, u32[]{:S(2)}) collective-permute-start(bf16[80,256]{1,0:T(8,128)(2,1)S(1)} %pad_maximum_fusion.5), channel_id=1, source_target_pairs={{0,2},{1,3},{2,0},{3,1},{4,6},{5,7},{6,4},{7,5},{8,10},{9,11},{10,... | collective-permute-start | bytes 122888 | tf_op jit(solution)/shard_map/ppermute | solution.py:210
  14.1 5.7 %collective-permute-start.2 = (bf16[256,384]{1,0:T(8,128)(2,1)S(1)}, bf16[256,384]{1,0:T(8,128)(2,1)S(1)}, u32[]{:S(2)}, u32[]{:S(2)}) collective-permute-start(bf16[256,384]{1,0:T(8,128)(2,1)S(1)} %pad_maximum_fusion.refs_0_), channel_id=1, source_target_pairs={{0,1},{1,0},{2,3},{3,2},{4,5},{5,4},{6,7},{7,6},{8,9},{9,8},{10,11... | collective-permute-start | bytes 589832 | tf_op jit(solution)/shard_map/ppermute | solution.py:210
  15.9 5.7 %collective-permute-start.3 = (bf16[256,384]{1,0:T(8,128)(2,1)S(1)}, bf16[256,384]{1,0:T(8,128)(2,1)S(1)}, u32[]{:S(2)}, u32[]{:S(2)}) collective-permute-start(bf16[256,384]{1,0:T(8,128)(2,1)S(1)} %pad_maximum_fusion.refs_0_), channel_id=1, source_target_pairs={{0,2},{1,3},{2,0},{3,1},{4,6},{5,7},{6,4},{7,5},{8,10},{9,11},{10,... | collective-permute-start | bytes 589832 | tf_op jit(solution)/shard_map/ppermute | solution.py:210
  17.4 5.2 %collective-permute-start.9 = (bf16[128,256]{1,0:T(8,128)(2,1)S(1)}, bf16[128,256]{1,0:T(8,128)(2,1)S(1)}, u32[]{:S(2)}, u32[]{:S(2)}) collective-permute-start(bf16[128,256]{1,0:T(8,128)(2,1)S(1)} %pad_maximum_fusion.3), channel_id=1, source_target_pairs={{0,16},{4,20},{8,24},{12,28},{16,0},{20,4},{24,8},{28,12},{1,17},{... | collective-permute-start | bytes 196616 | tf_op jit(solution)/shard_map/ppermute | solution.py:210
  19.7 4.3 %collective-permute-start.4 = (bf16[256,384]{1,0:T(8,128)(2,1)S(1)}, bf16[256,384]{1,0:T(8,128)(2,1)S(1)}, u32[]{:S(2)}, u32[]{:S(2)}) collective-permute-start(bf16[256,384]{1,0:T(8,128)(2,1)S(1)} %pad_maximum_fusion.refs_0_), channel_id=1, source_target_pairs={{0,4},{4,0},{8,12},{12,8},{16,20},{20,16},{24,28},{28,24},{1,5},{5... | collective-permute-start | bytes 589832 | tf_op jit(solution)/shard_map/ppermute | solution.py:210
  19.9 4.1 %collective-permute-start.5 = (bf16[256,384]{1,0:T(8,128)(2,1)S(1)}, bf16[256,384]{1,0:T(8,128)(2,1)S(1)}, u32[]{:S(2)}, u32[]{:S(2)}) collective-permute-start(bf16[256,384]{1,0:T(8,128)(2,1)S(1)} %collective-permute-done.2.refs_1_), channel_id=1, source_target_pairs={{0,4},{4,0},{8,12},{12,8},{16,20},{20,16},{24,28},{28,24},{1,5},{5... | collective-permute-start | bytes 589832 | tf_op jit(solution)/shard_map/ppermute | solution.py:210
  20.3 7.5 %collective-permute-start.7 = (bf16[256,384]{1,0:T(8,128)(2,1)S(1)}, bf16[256,384]{1,0:T(8,128)(2,1)S(1)}, u32[]{:S(2)}, u32[]{:S(2)}) collective-permute-start(bf16[256,384]{1,0:T(8,128)(2,1)S(1)} %collective-permute-done.2.refs_1_), channel_id=1, source_target_pairs={{0,2},{1,3},{2,0},{3,1},{4,6},{5,7},{6,4},{7,5},{8,10},{9,11},{10,... | collective-permute-start | bytes 589832 | tf_op jit(solution)/shard_map/ppermute | solution.py:210
  21.6 2.4 %collective-permute-start.6 = (bf16[256,384]{1,0:T(8,128)(2,1)S(1)}, bf16[256,384]{1,0:T(8,128)(2,1)S(1)}, u32[]{:S(2)}, u32[]{:S(2)}) collective-permute-start(bf16[256,384]{1,0:T(8,128)(2,1)S(1)} %collective-permute-done.3.refs_2_), channel_id=1, source_target_pairs={{0,4},{4,0},{8,12},{12,8},{16,20},{20,16},{24,28},{28,24},{1,5},{5... | collective-permute-start | bytes 589832 | tf_op jit(solution)/shard_map/ppermute | solution.py:210
  22.7 5.0 %collective-permute-start.10 = (bf16[256,256]{1,0:T(8,128)(2,1)S(1)}, bf16[256,256]{1,0:T(8,128)(2,1)S(1)}, u32[]{:S(2)}, u32[]{:S(2)}) collective-permute-start(bf16[256,256]{1,0:T(8,128)(2,1)S(1)} %pad_maximum_fusion.1.refs_6_), channel_id=1, source_target_pairs={{0,8},{4,12},{8,0},{12,4},{16,24},{20,28},{24,16},{28,20},{1,9},{5... | collective-permute-start | bytes 393224 | tf_op jit(solution)/shard_map/ppermute | solution.py:210
  27.7 1.4 %collective-permute-start.11 = (bf16[256,384]{1,0:T(8,128)(2,1)S(1)}, bf16[256,384]{1,0:T(8,128)(2,1)S(1)}, u32[]{:S(2)}, u32[]{:S(2)}) collective-permute-start(bf16[256,384]{1,0:T(8,128)(2,1)S(1)} %collective-permute-done.7.columns_ref.refs_6_), channel_id=1, source_target_pairs={{0,4},{4,0},{8,12},{12,8},{16,20},{20,16},{24,28},{28,24},{1,5},{5... | collective-permute-start | bytes 589832 | tf_op jit(solution)/shard_map/ppermute | solution.py:210
  30.1 1.5 %collective-permute-start.12 = (f32[128,128]{1,0:T(8,128)S(1)}, f32[128,128]{1,0:T(8,128)S(1)}, u32[]{:S(2)}, u32[]{:S(2)}) collective-permute-start(f32[128,128]{1,0:T(8,128)S(1)} %get-tuple-element.35), channel_id=1, source_target_pairs={{0,4},{4,0},{8,12},{12,8},{16,20},{20,16},{24,28},{28,24},{1,5},{5... | collective-permute-start | bytes 196616 | tf_op jit(solution)/shard_map/ppermute | solution.py:210
  31.6 4.4 %collective-permute-start.13 = (f32[128,128]{1,0:T(8,128)S(1)}, f32[128,128]{1,0:T(8,128)S(1)}, u32[]{:S(2)}, u32[]{:S(2)}) collective-permute-start(f32[128,128]{1,0:T(8,128)S(1)} %pad_maximum_fusion.4), channel_id=1, source_target_pairs={{0,1},{1,0},{2,3},{3,2},{4,5},{5,4},{6,7},{7,6},{8,9},{9,8},{10,11... | collective-permute-start | bytes 196616 | tf_op jit(solution)/shard_map/ppermute | solution.py:210
